TPU v7x, 512 devices: a whole 4x8x8 slice. The times are simulated.
512 devices in a mesh: lat: 64 (over z, y), chan: 2 (over core), obs: 4 (over x).
Axes of the slice: x: 4, y: 8, z: 8, core: 2. Of those that a mesh axis runs over, the one named last changes fastest.
Arguments:
- next_grad: bfloat16 [512, 1024, 256], P(('lat', 'obs'), None, 'chan'), may hold values from -6 to 6
- pre_act: bfloat16 [512, 1024, 256], P(('lat', 'obs'), None, 'chan'), may hold values from -6 to 6
- legendre: bfloat16 [512, 512, 512], P(('lat', 'obs')), may hold values from -1 to 1, as said below
- order_slots: int32 [512], replicated, may hold values from 0 to 511, as said below
- quad_weights: float32 [512], replicated, may hold values from 0.5 to 1.5
- spectral_gain: float32 [2, 512, 256], P(None, None, 'chan'), may hold values from -5 to 5
- saved_coeffs: bfloat16 [512, 2, 512, 256], P(('lat', 'obs'), None, None, 'chan'), may hold values from -0.029907227 to 0.029907227
- obs_value: bfloat16 [256, 16, 256], P(('lat', 'obs')), may hold values from -16 to 16
- obs_lat_frac: bfloat16 [256, 16, 256], P(('lat', 'obs')), may hold values from 0 to 1
- obs_lon_frac: bfloat16 [256, 16, 256], P(('lat', 'obs')), may hold values from 0 to 1
- obs_corner: int32 [256, 16, 256], P(('lat', 'obs')), may hold values from 0 to 1023
- obs_channel: int32 [256, 16, 256], P(('lat', 'obs')), may hold values from 0 to 255
- slot_counts: int32 [256, 256], P(('lat', 'obs')), may hold values from 0 to 16, as said below
Outputs:
- grid_grad: bfloat16 [512, 1024, 256], P(('lat', 'obs'), None, 'chan')
- gain_grad: float32 [2, 512, 256], P(None, None, 'chan')
Inputs may be any that keep to these rules, and one draw needn't show every extreme that they name: `order_slots`: each order from 0 to 511 stands at exactly one slot. `legendre`: entry [s, l, lat] is zero wherever l < order_slots[s]. `slot_counts`: at most 16; in every draw some tile receives 16 live slots from every source shard; slots at or beyond the count carry no observation.
All inputs are finite; a program needn't handle non-finite values.
Results may differ from a plain program's by a relative error of at most 0.0055.
Values may be sent and summed in bfloat16 or wider, within the bound.
No kernel may reach another device: no remote copies, remote signals or barrier semaphores. Data moves between devices by JAX's collectives and lax.ppermute only.
A program may use at most 64 MiB of HBM per device.

v0:
```python
import math

import jax
import jax.numpy as jnp
from jax import lax
from jax.sharding import PartitionSpec as P


def gelu_slope(pre_act):
    values = pre_act.astype(jnp.float32)
    normal_cdf = 0.5 * (1.0 + jax.scipy.special.erf(values * 0.7071067811865476))
    density = jnp.exp(-0.5 * values * values) * 0.3989422804014327
    return normal_cdf + values * density


def zonal_tables(orders, longitudes, lon_count, cos_weight, sin_weight):
    phase = orders[:, None] * longitudes[None, :] % lon_count
    angle = phase.astype(jnp.float32) * (2.0 * math.pi / lon_count)
    return (
        (cos_weight * jnp.cos(angle)).astype(jnp.bfloat16),
        (sin_weight * jnp.sin(angle)).astype(jnp.bfloat16),
    )


def adjoint_tiles(
    amounts, lat_frac, lon_frac, corners, channels, lat_dev, lon_count, chan_base, width
):
    received = amounts.size
    amounts = amounts.reshape(received)
    lat_frac = lat_frac.reshape(received)
    lon_frac = lon_frac.reshape(received)
    corners = corners.reshape(received)
    channels = channels.reshape(received)
    block_rows = min(512, received)
    cell_ids = lax.iota(jnp.int32, lat_dev * lon_count)
    chan_ids = chan_base + lax.iota(jnp.int32, width)
    nothing = jnp.zeros((), jnp.bfloat16)

    def add_block(counter, summed):
        offset = counter * block_rows
        lat_step = lax.dynamic_slice_in_dim(lat_frac, offset, block_rows).astype(jnp.float32)
        lon_step = lax.dynamic_slice_in_dim(lon_frac, offset, block_rows).astype(jnp.float32)
        corner_ids = lax.dynamic_slice_in_dim(corners, offset, block_rows)
        chan_rows = lax.dynamic_slice_in_dim(channels, offset, block_rows)
        amount_rows = lax.dynamic_slice_in_dim(amounts, offset, block_rows)
        top = corner_ids // lon_count
        left = corner_ids % lon_count
        right = (left + 1) % lon_count
        lower = top * lon_count
        upper = lower + lon_count
        weights = (
            (1.0 - lat_step) * (1.0 - lon_step),
            (1.0 - lat_step) * lon_step,
            lat_step * (1.0 - lon_step),
            lat_step * lon_step,
        )
        places = (lower + left, lower + right, upper + left, upper + right)
        stencil = jnp.zeros((block_rows, lat_dev * lon_count), jnp.bfloat16)
        for weight, place in zip(weights, places):
            stencil = stencil + jnp.where(
                cell_ids[None, :] == place[:, None], weight.astype(jnp.bfloat16)[:, None], nothing
            )
        sources = jnp.where(chan_rows[:, None] == chan_ids[None, :], amount_rows[:, None], nothing)
        return summed + lax.dot_general(
            stencil, sources, (((0,), (0,)), ((), ())), preferred_element_type=jnp.float32
        )

    start_sum = jnp.zeros((lat_dev * lon_count, width), jnp.float32)
    summed = lax.fori_loop(0, received // block_rows, add_block, start_sum)
    return summed.reshape(lat_dev, lon_count, width)


def on_device(
    next_grad,
    pre_act,
    legendre,
    order_slots,
    quad_weights,
    spectral_gain,
    saved_coeffs,
    obs_value,
    obs_lat_frac,
    obs_lon_frac,
    obs_corner,
    obs_channel,
    slot_counts,
):
    lat_dev, lon_count, width = next_grad.shape
    lat_size = lax.axis_size("lat")
    obs_size = lax.axis_size("obs")
    slot_dev, degrees, lat_count = legendre.shape
    total_orders = order_slots.shape[0]
    capacity = obs_value.shape[1]
    alive_slots = lax.iota(jnp.int32, capacity)[:, None] < slot_counts[0][None, :]
    masked = jnp.where(alive_slots, obs_value[0], jnp.zeros((), jnp.bfloat16)).reshape(
        capacity, lat_size, obs_size
    )
    lat_frac = obs_lat_frac[0].reshape(capacity, lat_size, obs_size)
    lon_frac = obs_lon_frac[0].reshape(capacity, lat_size, obs_size)
    corners = obs_corner[0].reshape(capacity, lat_size, obs_size)
    channels = obs_channel[0].reshape(capacity, lat_size, obs_size)
    arrived = (
        lax.all_to_all(
            lax.all_to_all(masked, "lat", split_axis=1, concat_axis=1, tiled=True),
            "obs",
            split_axis=2,
            concat_axis=2,
            tiled=True,
        ),
        lax.all_to_all(
            lax.all_to_all(lat_frac, "lat", split_axis=1, concat_axis=1, tiled=True),
            "obs",
            split_axis=2,
            concat_axis=2,
            tiled=True,
        ),
        lax.all_to_all(
            lax.all_to_all(lon_frac, "lat", split_axis=1, concat_axis=1, tiled=True),
            "obs",
            split_axis=2,
            concat_axis=2,
            tiled=True,
        ),
        lax.all_to_all(
            lax.all_to_all(corners, "lat", split_axis=1, concat_axis=1, tiled=True),
            "obs",
            split_axis=2,
            concat_axis=2,
            tiled=True,
        ),
        lax.all_to_all(
            lax.all_to_all(channels, "lat", split_axis=1, concat_axis=1, tiled=True),
            "obs",
            split_axis=2,
            concat_axis=2,
            tiled=True,
        ),
    )
    chan_base = lax.axis_index("chan") * width
    obs_grad = adjoint_tiles(
        arrived[0],
        arrived[1],
        arrived[2],
        arrived[3],
        arrived[4],
        lat_dev,
        lon_count,
        chan_base,
        width,
    )
    out_grad = next_grad.astype(jnp.float32) + obs_grad
    pre_grad = (out_grad * gelu_slope(pre_act)).astype(jnp.bfloat16)
    longitudes = lax.iota(jnp.int32, lon_count)
    crossed_orders = jnp.transpose(
        order_slots.reshape(lat_size, obs_size, slot_dev), (1, 0, 2)
    ).reshape(total_orders)
    legendre_view = legendre.reshape(slot_dev, degrees, lat_size, obs_size, lat_dev)
    weight_view = quad_weights.reshape(lat_size, obs_size, lat_dev)
    factor = jnp.where(order_slots == 0, 1.0, 2.0).astype(jnp.float32)[:, None]
    cosine, sine = zonal_tables(order_slots, longitudes, lon_count, factor, -factor)
    real_part = jnp.einsum("mn,knc->mkc", cosine, pre_grad, preferred_element_type=jnp.float32)
    imag_part = jnp.einsum("mn,knc->mkc", sine, pre_grad, preferred_element_type=jnp.float32)
    by_order = lax.all_to_all(
        lax.all_to_all(
            jnp.stack([real_part, imag_part], axis=1).astype(jnp.bfloat16),
            "lat",
            split_axis=0,
            concat_axis=2,
            tiled=True,
        ),
        "obs",
        split_axis=0,
        concat_axis=2,
        tiled=True,
    )
    order_view = by_order.reshape(slot_dev, 2, obs_size, lat_size, lat_dev, width)
    up_grad = jnp.einsum(
        "iljka,irkjac->irlc", legendre_view, order_view, preferred_element_type=jnp.float32
    )
    saved = saved_coeffs.astype(jnp.float32)
    gain_terms = jnp.stack(
        [
            jnp.sum(up_grad[:, 0] * saved[:, 0] + up_grad[:, 1] * saved[:, 1], axis=0),
            jnp.sum(up_grad[:, 1] * saved[:, 0] - up_grad[:, 0] * saved[:, 1], axis=0),
        ]
    )
    gain_grad = lax.psum(gain_terms, ("lat", "obs"))
    gain_real = spectral_gain[0]
    gain_imag = spectral_gain[1]
    coeff_grad = jnp.stack(
        [
            gain_real * up_grad[:, 0] + gain_imag * up_grad[:, 1],
            gain_real * up_grad[:, 1] - gain_imag * up_grad[:, 0],
        ],
        axis=1,
    ).astype(jnp.bfloat16)
    analysed = jnp.einsum(
        "iljka,irlc->irjkac", legendre_view, coeff_grad, preferred_element_type=jnp.float32
    )
    lat_grad = (
        (analysed * weight_view[None, None, :, :, :, None])
        .astype(jnp.bfloat16)
        .reshape(slot_dev, 2, lat_count, width)
    )
    by_lat = lax.all_to_all(
        lax.all_to_all(lat_grad, "lat", split_axis=2, concat_axis=0, tiled=True),
        "obs",
        split_axis=2,
        concat_axis=0,
        tiled=True,
    )
    scale = jnp.full((total_orders, 1), 1.0 / lon_count, jnp.float32)
    cosine, sine = zonal_tables(crossed_orders, longitudes, lon_count, scale, -scale)
    spectral_grad = jnp.einsum(
        "mkc,mn->knc", by_lat[:, 0], cosine, preferred_element_type=jnp.float32
    )
    spectral_grad = spectral_grad + jnp.einsum(
        "mkc,mn->knc", by_lat[:, 1], sine, preferred_element_type=jnp.float32
    )
    grid_grad = (out_grad + spectral_grad).astype(jnp.bfloat16)
    return (grid_grad, gain_grad)


def solution(mesh):
    in_specs = (
        P(("lat", "obs"), None, "chan"),
        P(("lat", "obs"), None, "chan"),
        P(("lat", "obs"), None, None),
        P(),
        P(),
        P(None, None, "chan"),
        P(("lat", "obs"), None, None, "chan"),
        P(("lat", "obs"), None, None),
        P(("lat", "obs"), None, None),
        P(("lat", "obs"), None, None),
        P(("lat", "obs"), None, None),
        P(("lat", "obs"), None, None),
        P(("lat", "obs"), None),
    )
    out_specs = (P(("lat", "obs"), None, "chan"), P(None, None, "chan"))
    return jax.shard_map(
        on_device, mesh=mesh, in_specs=in_specs, out_specs=out_specs, check_vma=False
    )
```

profile of v0, /device:TPU:6, one launch (start us, length us, event | category | flops | bytes accessed | tf_op | source)
XLA Modules:
  0.0 503.7 jit_solution(1128982922786016238)
XLA Ops:
  7.2 0.8 copy.98
  8.5 1.3 reduce.5
  10.0 0.8 fusion.88
  10.7 16.6 %all-to-all-start.8 = ((bf16[16,64,4]{0,2,1:T(4,128)(2,1)}), bf16[16,64,4]{0,2,1:T(4,128)(2,1)S(1)}, u32[]{:S(2)}, u32[]{:S(2)}) async-start(bf16[16,64,4]{0,2,1:T(4,128)(2,1)} %fusion.88), calls=%async_computation.8 | async-start | bytes 131072 | tf_op jit(solution)/shard_map/all_to_all | solution.py:104
  27.4 1.4 copy.89
  28.8 10.8 %all-to-all-done.8 = bf16[16,64,4]{0,2,1:T(4,128)(2,1)S(1)} async-done(((bf16[16,64,4]{0,2,1:T(4,128)(2,1)}), bf16[16,64,4]{0,2,1:T(4,128)(2,1)S(1)}, u32[]{:S(2)}, u32[]{:S(2)}) %all-to-all-start.8) | async-done | bytes 8224 | tf_op jit(solution)/shard_map/all_to_all | solution.py:104
  39.6 4.6 all-to-all-start.2
  44.2 1.4 copy.92
  45.6 10.8 %all-to-all-done.2 = bf16[16,64,4]{0,2,1:T(4,128)(2,1)S(1)} async-done(((bf16[16,64,4]{0,2,1:T(4,128)(2,1)}), bf16[16,64,4]{0,2,1:T(4,128)(2,1)S(1)}, u32[]{:S(2)}, u32[]{:S(2)}) %all-to-all-start.2) | async-done | bytes 8224 | tf_op jit(solution)/shard_map/all_to_all | solution.py:111
  56.4 4.6 all-to-all-start.4
  61.1 0.7 reshape.104
  61.8 11.4 %all-to-all-done.4 = bf16[16,64,4]{0,2,1:T(4,128)(2,1)S(1)} async-done(((bf16[16,64,4]{0,2,1:T(4,128)(2,1)}), bf16[16,64,4]{0,2,1:T(4,128)(2,1)S(1)}, u32[]{:S(2)}, u32[]{:S(2)}) %all-to-all-start.4) | async-done | bytes 8224 | tf_op jit(solution)/shard_map/all_to_all | solution.py:118
  73.3 4.8 all-to-all-start.9
  78.1 0.7 reshape.98
  78.8 2.5 all-to-all-done.9
  81.3 5.3 %all-to-all-start.3 = ((bf16[4,2,512]{2,1,0:T(2,128)(2,1)}), bf16[4,2,512]{2,1,0:T(2,128)(2,1)S(1)}, u32[]{:S(2)}, u32[]{:S(2)}) async-start(bf16[4,2,512]{2,1,0:T(2,128)(2,1)} %reshape.98), calls=%async_computation.3 | async-start | bytes 16384 | tf_op jit(solution)/shard_map/all_to_all | solution.py:110
  86.7 0.7 reshape.100
  87.4 2.5 all-to-all-done.3
  89.8 5.3 %all-to-all-start.5 = ((bf16[4,2,512]{2,1,0:T(2,128)(2,1)}), bf16[4,2,512]{2,1,0:T(2,128)(2,1)S(1)}, u32[]{:S(2)}, u32[]{:S(2)}) async-start(bf16[4,2,512]{2,1,0:T(2,128)(2,1)} %reshape.100), calls=%async_computation.5 | async-start | bytes 16384 | tf_op jit(solution)/shard_map/all_to_all | solution.py:117
  95.1 0.8 copy.86
  95.9 2.5 all-to-all-done.5
  98.4 4.6 all-to-all-start
  103.0 0.8 copy.95
  103.8 11.9 %all-to-all-done = s32[16,64,4]{0,2,1:T(4,128)S(1)} async-done(((s32[16,64,4]{0,2,1:T(4,128)}), s32[16,64,4]{0,2,1:T(4,128)S(1)}, u32[]{:S(2)}, u32[]{:S(2)}) %all-to-all-start) | async-done | bytes 16416 | tf_op jit(solution)/shard_map/all_to_all | solution.py:125
  115.7 4.6 all-to-all-start.6
  120.4 0.7 reshape.96
  121.1 11.9 %all-to-all-done.6 = s32[16,64,4]{0,2,1:T(4,128)S(1)} async-done(((s32[16,64,4]{0,2,1:T(4,128)}), s32[16,64,4]{0,2,1:T(4,128)S(1)}, u32[]{:S(2)}, u32[]{:S(2)}) %all-to-all-start.6) | async-done | bytes 16416 | tf_op jit(solution)/shard_map/all_to_all | solution.py:132
  133.0 5.3 %all-to-all-start.1 = ((s32[4,1,1024]{2,1,0:T(1,128)}), s32[4,1,1024]{2,1,0:T(1,128)S(1)}, u32[]{:S(2)}, u32[]{:S(2)}) async-start(s32[4,1,1024]{2,1,0:T(1,128)} %reshape.96), calls=%async_computation.1 | async-start | bytes 32768 | tf_op jit(solution)/shard_map/all_to_all | solution.py:124
  138.4 0.7 reshape.102
  139.1 2.5 all-to-all-done.1
  141.6 5.3 %all-to-all-start.7 = ((s32[4,1,1024]{2,1,0:T(1,128)}), s32[4,1,1024]{2,1,0:T(1,128)S(1)}, u32[]{:S(2)}, u32[]{:S(2)}) async-start(s32[4,1,1024]{2,1,0:T(1,128)} %reshape.102), calls=%async_computation.7 | async-start | bytes 32768 | tf_op jit(solution)/shard_map/all_to_all | solution.py:131
  149.4 0.6 reduce.6
  150.6 0.6 reduce.7
  151.9 26.5 %while.17 = (s32[]{:T(128)}, f32[2048,128]{1,0:T(8,128)S(1)}, s32[4096]{0:T(1024)S(1)}, bf16[4096]{0:T(1024)(128)(2,1)S(1)}, bf16[4096]{0:T(1024)(128)(2,1)S(1)}...) while((s32[]{:T(128)}, f32[2048,128]{1,0:T(8,128)S(1)}, ...), condition=%wide.region_1.2_spmd.clone.clone, body=%wide.region_0.1_spmd.clone.clone.sunk | while | flops 285898880 | bytes 2142405 | solution.py:69
  152.3 2.9 convolution_add_fusion.3
  155.6 2.9 convolution_add_fusion.3
  159.0 2.9 convolution_add_fusion.3
  162.3 2.9 convolution_add_fusion.3
  165.6 2.9 convolution_add_fusion.3
  168.9 2.9 convolution_add_fusion.3
  172.2 2.9 convolution_add_fusion.3
  175.5 2.9 convolution_add_fusion.3
  178.5 0.6 fusion.84
  179.4 8.6 %fusion.56 = bf16[512,1,2,128]{3,0,2,1:T(8,128)(2,1)S(1)} fusion(bf16[2,1024,128]{2,1,0:T(8,128)(2,1)S(1)} %fusion.84, f32[512]{0:T(512)S(1)} %get-tuple-element.328, s32[512]{0:T(512)S(1)} %copy-done.11), kind=kOutput, calls=%fused_computation.93 | convolution fusion | flops 276955136 | bytes 790528 | tf_op jit(solution)/shard_map/mn,knc->mkc/dot_general | solution.py:161
  188.0 8.7 %fusion.57 = bf16[512,1,2,128]{3,0,2,1:T(8,128)(2,1)S(1)} fusion(bf16[2,1024,128]{2,1,0:T(8,128)(2,1)S(1)} %fusion.84, f32[512]{0:T(512)S(1)} %get-tuple-element.329, s32[512]{0:T(512)S(1)} %copy-done.11), kind=kOutput, calls=%fused_computation.94 | convolution fusion | flops 276955136 | bytes 790528 | tf_op jit(solution)/shard_map/mn,knc->mkc/dot_general | solution.py:162
  197.3 19.3 %all_to_all.119 = bf16[512,2,2,128]{3,2,1,0:T(2,128)(2,1)S(1)} all-to-all(bf16[512,2,2,128]{3,2,1,0:T(2,128)(2,1)S(1)} %copy.105), channel_id=1, replica_groups=mesh['lat'=64,'chan'=2,'obs'=4] {'lat'}, dimensions={0} | all-to-all | bytes 1048576 | tf_op jit(solution)/shard_map/all_to_all | solution.py:164
  216.8 0.9 copy.108
  217.7 5.3 %all-to-all-start.11 = ((bf16[8,2,128,128]{3,2,1,0:T(8,128)(2,1)}), bf16[8,2,128,128]{3,2,1,0:T(8,128)(2,1)S(1)}, u32[]{:S(2)}, u32[]{:S(2)}) async-start(bf16[8,2,128,128]{3,2,1,0:T(8,128)(2,1)} %copy.108), calls=%async_computation.11 | async-start | bytes 1048576 | tf_op jit(solution)/shard_map/all_to_all | solution.py:163
  223.0 1.0 copy.110
  224.2 0.8 copy.113
  225.5 0.5 copy-done.12
  226.3 2.7 all-to-all-done.11
  229.0 1.4 convolution_bitcast_fusion
  230.8 0.7 fusion.55
  232.1 1.3 copy.118
  233.4 5.1 %all-to-all-start.12 = ((bf16[2,2,512,128]{3,1,0,2:T(2,128)(2,1)}), bf16[2,2,512,128]{3,1,0,2:T(2,128)(2,1)S(1)}, u32[]{:S(2)}, u32[]{:S(2)}) async-start(bf16[2,2,512,128]{3,1,0,2:T(2,128)(2,1)} %copy.118), calls=%async_computation.12 | async-start | bytes 1048576 | tf_op jit(solution)/shard_map/all_to_all | solution.py:206
  238.5 0.8 pad_maximum_fusion.1
  239.4 14.6 %all-to-all-done.12 = bf16[2,2,512,128]{3,1,0,2:T(2,128)(2,1)S(1)} async-done(((bf16[2,2,512,128]{3,1,0,2:T(2,128)(2,1)}), bf16[2,2,512,128]{3,1,0,2:T(2,128)(2,1)S(1)}, u32[]{:S(2)}, u32[]{:S(2)}) %all-to-all-start.12) | async-done | bytes 524320 | tf_op jit(solution)/shard_map/all_to_all | solution.py:206
  254.2 1.2 copy.121
  255.4 5.5 %all-to-all-start.13 = ((bf16[128,2,8,128]{3,1,0,2:T(2,128)(2,1)}), bf16[128,2,8,128]{3,1,0,2:T(2,128)(2,1)S(1)}, u32[]{:S(2)}, u32[]{:S(2)}) async-start(bf16[128,2,8,128]{3,1,0,2:T(2,128)(2,1)} %copy.121), calls=%async_computation.13 | async-start | bytes 1048576 | tf_op jit(solution)/shard_map/all_to_all | solution.py:205
  261.2 216.4 %all-reduce.2.cloned.1.call-done = f32[2,512,128]{1,2,0:T(8,128)} async-done(((f32[2,512,128]{1,2,0:T(8,128)}), f32[2,512,128]{1,2,0:T(8,128)}) %all-reduce.2.cloned.1.call-update) | async-done | bytes 524304 | tf_op jit(solution)/shard_map/psum | solution.py:187
  477.7 2.0 copy.125
  479.9 7.9 %fusion.66 = f32[1024,2,128]{2,0,1:T(8,128)S(1)} fusion(s32[512]{0:T(512)S(1)} %mul.216, bf16[512,2,2,128]{3,0,2,1:T(8,128)(2,1)S(1)} %bitcast.105), kind=kOutput, calls=%fused_computation.103 | convolution fusion | flops 276824064 | bytes 1312768 | tf_op jit(solution)/shard_map/mkc,mn->knc/dot_general | solution.py:214
  487.8 9.1 %fusion.54 = bf16[2,1024,128]{2,1,0:T(8,128)(2,1)} fusion(f32[1024,2,128]{2,0,1:T(8,128)S(1)} %fusion.66, s32[512]{0:T(512)S(1)} %mul.216, f32[2,1024,128]{2,1,0:T(8,128)S(1)} %bitcast.104, bf16[2,1024,128]{2,1,0:T(8,128)(2,1)S(1)} %copy-done.6, bf16[512,2,2,128]{3,0,2,1:T(8,128)(2,1)S(1)} %bitcast.106), kind=kOutput, calls=%fused_computation.89 | convolution fusion | flops 278134784 | bytes 3409920 | tf_op jit(solution)/shard_map/mkc,mn->knc/dot_general | solution.py:217
  (121 shorter events, 11.8 us)
Async XLA Ops:
  7.2 88.0 %copy-start.9 = (s32[1,16,256]{2,1,0:T(8,128)S(1)}, s32[1,16,256]{2,1,0:T(8,128)}, u32[]{:S(2)}) copy-start(s32[1,16,256]{2,1,0:T(8,128)} %param.25) | copy-start | bytes 49156
  7.2 95.8 %copy-start.10 = (s32[1,16,256]{2,1,0:T(8,128)S(1)}, s32[1,16,256]{2,1,0:T(8,128)}, u32[]{:S(2)}) copy-start(s32[1,16,256]{2,1,0:T(8,128)} %param.26) | copy-start | bytes 49156
  10.7 28.8 %all-to-all-start.8 = ((bf16[16,64,4]{0,2,1:T(4,128)(2,1)}), bf16[16,64,4]{0,2,1:T(4,128)(2,1)S(1)}, u32[]{:S(2)}, u32[]{:S(2)}) async-start(bf16[16,64,4]{0,2,1:T(4,128)(2,1)} %fusion.88), calls=%async_computation.8 | async-start | bytes 131072 | tf_op jit(solution)/shard_map/all_to_all | solution.py:104
  27.3 119.5 %copy-start.11 = (s32[512]{0:T(512)S(1)}, s32[512]{0:T(512)}, u32[]{:S(2)}) copy-start(s32[512]{0:T(512)} %param.18) | copy-start | bytes 6148
  39.6 16.8 %all-to-all-start.2 = ((bf16[16,64,4]{0,2,1:T(4,128)(2,1)}), bf16[16,64,4]{0,2,1:T(4,128)(2,1)S(1)}, u32[]{:S(2)}, u32[]{:S(2)}) async-start(bf16[16,64,4]{0,2,1:T(4,128)(2,1)} %bitcast.1), calls=%async_computation.2 | async-start | bytes 131072 | tf_op jit(solution)/shard_map/all_to_all | solution.py:111
  56.4 16.8 %all-to-all-start.4 = ((bf16[16,64,4]{0,2,1:T(4,128)(2,1)}), bf16[16,64,4]{0,2,1:T(4,128)(2,1)S(1)}, u32[]{:S(2)}, u32[]{:S(2)}) async-start(bf16[16,64,4]{0,2,1:T(4,128)(2,1)} %bitcast.2), calls=%async_computation.4 | async-start | bytes 131072 | tf_op jit(solution)/shard_map/all_to_all | solution.py:118
  73.3 8.0 %all-to-all-start.9 = ((bf16[4,2,512]{2,1,0:T(2,128)(2,1)}), bf16[4,2,512]{2,1,0:T(2,128)(2,1)S(1)}, u32[]{:S(2)}, u32[]{:S(2)}) async-start(bf16[4,2,512]{2,1,0:T(2,128)(2,1)} %reshape.104), calls=%async_computation.9 | async-start | bytes 16384 | tf_op jit(solution)/shard_map/all_to_all | solution.py:103
  81.3 8.5 %all-to-all-start.3 = ((bf16[4,2,512]{2,1,0:T(2,128)(2,1)}), bf16[4,2,512]{2,1,0:T(2,128)(2,1)S(1)}, u32[]{:S(2)}, u32[]{:S(2)}) async-start(bf16[4,2,512]{2,1,0:T(2,128)(2,1)} %reshape.98), calls=%async_computation.3 | async-start | bytes 16384 | tf_op jit(solution)/shard_map/all_to_all | solution.py:110
  89.8 8.5 %all-to-all-start.5 = ((bf16[4,2,512]{2,1,0:T(2,128)(2,1)}), bf16[4,2,512]{2,1,0:T(2,128)(2,1)S(1)}, u32[]{:S(2)}, u32[]{:S(2)}) async-start(bf16[4,2,512]{2,1,0:T(2,128)(2,1)} %reshape.100), calls=%async_computation.5 | async-start | bytes 16384 | tf_op jit(solution)/shard_map/all_to_all | solution.py:117
  98.4 17.3 %all-to-all-start = ((s32[16,64,4]{0,2,1:T(4,128)}), s32[16,64,4]{0,2,1:T(4,128)S(1)}, u32[]{:S(2)}, u32[]{:S(2)}) async-start(s32[16,64,4]{0,2,1:T(4,128)} %bitcast), calls=%async_computation | async-start | bytes 262144 | tf_op jit(solution)/shard_map/all_to_all | solution.py:125
  115.7 17.3 %all-to-all-start.6 = ((s32[16,64,4]{0,2,1:T(4,128)}), s32[16,64,4]{0,2,1:T(4,128)S(1)}, u32[]{:S(2)}, u32[]{:S(2)}) async-start(s32[16,64,4]{0,2,1:T(4,128)} %bitcast.3), calls=%async_computation.6 | async-start | bytes 262144 | tf_op jit(solution)/shard_map/all_to_all | solution.py:132
  133.0 8.6 %all-to-all-start.1 = ((s32[4,1,1024]{2,1,0:T(1,128)}), s32[4,1,1024]{2,1,0:T(1,128)S(1)}, u32[]{:S(2)}, u32[]{:S(2)}) async-start(s32[4,1,1024]{2,1,0:T(1,128)} %reshape.96), calls=%async_computation.1 | async-start | bytes 32768 | tf_op jit(solution)/shard_map/all_to_all | solution.py:124
  141.6 9.0 %all-to-all-start.7 = ((s32[4,1,1024]{2,1,0:T(1,128)}), s32[4,1,1024]{2,1,0:T(1,128)S(1)}, u32[]{:S(2)}, u32[]{:S(2)}) async-start(s32[4,1,1024]{2,1,0:T(1,128)} %reshape.102), calls=%async_computation.7 | async-start | bytes 32768 | tf_op jit(solution)/shard_map/all_to_all | solution.py:131
  151.9 26.6 %copy-start.4 = (bf16[2,1024,128]{2,1,0:T(8,128)(2,1)S(1)}, bf16[2,1024,128]{2,1,0:T(8,128)(2,1)}, u32[]{:S(2)}) copy-start(bf16[2,1024,128]{2,1,0:T(8,128)(2,1)} %param.16) | copy-start | bytes 1572868
  151.9 26.6 %copy-start.5 = (bf16[2,1024,128]{2,1,0:T(8,128)(2,1)S(1)}, bf16[2,1024,128]{2,1,0:T(8,128)(2,1)}, u32[]{:S(2)}) copy-start(bf16[2,1024,128]{2,1,0:T(8,128)(2,1)} %param.15) | copy-start | bytes 1572868
  178.4 1.0 copy-start.2
  216.8 6.2 %copy-start.1 = (bf16[2,512,512]{2,1,0:T(8,128)(2,1)S(1)}, bf16[2,512,512]{2,1,0:T(8,128)(2,1)}, u32[]{:S(2)}) copy-start(bf16[2,512,512]{2,1,0:T(8,128)(2,1)} %param.17) | copy-start | bytes 3145732
  217.7 11.3 %all-to-all-start.11 = ((bf16[8,2,128,128]{3,2,1,0:T(8,128)(2,1)}), bf16[8,2,128,128]{3,2,1,0:T(8,128)(2,1)S(1)}, u32[]{:S(2)}, u32[]{:S(2)}) async-start(bf16[8,2,128,128]{3,2,1,0:T(8,128)(2,1)} %copy.108), calls=%async_computation.11 | async-start | bytes 1048576 | tf_op jit(solution)/shard_map/all_to_all | solution.py:163
  223.0 1.0 copy-start.7
  224.1 1.0 copy-start.8
  225.3 0.7 copy-start.12
  229.0 1.4 copy-start
  233.4 20.6 %all-to-all-start.12 = ((bf16[2,2,512,128]{3,1,0,2:T(2,128)(2,1)}), bf16[2,2,512,128]{3,1,0,2:T(2,128)(2,1)S(1)}, u32[]{:S(2)}, u32[]{:S(2)}) async-start(bf16[2,2,512,128]{3,1,0,2:T(2,128)(2,1)} %copy.118), calls=%async_computation.12 | async-start | bytes 1048576 | tf_op jit(solution)/shard_map/all_to_all | solution.py:206
  238.5 239.2 %all-reduce.2.cloned.1.call-start = ((), (), s32[]{:S(2)}) async-start(), calls=%async_computation.14 | async-start | bytes 1048576 | tf_op jit(solution)/shard_map/psum | solution.py:187
  255.4 224.4 %all-to-all-start.13 = ((bf16[128,2,8,128]{3,1,0,2:T(2,128)(2,1)}), bf16[128,2,8,128]{3,1,0,2:T(2,128)(2,1)S(1)}, u32[]{:S(2)}, u32[]{:S(2)}) async-start(bf16[128,2,8,128]{3,1,0,2:T(2,128)(2,1)} %copy.121), calls=%async_computation.13 | async-start | bytes 1048576 | tf_op jit(solution)/shard_map/all_to_all | solution.py:205
  479.9 7.9 %copy-start.3 = (f32[2048,128]{1,0:T(8,128)S(1)}, f32[2048,128]{1,0:T(8,128)}, u32[]{:S(2)}) copy-start(f32[2048,128]{1,0:T(8,128)} %copy-done.2) | copy-start | bytes 3145732
  479.9 7.9 %copy-start.6 = (bf16[2,1024,128]{2,1,0:T(8,128)(2,1)S(1)}, bf16[2,1024,128]{2,1,0:T(8,128)(2,1)}, u32[]{:S(2)}) copy-start(bf16[2,1024,128]{2,1,0:T(8,128)(2,1)} %param.15) | copy-start | bytes 1572868
Sparse Core Ops, SparseCore 0:
  244.4 233.2 all-reduce.1
where the time goes:
time: 505 us; the launch traced here: 504 us
  waiting for transfers between devices  300 us (59%)
  starting transfers between devices  76.9 us (15%)
  matrix products  59.3 us (12%)
  local copies, waits for them, and re-layouts  25.6 us (5%)
  blocking collectives  19.3 us (4%)
  between operations  14.5 us (3%)
  other arithmetic  7.4 us (1%)
    psum x1, waiting for transfers between devices, on_device(): gain_grad = lax.psum(gain_terms, ('lat', 'obs'))  216 us
    dot_general x8, matrix products, add_block(): lax.dot_general(stencil, sources, (((0,), (0,)), ((), ())), preferred_ele...  22.9 us
    all_to_all x1, blocking collectives, on_device(): lax.all_to_all(jnp.stack([real_part, imag_part], axis=1).astype(jnp.bfloa...  19.3 us
    all_to_all x1, starting transfers between devices, on_device(): lax.all_to_all(masked, 'lat', split_axis=1, concat_axis=1, tiled=True)  16.6 us
    all_to_all x1, waiting for transfers between devices, on_device(): lax.all_to_all(lat_grad, 'lat', split_axis=2, concat_axis=0, tiled=True)  14.6 us
    unnamed x45, local copies, waits for them, and re-layouts  14 us
    all_to_all x1, waiting for transfers between devices, on_device(): lax.all_to_all(corners, 'lat', split_axis=1, concat_axis=1, tiled=True)  11.9 us
    all_to_all x1, waiting for transfers between devices, on_device(): lax.all_to_all(channels, 'lat', split_axis=1, concat_axis=1, tiled=True)  11.9 us
  transfers between devices with their start and end apart: 14, of which 12 were waited for; matrix products, arithmetic and copies ran while one was open for 4% of the time, Pallas kernels for 0%

commit v1 on v0

v1 whole, which is shorter than its diff:
```python
import math

import jax
import jax.numpy as jnp
import numpy as np
from jax import lax
from jax.experimental import pallas as pl
from jax.experimental.pallas import tpu as pltpu
from jax.sharding import PartitionSpec as P

BF = jnp.bfloat16
F32 = jnp.float32
NT = (((1,), (1,)), ((), ()))
RANKS = ("lat", "obs")


def dot(left, right):
    return jnp.dot(left, right, preferred_element_type=F32)


def dot_nt(left, right):
    return lax.dot_general(left, right, NT, preferred_element_type=F32)


def call(kernel, out_shape, scratch=(), smem=0, flops=0, limit=40):
    outs = out_shape if isinstance(out_shape, tuple) else (out_shape,)
    moved = sum(math.prod(o.shape) * o.dtype.itemsize for o in outs)

    def run(*args):
        specs = [
            pl.BlockSpec(memory_space=pltpu.SMEM if i < smem else pltpu.VMEM)
            for i in range(len(args))
        ]
        total = moved + sum(math.prod(a.shape) * a.dtype.itemsize for a in args)
        return pl.pallas_call(
            kernel,
            out_shape=out_shape,
            in_specs=specs,
            out_specs=jax.tree.map(lambda _: pl.BlockSpec(memory_space=pltpu.VMEM), out_shape),
            scratch_shapes=list(scratch),
            compiler_params=pltpu.CompilerParams(vmem_limit_bytes=limit << 20),
            cost_estimate=pl.CostEstimate(flops=flops, bytes_accessed=total, transcendentals=0),
        )(*args)

    return run


def iota(shape, axis):
    return lax.broadcasted_iota(jnp.int32, shape, axis)


def pack_kernel(base_ref, value_ref, lat_ref, lon_ref, corner_ref, chan_ref, count_ref, out_ref):
    capacity, tiles = value_ref.shape
    alive = iota((capacity, tiles), 0) < count_ref[...]
    value = jnp.where(alive, value_ref[...].astype(F32), 0.0)
    corner = corner_ref[...]
    fields = [
        value,
        lat_ref[...].astype(F32),
        lon_ref[...].astype(F32),
        (corner // 32).astype(F32),
        (corner % 32).astype(F32),
        (chan_ref[...] - base_ref[0]).astype(F32),
        jnp.zeros((128 - 6 * capacity, tiles), F32),
    ]
    out_ref[...] = jnp.concatenate(fields, axis=0).T.astype(BF)


def ready_kernel(pre_ref, legendre_ref, quad_ref, slope_ref, up_ref, down_ref, weight_ref):
    values = pre_ref[...].astype(F32)
    cdf = 0.5 * (1.0 + lax.erf(values * 0.7071067811865476))
    density = jnp.exp(-0.5 * values * values) * 0.3989422804014327
    slope_ref[...] = cdf + values * density
    lats = legendre_ref.shape[2]
    half = lats // 2
    place = iota((lats, lats), 0)
    lat = iota((lats, lats), 1)
    pick = ((place % half) * 2 + place // half == lat).astype(BF)
    for s in range(legendre_ref.shape[0]):
        table = legendre_ref[s]
        up_ref[s] = dot_nt(table, pick).astype(BF)
        down_ref[s] = dot_nt(pick, table).astype(BF)
    for k in range(2):
        column = quad_ref[:, k : k + 1]
        weight_ref[k * half : (k + 1) * half, :] = jnp.broadcast_to(column, (half, 128))


def synth_kernel(
    slots_ref, next_ref, slope_ref, table_ref, order_ref, sent_ref, grad_ref, rows_ref, cols_ref, acc_ref, msg_ref
):
    lat_dev, lons, width = next_ref.shape
    ranks = slots_ref.shape[0]
    capacity = 16
    fields = slots_ref[...].astype(F32).T
    value = fields[0:16]
    lat_step = fields[16:32]
    lon_step = fields[32:48]
    corner = (fields[48:64] * 32.0 + fields[64:80]).astype(jnp.int32)
    chan = fields[80:96].astype(jnp.int32)
    weights = (
        (1.0 - lat_step) * (1.0 - lon_step),
        lat_step * (1.0 - lon_step),
        (1.0 - lat_step) * lon_step,
        lat_step * lon_step,
    )
    chan_ids = iota((width, ranks), 0)
    for p in range(capacity):
        hit = chan_ids == chan[p : p + 1]
        for k in range(4):
            cols_ref[k * width : (k + 1) * width, p * ranks : (p + 1) * ranks] = jnp.where(
                hit, weights[k][p : p + 1], 0.0
            ).astype(BF)
    block = 256
    for j in range(lons // block):
        lon_ids = iota((block, ranks), 0) + j * block
        for p in range(capacity):
            rows_ref[:, p * ranks : (p + 1) * ranks] = jnp.where(
                lon_ids == corner[p : p + 1], value[p : p + 1], 0.0
            ).astype(BF)
        found = dot_nt(rows_ref[...], cols_ref[...])
        acc_ref[8 + j * block : 8 + (j + 1) * block, :] = found
    acc_ref[7:8, 2 * width :] = acc_ref[7 + lons : 8 + lons, 2 * width :]
    halves = []
    for h in range(2):
        at = h * (lons // 2)
        parts = []
        for k in range(lat_dev):
            here = acc_ref[8 + at : 8 + at + lons // 2, k * width : (k + 1) * width]
            left = acc_ref[7 + at : 7 + at + lons // 2, (2 + k) * width : (3 + k) * width]
            total = next_ref[k, at : at + lons // 2, :].astype(F32) + (here + left)
            grad_ref[k, at : at + lons // 2, :] = total
            parts.append((total * slope_ref[k, at : at + lons // 2, :]).astype(BF))
        halves.extend(parts)
    field = jnp.concatenate(halves, axis=1)
    orders = table_ref.shape[1]
    order_ids = iota((orders, 1), 0)
    sign = jnp.where(order_ids % 2 == 0, 1.0, -1.0)
    scale = jnp.where(order_ids == 0, 1.0, 2.0)
    pair = lat_dev * width
    for r in range(2):
        both = dot(table_ref[r], field)
        total = (both[:, :pair] + sign * both[:, pair:]) * (scale if r == 0 else -scale)
        total = total.astype(BF)
        for s in range(2):
            chosen = (iota((ranks, orders), 1) == order_ref[:, s : s + 1]).astype(BF)
            placed = dot(chosen, total)
            for k in range(lat_dev):
                row = s * 4 + r * 2 + k
                msg_ref[pl.ds(row, ranks, stride=8), :] = placed[:, k * width : (k + 1) * width]
    sent_ref[...] = msg_ref[...].reshape(ranks, 8, width).astype(BF)


def legendre_kernel(
    got_ref, up_ref, down_ref, weight_ref, saved_ref, gain_ref, first_ref, second_ref, msg_ref
):
    ranks, rows, width = got_ref.shape
    msg_ref[...] = got_ref[...].astype(F32).reshape(ranks * rows, width)
    gain_real = gain_ref[0]
    gain_imag = gain_ref[1]
    terms = [None, None]
    columns = []
    for s in range(2):
        parts = []
        for r in range(2):
            lanes = [
                msg_ref[pl.ds(s * 4 + r * 2 + k, ranks, stride=8), :].astype(BF) for k in range(2)
            ]
            parts.append(jnp.concatenate(lanes, axis=0))
        columns.append(jnp.concatenate(parts, axis=1))
    for s in range(2):
        found = dot(up_ref[s], columns[s])
        real = found[:, :width]
        imag = found[:, width:]
        saved_real = saved_ref[s, 0].astype(F32)
        saved_imag = saved_ref[s, 1].astype(F32)
        new = (real * saved_real + imag * saved_imag, imag * saved_real - real * saved_imag)
        terms = [n if t is None else t + n for t, n in zip(terms, new)]
        coeff = jnp.concatenate(
            [gain_real * real + gain_imag * imag, gain_real * imag - gain_imag * real], axis=1
        ).astype(BF)
        lat_grad = dot(down_ref[s], coeff)
        for r in range(2):
            weighted = lat_grad[:, r * width : (r + 1) * width] * weight_ref[...]
            for k in range(2):
                msg_ref[pl.ds(r * 2 + k, ranks, stride=8), :] = weighted[k * ranks : (k + 1) * ranks]
        if s == 1:
            second_ref[...] = msg_ref[...].reshape(ranks, 8, width).astype(BF)
        else:
            first_ref[...] = msg_ref[...].reshape(ranks, 8, width).astype(BF)
    for g in range(2):
        for h in range(2):
            msg_ref[pl.ds(4 + g * 2 + h, ranks, stride=8), :] = terms[g][h * ranks : (h + 1) * ranks]
    whole = msg_ref[...].reshape(ranks, 8, width).astype(BF)
    row = iota((ranks, 8, width), 1)
    first_ref[...] = jnp.where(row < 4, first_ref[...].astype(F32), whole.astype(F32)).astype(BF)


def share_kernel(got_ref, half_ref, sent_ref):
    total = jnp.sum(got_ref[...].astype(F32), axis=0, keepdims=True)
    row = iota(got_ref.shape, 1)
    sent_ref[...] = jnp.where(row < 4, half_ref[...].astype(F32), total).astype(BF)


def spectral_part(got_ref, order_ref, table_ref, msg_ref, s):
    ranks, rows, width = got_ref.shape
    orders = table_ref.shape[1]
    msg_ref[...] = got_ref[...].astype(F32).reshape(ranks * rows, width)
    order_ids = iota((orders, 1), 0)
    sign = jnp.where(order_ids % 2 == 0, 1.0, -1.0)
    chosen = (iota((orders, ranks), 0) == order_ref[s : s + 1, :]).astype(BF)
    total = None
    for r in range(2):
        lanes = [msg_ref[pl.ds(r * 2 + k, ranks, stride=8), :].astype(BF) for k in range(2)]
        placed = dot(chosen, jnp.concatenate(lanes, axis=1))
        both = jnp.concatenate([placed, placed * sign], axis=1).astype(BF)
        part = dot(table_ref[r], both)
        total = part if total is None else total - part
    return total * (1.0 / (2 * orders))


def first_kernel(got_ref, order_ref, table_ref, grad_ref, out_ref, msg_ref):
    lat_dev, lons, width = grad_ref.shape
    part = spectral_part(got_ref, order_ref, table_ref, msg_ref, 0)
    half = lons // 2
    for h in range(2):
        for k in range(lat_dev):
            at = (h * lat_dev + k) * width
            out_ref[k, h * half : (h + 1) * half, :] = (
                grad_ref[k, h * half : (h + 1) * half, :] + part[:, at : at + width]
            )


def second_kernel(got_ref, order_ref, table_ref, grad_ref, out_ref, gain_ref, msg_ref):
    lat_dev, lons, width = grad_ref.shape
    ranks = got_ref.shape[0]
    part = spectral_part(got_ref, order_ref, table_ref, msg_ref, 1)
    half = lons // 2
    for h in range(2):
        for k in range(lat_dev):
            at = (h * lat_dev + k) * width
            out_ref[k, h * half : (h + 1) * half, :] = (
                grad_ref[k, h * half : (h + 1) * half, :] + part[:, at : at + width]
            ).astype(BF)
    for g in range(2):
        for h in range(2):
            gain_ref[g, h * ranks : (h + 1) * ranks, :] = msg_ref[
                pl.ds(4 + g * 2 + h, ranks, stride=8), :
            ]


def exchange(message):
    return lax.all_to_all(message, RANKS, split_axis=0, concat_axis=0, tiled=True)


def on_device(
    next_grad,
    pre_act,
    legendre,
    order_slots,
    quad_weights,
    spectral_gain,
    saved_coeffs,
    obs_value,
    obs_lat_frac,
    obs_lon_frac,
    obs_corner,
    obs_channel,
    slot_counts,
):
    lat_dev, lons, width = next_grad.shape
    slot_dev, degrees, lats = legendre.shape
    orders = order_slots.shape[0]
    ranks = lax.axis_size("lat") * lax.axis_size("obs")
    shape = jax.ShapeDtypeStruct

    index = np.arange(orders)
    angle = ((index[:, None] * index[None, :]) % lons).astype(np.float32) * np.float32(
        2.0 * math.pi / lons
    )
    table = jnp.asarray(np.stack([np.cos(angle), np.sin(angle)]).astype(jnp.bfloat16))

    base = (lax.axis_index("chan") * width).astype(jnp.int32).reshape(1)
    packed = call(pack_kernel, shape((ranks, 128), BF), smem=1)(
        base,
        obs_value[0],
        obs_lat_frac[0],
        obs_lon_frac[0],
        obs_corner[0],
        obs_channel[0],
        slot_counts,
    )
    slots = exchange(packed.reshape(ranks, 1, 128)).reshape(ranks, 128)

    slope, up_table, down_table, weight = call(
        ready_kernel,
        (
            shape(next_grad.shape, F32),
            shape(legendre.shape, BF),
            shape((slot_dev, lats, degrees), BF),
            shape((lats, 128), F32),
        ),
        flops=4 * 2 * 512**3,
    )(pre_act, legendre, quad_weights.reshape(ranks, 2))

    order_columns = order_slots.reshape(ranks, 2)
    order_rows = order_columns.T
    message = shape((ranks, 8, width), BF)
    rows = pltpu.VMEM((ranks * 8, width), F32)
    sent, out_grad = call(
        synth_kernel,
        (message, shape(next_grad.shape, F32)),
        scratch=[
            pltpu.VMEM((256, 16 * ranks), BF),
            pltpu.VMEM((4 * width, 16 * ranks), BF),
            pltpu.VMEM((lons + 8, 4 * width), F32),
            rows,
        ],
        flops=2 * 1024 * 4096 * 512,
    )(slots, next_grad, slope, table, order_columns)
    by_order = exchange(sent)
    first, second = call(legendre_kernel, (message, message), scratch=[rows], flops=2 * 512**3 * 4)(
        by_order, up_table, down_table, weight, saved_coeffs, spectral_gain
    )
    first = exchange(first)
    second = exchange(call(share_kernel, message)(first, second))
    partial = call(first_kernel, shape(next_grad.shape, F32), scratch=[rows], flops=2 * 512**3 * 3)(
        first, order_rows, table, out_grad
    )
    return call(
        second_kernel,
        (shape(next_grad.shape, BF), shape((2, degrees, width), F32)),
        scratch=[rows],
        flops=2 * 512**3 * 3,
    )(second, order_rows, table, partial)


def solution(mesh):
    ranks = P(RANKS, None, None)
    in_specs = (
        P(RANKS, None, "chan"),
        P(RANKS, None, "chan"),
        ranks,
        P(),
        P(),
        P(None, None, "chan"),
        P(RANKS, None, None, "chan"),
        ranks,
        ranks,
        ranks,
        ranks,
        ranks,
        P(RANKS, None),
    )
    out_specs = (P(RANKS, None, "chan"), P(None, None, "chan"))
    return jax.shard_map(
        on_device, mesh=mesh, in_specs=in_specs, out_specs=out_specs, check_vma=False
    )
```

time: 505 us -> 143 us (0.28)
  waiting for transfers between devices: 300 us -> 22.8 us
  matrix products: 59.3 us -> 0 us
  starting transfers between devices: 76.9 us -> 30.7 us
  blocking collectives: 19.3 us -> 60.9 us
  Pallas kernels: 0 us -> 13.8 us
  between operations: 14.5 us -> 0.84 us
  local copies, waits for them, and re-layouts: 25.6 us -> 12.8 us
  other arithmetic: 7.4 us -> 0 us
    psum x1 -> x0, waiting for transfers between devices: 216 us -> none  [on_device(): gain_grad = lax.psum(gain_terms, ('lat', 'obs'))]
    all_to_all x13 -> x2, waiting for transfers between devices: 84 us -> 22.8 us  [exchange(): lax.all_to_all(message, RANKS, split_axis=0, concat_axis=0, tiled=True)]
    dot_general x14 -> x0, matrix products: 59.3 us -> none  [the longest x8 22.9 us: add_block(): lax.dot_general(stencil, sources, (((0,), (0,)), ((), ())), preferred_ele...]
    all_to_all x13 -> x2, starting transfers between devices: 76.9 us -> 30.7 us  [exchange(): lax.all_to_all(message, RANKS, split_axis=0, concat_axis=0, tiled=True)]
    all_to_all x1 -> x2, blocking collectives: 19.3 us -> 60.9 us  [exchange(): lax.all_to_all(message, RANKS, split_axis=0, concat_axis=0, tiled=True)]
    pallas_call x0 -> x7, Pallas kernels: none -> 13.8 us  [run(): pl.pallas_call(kernel, out_shape=out_shape, in_specs=specs, out_specs=jax...]
  transfers between devices with their start and end apart: 14 -> 2, of which waited for: 12 -> 2; matrix products, arithmetic and copies ran while one was open for 4% -> 0% of each run, Pallas kernels for 0% -> 2%
where the time goes in v1:
time: 143 us; the launch traced here: 142 us
  blocking collectives  60.9 us (43%)
  starting transfers between devices  30.7 us (21%)
  waiting for transfers between devices  22.8 us (16%)
  Pallas kernels  13.8 us (10%)
  local copies, waits for them, and re-layouts  12.8 us (9%)
    all_to_all x2, blocking collectives, exchange(): lax.all_to_all(message, RANKS, split_axis=0, concat_axis=0, tiled=True)  60.9 us
    all_to_all x2, starting transfers between devices, exchange(): lax.all_to_all(message, RANKS, split_axis=0, concat_axis=0, tiled=True)  30.7 us
    all_to_all x2, waiting for transfers between devices, exchange(): lax.all_to_all(message, RANKS, split_axis=0, concat_axis=0, tiled=True)  22.8 us
    pallas_call x7, Pallas kernels, run(): pl.pallas_call(kernel, out_shape=out_shape, in_specs=specs, out_specs=jax...  13.8 us
    unnamed x45, local copies, waits for them, and re-layouts  11.7 us
  transfers between devices with their start and end apart: 2, of which 2 were waited for; matrix products, arithmetic and copies ran while one was open for 0% of the time, Pallas kernels for 2%

profile of v1, /device:TPU:6, one launch (start us, length us, event | category | flops | bytes accessed | tf_op | source)
XLA Modules:
  0.0 141.8 jit_solution(1021660521268275306)
XLA Ops:
  0.6 0.0 copy-start.3
  0.6 0.0 copy-start.8
  0.7 0.7 copy-done.3
  1.4 0.0 copy-done.8
  1.4 0.0 copy-start.4
  1.4 0.7 copy-done.4
  2.1 0.0 copy-start.5
  2.1 0.7 copy-done.5
  2.8 0.0 copy-start.6
  2.8 0.7 copy-done.6
  3.5 0.0 copy-start.7
  3.5 0.7 copy-done.7
  4.2 0.0 copy-start.10
  4.2 0.1 shard_map.149
  4.3 0.8 copy.20
  5.0 0.0 copy-start.20
  5.0 21.5 %all-to-all-start = ((bf16[256,1,128]{2,1,0:T(2,128)(2,1)}), bf16[256,1,128]{2,1,0:T(2,128)(2,1)S(1)}, u32[]{:S(2)}, u32[]{:S(2)}) async-start(bf16[256,1,128]{2,1,0:T(2,128)(2,1)} %copy.20), calls=%async_computation | async-start | bytes 262144 | tf_op jit(solution)/shard_map/all_to_all | solution.py:252
  26.5 0.0 copy-done.20
  26.5 0.0 copy-start.21
  26.6 0.1 reshape.22.quad_ref
  26.7 0.5 copy-done.21
  27.2 0.1 reshape.23.order_ref
  27.4 0.0 copy-done.10
  27.4 0.0 copy-start.9
  27.4 1.2 copy-done.9
  28.6 0.0 copy-start
  28.6 0.0 copy-start.11
  28.6 2.0 %shard_map.150 = (f32[2,1024,128]{2,1,0:T(8,128)S(1)}, bf16[2,512,512]{2,1,0:T(8,128)(2,1)S(1)}, bf16[2,512,512]{2,1,0:T(8,128)(2,1)S(1)}, f32[512,128]{1,0:T(8,128)S(1)}) custom-call(bf16[2,1024,128]{2,1,0:T(8,128)(2,1)S(1)} %copy-done.10, bf16[2,512,512]{2,1,0:T(8,128)(2,1)S(1)} %copy-done.9, f32[256,2]{1,0:T(8,128)S(1)} %reshape.22.quad_ref), custom_call_target="tpu_custom_call" | custom-call | flops 1073741824 | bytes 4982784 | tf_op jit(solution)/shard_map/pallas_call | solution.py:35
  30.6 0.0 copy-start.14
  30.7 1.0 copy-done.14
  31.7 0.0 copy-start.16
  31.7 1.0 copy-done.16
  32.6 0.0 copy-start.18
  32.6 1.0 copy-done.18
  33.6 5.7 %all-to-all-done = bf16[256,1,128]{2,1,0:T(2,128)(2,1)S(1)} async-done(((bf16[256,1,128]{2,1,0:T(2,128)(2,1)}), bf16[256,1,128]{2,1,0:T(2,128)(2,1)S(1)}, u32[]{:S(2)}, u32[]{:S(2)}) %all-to-all-start) | async-done | bytes 65568 | tf_op jit(solution)/shard_map/all_to_all | solution.py:252
  39.3 0.0 copy-done
  39.3 0.0 copy-done.11
  39.3 0.0 copy-start.19
  39.3 1.2 copy-done.19
  40.6 0.0 copy-start.15
  40.6 0.0 copy-start.17
  40.6 5.9 %shard_map.151 = (bf16[256,8,128]{2,1,0:T(8,128)(2,1)S(1)}, f32[2,1024,128]{2,1,0:T(8,128)S(1)}) custom-call(bf16[256,128]{1,0:T(8,128)(2,1)S(1)} %bitcast.12, bf16[2,1024,128]{2,1,0:T(8,128)(2,1)S(1)} %copy-done.11, f32[2,1024,128]{2,1,0:T(8,128)S(1)} %copy-done.19, bf16[2,512,512]{2,1,0:T(8,128)(2,1)S(1)} %copy-done, s32[256,2]{1,0:T(8,128)S(1)} %reshape.23.order_ref), custom_call_target="tpu_custom_call" | custom-call | flops 4294967296 | bytes 4261888 | tf_op jit(solution)/shard_map/pallas_call | solution.py:35
  46.4 0.0 copy-start.12
  46.4 0.0 copy-start.13
  46.4 32.4 %all_to_all.20.got_ref = bf16[256,8,128]{2,1,0:T(8,128)(2,1)S(1)} all-to-all(bf16[256,8,128]{2,1,0:T(8,128)(2,1)S(1)} %get-tuple-element.11), channel_id=1, replica_groups=mesh['lat'=64,'chan'=2,'obs'=4] {'lat','obs'}, dimensions={0} | all-to-all | bytes 1048576 | tf_op jit(solution)/shard_map/all_to_all | solution.py:252
  78.9 0.0 copy-done.15
  78.9 0.0 copy-done.17
  78.9 0.0 copy-done.12
  78.9 0.0 copy-done.13
  78.9 1.4 shard_map.152
  80.3 28.5 %all_to_all.21.got_ref = bf16[256,8,128]{2,1,0:T(8,128)(2,1)S(1)} all-to-all(bf16[256,8,128]{2,1,0:T(8,128)(2,1)S(1)} %get-tuple-element.15), channel_id=1, replica_groups=mesh['lat'=64,'chan'=2,'obs'=4] {'lat','obs'}, dimensions={0} | all-to-all | bytes 1048576 | tf_op jit(solution)/shard_map/all_to_all | solution.py:252
  108.7 1.1 shard_map.153
  109.9 9.2 %all-to-all-start.3 = ((bf16[256,8,128]{2,1,0:T(8,128)(2,1)}), bf16[256,8,128]{2,1,0:T(8,128)(2,1)S(1)}, u32[]{:S(2)}, u32[]{:S(2)}) async-start(bf16[256,8,128]{2,1,0:T(8,128)(2,1)} %shard_map.153), calls=%async_computation.3 | async-start | bytes 1048576 | tf_op jit(solution)/shard_map/all_to_all | solution.py:252
  119.1 0.1 copy.21
  119.2 1.2 shard_map.154.grad_ref
  120.4 0.0 copy-start.1
  120.4 1.0 copy-done.1
  121.4 17.1 %all-to-all-done.3.got_ref = bf16[256,8,128]{2,1,0:T(8,128)(2,1)S(1)} async-done(((bf16[256,8,128]{2,1,0:T(8,128)(2,1)}), bf16[256,8,128]{2,1,0:T(8,128)(2,1)S(1)}, u32[]{:S(2)}, u32[]{:S(2)}) %all-to-all-start.3) | async-done | bytes 524320 | tf_op jit(solution)/shard_map/all_to_all | solution.py:252
  138.5 0.0 copy-start.2
  138.5 1.2 copy-done.2
  139.7 2.1 %shard_map.155 = (bf16[2,1024,128]{2,1,0:T(8,128)(2,1)}, f32[2,512,128]{2,1,0:T(8,128)}) custom-call(bf16[256,8,128]{2,1,0:T(8,128)(2,1)S(1)} %all-to-all-done.3.got_ref, s32[2,256]{1,0:T(2,128)S(1)} %bitcast.16, bf16[2,512,512]{2,1,0:T(8,128)(2,1)S(1)} %copy-done, f32[2,1024,128]{2,1,0:T(8,128)S(1)} %copy-done.2), custom_call_target="tpu_custom_call" | custom-call | flops 805306368 | bytes 3672064 | tf_op jit(solution)/shard_map/pallas_call | solution.py:35
  (1 shorter events, 0.0 us)
Async XLA Ops:
  0.6 0.7 copy-start.3
  0.6 0.7 copy-start.8
  1.4 0.7 copy-start.4
  2.1 0.7 copy-start.5
  2.8 0.7 copy-start.6
  3.5 0.7 copy-start.7
  4.2 23.2 %copy-start.10 = (bf16[2,1024,128]{2,1,0:T(8,128)(2,1)S(1)}, bf16[2,1024,128]{2,1,0:T(8,128)(2,1)}, u32[]{:S(2)}) copy-start(bf16[2,1024,128]{2,1,0:T(8,128)(2,1)} %pre_ref.1) | copy-start | bytes 1572868
  5.0 21.5 %copy-start.20 = (f32[512]{0:T(512)S(1)}, f32[512]{0:T(512)}, u32[]{:S(2)}) copy-start(f32[512]{0:T(512)} %param.18) | copy-start | bytes 6148
  5.0 34.3 %all-to-all-start = ((bf16[256,1,128]{2,1,0:T(2,128)(2,1)}), bf16[256,1,128]{2,1,0:T(2,128)(2,1)S(1)}, u32[]{:S(2)}, u32[]{:S(2)}) async-start(bf16[256,1,128]{2,1,0:T(2,128)(2,1)} %copy.20), calls=%async_computation | async-start | bytes 262144 | tf_op jit(solution)/shard_map/all_to_all | solution.py:252
  26.5 0.7 copy-start.21
  27.4 1.2 copy-start.9
  28.6 10.7 %copy-start = (bf16[2,512,512]{2,1,0:T(8,128)(2,1)S(1)}, bf16[2,512,512]{2,1,0:T(8,128)(2,1)}, u32[]{:S(2)}) copy-start(bf16[2,512,512]{2,1,0:T(8,128)(2,1)} %constant.10.clone.table_ref) | copy-start | bytes 3145732
  28.6 10.7 %copy-start.11 = (bf16[2,1024,128]{2,1,0:T(8,128)(2,1)S(1)}, bf16[2,1024,128]{2,1,0:T(8,128)(2,1)}, u32[]{:S(2)}) copy-start(bf16[2,1024,128]{2,1,0:T(8,128)(2,1)} %next_ref.1) | copy-start | bytes 1572868
  30.6 1.0 copy-start.14
  31.7 1.0 copy-start.16
  32.6 1.0 copy-start.18
  39.3 1.2 copy-start.19
  40.6 38.3 %copy-start.15 = (bf16[2,512,512]{2,1,0:T(8,128)(2,1)S(1)}, bf16[2,512,512]{2,1,0:T(8,128)(2,1)}, u32[]{:S(2)}) copy-start(bf16[2,512,512]{2,1,0:T(8,128)(2,1)} %copy-done.14) | copy-start | bytes 3145732
  40.6 38.3 %copy-start.17 = (bf16[2,512,512]{2,1,0:T(8,128)(2,1)S(1)}, bf16[2,512,512]{2,1,0:T(8,128)(2,1)}, u32[]{:S(2)}) copy-start(bf16[2,512,512]{2,1,0:T(8,128)(2,1)} %copy-done.16) | copy-start | bytes 3145732
  46.4 32.5 %copy-start.12 = (bf16[2,2,512,128]{3,2,1,0:T(8,128)(2,1)S(1)}, bf16[2,2,512,128]{3,2,1,0:T(8,128)(2,1)}, u32[]{:S(2)}) copy-start(bf16[2,2,512,128]{3,2,1,0:T(8,128)(2,1)} %saved_ref.1) | copy-start | bytes 1572868
  46.4 32.4 %copy-start.13 = (f32[2,512,128]{2,1,0:T(8,128)S(1)}, f32[2,512,128]{2,1,0:T(8,128)}, u32[]{:S(2)}) copy-start(f32[2,512,128]{2,1,0:T(8,128)} %gain_ref.1) | copy-start | bytes 1572868
  109.9 28.6 %all-to-all-start.3 = ((bf16[256,8,128]{2,1,0:T(8,128)(2,1)}), bf16[256,8,128]{2,1,0:T(8,128)(2,1)S(1)}, u32[]{:S(2)}, u32[]{:S(2)}) async-start(bf16[256,8,128]{2,1,0:T(8,128)(2,1)} %shard_map.153), calls=%async_computation.3 | async-start | bytes 1048576 | tf_op jit(solution)/shard_map/all_to_all | solution.py:252
  120.4 1.0 copy-start.1
  138.5 1.2 copy-start.2

commit v2 on v1

v2 whole, which is shorter than its diff:
```python
import math

import jax
import jax.numpy as jnp
import numpy as np
from jax import lax
from jax.experimental import pallas as pl
from jax.experimental.pallas import tpu as pltpu
from jax.sharding import PartitionSpec as P

BF = jnp.bfloat16
F32 = jnp.float32
NT = (((1,), (1,)), ((), ()))
RANKS = ("lat", "obs")


def dot(left, right):
    return jnp.dot(left, right, preferred_element_type=F32)


def dot_nt(left, right):
    return lax.dot_general(left, right, NT, preferred_element_type=F32)


def call(kernel, out_shape, scratch=(), smem=0, far=False, far_out=False, flops=0, limit=16):
    outs = out_shape if isinstance(out_shape, tuple) else (out_shape,)
    moved = sum(math.prod(o.shape) * o.dtype.itemsize for o in outs)

    def run(*args):
        rest = pltpu.HBM if far else pltpu.VMEM
        specs = [
            pl.BlockSpec(memory_space=pltpu.SMEM if i < smem else rest) for i in range(len(args))
        ]
        total = moved + sum(math.prod(a.shape) * a.dtype.itemsize for a in args)
        return pl.pallas_call(
            kernel,
            out_shape=out_shape,
            in_specs=specs,
            out_specs=jax.tree.map(
                lambda _: pl.BlockSpec(memory_space=pltpu.HBM if far_out else pltpu.VMEM), out_shape
            ),
            scratch_shapes=list(scratch),
            compiler_params=pltpu.CompilerParams(vmem_limit_bytes=limit << 20),
            cost_estimate=pl.CostEstimate(flops=flops, bytes_accessed=total, transcendentals=0),
        )(*args)

    return run


def iota(shape, axis):
    return lax.broadcasted_iota(jnp.int32, shape, axis)


def pack_kernel(base_ref, *refs):
    sources, out_ref, buffers, sems = refs[:6], refs[6], refs[7:13], refs[13]
    copies = [
        pltpu.make_async_copy(source, buffer, sems.at[i])
        for i, (source, buffer) in enumerate(zip(sources, buffers))
    ]
    for copy in copies:
        copy.start()
    for copy in copies:
        copy.wait()
    value, lat_frac, lon_frac, corner, chan, counts = [buffer[...] for buffer in buffers]
    capacity, tiles = value.shape
    alive = iota((capacity, tiles), 0) < counts
    fields = [
        jnp.where(alive, value.astype(F32), 0.0),
        lat_frac.astype(F32),
        lon_frac.astype(F32),
        corner.astype(F32),
        (chan - base_ref[0]).astype(F32),
        jnp.zeros((128 - 5 * capacity, tiles), F32),
    ]
    out_ref[...] = jnp.concatenate(fields, axis=0).T


def ready_kernel(
    pre_ref, legendre_ref, quad_ref, order_ref, slope_ref, up_ref, down_ref, weight_ref, cols_ref, rows_ref
):
    values = pre_ref[...].astype(F32)
    cdf = 0.5 * (1.0 + lax.erf(values * 0.7071067811865476))
    density = jnp.exp(-0.5 * values * values) * 0.3989422804014327
    slope_ref[...] = cdf + values * density
    lats = legendre_ref.shape[2]
    half = lats // 2
    place = iota((lats, lats), 0)
    chosen = (place % half) * 2 + place // half == iota((lats, lats), 1)
    pick = chosen.astype(BF)
    for s in range(legendre_ref.shape[0]):
        table = legendre_ref[s]
        up_ref[s] = dot_nt(table, pick).astype(BF)
        down_ref[s] = dot_nt(pick, table).astype(BF)
    quad = jnp.sum(jnp.where(chosen, quad_ref[...], 0.0), axis=1, keepdims=True)
    weight_ref[...] = jnp.broadcast_to(quad, weight_ref.shape)
    order = jnp.where(chosen, order_ref[...].astype(F32), 0.0)
    order = jnp.sum(order, axis=1, keepdims=True).astype(jnp.int32)
    order = jnp.broadcast_to(order, cols_ref.shape)
    cols_ref[...] = order
    rows_ref[...] = order.T[:8]


def tall(row, count):
    block = jnp.broadcast_to(row, (16, row.shape[1])).astype(BF)
    return jnp.concatenate([block] * (count // 16), axis=0)


def synth_kernel(
    slots_ref, next_ref, slope_ref, table_ref, order_ref, sent_ref, grad_ref, rows_ref, cols_ref, field_ref, msg_ref
):
    lat_dev, lons, width = next_ref.shape
    ranks = slots_ref.shape[0]
    capacity = 16
    groups = lons // 4
    fields = slots_ref[...].T
    value = fields[0:16]
    lat_step = fields[16:32]
    lon_step = fields[32:48]
    corner = fields[48:64].astype(jnp.int32)
    chan = fields[64:80]
    group = (corner // 4).astype(F32)
    place = corner % 4
    at_left = ((1.0 - lat_step) * (1.0 - lon_step), lat_step * (1.0 - lon_step))
    at_right = ((1.0 - lat_step) * lon_step, lat_step * lon_step)
    weights = [
        jnp.where(place == j, at_left[k], 0.0) + jnp.where(place == j - 1, at_right[k], 0.0)
        for j in range(5)
        for k in range(lat_dev)
    ]
    chan_ids = iota((width, ranks), 0).astype(F32).astype(BF)
    group_ids = iota((groups, ranks), 0).astype(F32).astype(BF)
    nothing = jnp.zeros((), BF)
    for p in range(capacity):
        span = slice(p * ranks, (p + 1) * ranks)
        rows_ref[:, span] = jnp.where(
            group_ids == tall(group[p : p + 1], groups), tall(value[p : p + 1], groups), nothing
        )
        hit = chan_ids == tall(chan[p : p + 1], width)
        for i, weight in enumerate(weights):
            cols_ref[i * width : (i + 1) * width, span] = jnp.where(
                hit, tall(weight[p : p + 1], width), nothing
            )
    pair = lat_dev * width
    found = [
        dot_nt(rows_ref[...], cols_ref[j * pair : (j + 1) * pair, :]) for j in range(5)
    ]
    found[0] = found[0] + pltpu.roll(found[4], 1, 0)
    for j in range(4):
        for k in range(lat_dev):
            field_ref[k, pl.ds(j, groups, stride=4), :] = found[j][:, k * width : (k + 1) * width]
    halves = []
    for h in range(2):
        at = h * (lons // 2)
        parts = []
        for k in range(lat_dev):
            total = next_ref[k, at : at + lons // 2, :].astype(F32) + field_ref[
                k, at : at + lons // 2, :
            ]
            grad_ref[k, at : at + lons // 2, :] = total
            parts.append((total * slope_ref[k, at : at + lons // 2, :]).astype(BF))
        halves.extend(parts)
    field = jnp.concatenate(halves, axis=1)
    orders = table_ref.shape[1]
    order_ids = iota((orders, 1), 0)
    sign = jnp.where(order_ids % 2 == 0, 1.0, -1.0)
    scale = jnp.where(order_ids == 0, 1.0, 2.0)
    for r in range(2):
        both = dot(table_ref[r], field)
        total = (both[:, :pair] + sign * both[:, pair:]) * (scale if r == 0 else -scale)
        total = total.astype(BF)
        for s in range(2):
            chosen = (iota((ranks, orders), 1) == order_ref[s * ranks : (s + 1) * ranks, 0:1]).astype(BF)
            placed = dot(chosen, total)
            for k in range(lat_dev):
                row = s * 4 + r * 2 + k
                msg_ref[pl.ds(row, ranks, stride=8), :] = placed[:, k * width : (k + 1) * width]
    sent_ref[...] = msg_ref[...].reshape(ranks, 8, width).astype(BF)


def legendre_kernel(
    got_ref, up_ref, down_ref, weight_ref, saved_ref, gain_ref, first_ref, second_ref, msg_ref, out_ref
):
    ranks, rows, width = got_ref.shape
    msg_ref[...] = got_ref[...].astype(F32).reshape(ranks * rows, width)
    gain_real = gain_ref[0]
    gain_imag = gain_ref[1]
    terms = [None, None]
    for s in range(2):
        parts = []
        for r in range(2):
            lanes = [
                msg_ref[pl.ds(s * 4 + r * 2 + k, ranks, stride=8), :].astype(BF) for k in range(2)
            ]
            parts.append(jnp.concatenate(lanes, axis=0))
        found = dot(up_ref[s], jnp.concatenate(parts, axis=1))
        real = found[:, :width]
        imag = found[:, width:]
        saved_real = saved_ref[s, 0].astype(F32)
        saved_imag = saved_ref[s, 1].astype(F32)
        new = (real * saved_real + imag * saved_imag, imag * saved_real - real * saved_imag)
        terms = [n if t is None else t + n for t, n in zip(terms, new)]
        coeff = jnp.concatenate(
            [gain_real * real + gain_imag * imag, gain_real * imag - gain_imag * real], axis=1
        ).astype(BF)
        lat_grad = dot(down_ref[s], coeff)
        for r in range(2):
            weighted = lat_grad[:, r * width : (r + 1) * width] * weight_ref[...]
            for k in range(2):
                out_ref[s, pl.ds(r * 2 + k, ranks, stride=8), :] = weighted[
                    k * ranks : (k + 1) * ranks
                ]
    for g in range(2):
        for h in range(2):
            part = terms[g][h * ranks : (h + 1) * ranks]
            for s in range(2):
                out_ref[s, pl.ds(4 + g * 2 + h, ranks, stride=8), :] = part
    first_ref[...] = out_ref[0].reshape(ranks, rows, width).astype(BF)
    second_ref[...] = out_ref[1].reshape(ranks, rows, width).astype(BF)


def share_kernel(got_ref, half_ref, sent_ref):
    ranks, rows, width = got_ref.shape
    part = ranks // 16
    total = got_ref[0:part].astype(F32)
    for i in range(1, 16):
        total = total + got_ref[i * part : (i + 1) * part].astype(F32)
    total = jnp.sum(total, axis=0, keepdims=True).astype(BF)
    sent_ref[...] = jnp.where(iota(got_ref.shape, 1) < 4, half_ref[...], total)


def natural(msg_ref, order_ref, orders, s):
    ranks = msg_ref.shape[0] // 8
    sign = jnp.where(iota((orders, 1), 0) % 2 == 0, 1.0, -1.0)
    chosen = (iota((orders, ranks), 0) == order_ref[0:1, s * ranks : (s + 1) * ranks]).astype(BF)
    both = []
    for r in range(2):
        lanes = [msg_ref[pl.ds(r * 2 + k, ranks, stride=8), :].astype(BF) for k in range(2)]
        placed = dot(chosen, jnp.concatenate(lanes, axis=1))
        both.append(jnp.concatenate([placed, placed * sign], axis=1).astype(BF))
    return both


def first_kernel(got_ref, order_ref, table_ref, grad_ref, out_ref, msg_ref):
    lat_dev, lons, width = grad_ref.shape
    half = lons // 2
    msg_ref[...] = got_ref[...].astype(F32).reshape(msg_ref.shape)
    both = natural(msg_ref, order_ref, half, 0)
    part = (dot(table_ref[0], both[0]) - dot(table_ref[1], both[1])) * (1.0 / lons)
    for h in range(2):
        span = slice(h * half, (h + 1) * half)
        for k in range(lat_dev):
            at = (h * lat_dev + k) * width
            out_ref[k, span, :] = grad_ref[k, span, :] + part[:, at : at + width]


def second_kernel(got_ref, order_ref, table_ref, grad_ref, out_ref, gain_ref, msg_ref, field_ref, share_ref, sems):
    lat_dev, lons, width = grad_ref.shape
    ranks = got_ref.shape[0]
    half = lons // 2
    msg_ref[...] = got_ref[...].astype(F32).reshape(msg_ref.shape)
    for g in range(2):
        for h in range(2):
            share_ref[g, h * ranks : (h + 1) * ranks, :] = msg_ref[
                pl.ds(4 + g * 2 + h, ranks, stride=8), :
            ]
    copies = [pltpu.make_async_copy(share_ref, gain_ref, sems.at[0])]
    copies[0].start()
    both = natural(msg_ref, order_ref, half, 1)
    block = half // 4
    for i in range(4):
        rows = slice(i * block, (i + 1) * block)
        part = dot(table_ref[0, rows, :], both[0]) - dot(table_ref[1, rows, :], both[1])
        part = part * (1.0 / lons)
        for h in range(2):
            span = slice(h * half + i * block, h * half + (i + 1) * block)
            for k in range(lat_dev):
                at = (h * lat_dev + k) * width
                field_ref[k, span, :] = (grad_ref[k, span, :] + part[:, at : at + width]).astype(BF)
            copies.append(
                pltpu.make_async_copy(
                    field_ref.at[:, span, :], out_ref.at[:, span, :], sems.at[len(copies)]
                )
            )
            copies[-1].start()
    for copy in copies:
        copy.wait()


def exchange(message):
    return lax.all_to_all(message, RANKS, split_axis=0, concat_axis=0, tiled=True)


def on_device(
    next_grad,
    pre_act,
    legendre,
    order_slots,
    quad_weights,
    spectral_gain,
    saved_coeffs,
    obs_value,
    obs_lat_frac,
    obs_lon_frac,
    obs_corner,
    obs_channel,
    slot_counts,
):
    lat_dev, lons, width = next_grad.shape
    slot_dev, degrees, lats = legendre.shape
    orders = order_slots.shape[0]
    ranks = lax.axis_size("lat") * lax.axis_size("obs")
    shape = jax.ShapeDtypeStruct

    index = np.arange(orders)
    angle = ((index[:, None] * index[None, :]) % lons).astype(np.float32) * np.float32(
        2.0 * math.pi / lons
    )
    table = jnp.asarray(np.stack([np.cos(angle), np.sin(angle)]).astype(jnp.bfloat16))

    base = (lax.axis_index("chan") * width).astype(jnp.int32).reshape(1)
    slot_args = (
        obs_value[0],
        obs_lat_frac[0],
        obs_lon_frac[0],
        obs_corner[0],
        obs_channel[0],
        slot_counts,
    )
    slots = exchange(
        call(
            pack_kernel,
            shape((ranks, 128), F32),
            scratch=[pltpu.VMEM(a.shape, a.dtype) for a in slot_args]
            + [pltpu.SemaphoreType.DMA((len(slot_args),))],
            smem=1,
            far=True,
            limit=60,
        )(base, *slot_args)
    )

    slope, up_table, down_table, weight, order_columns, order_rows = call(
        ready_kernel,
        (
            shape(next_grad.shape, F32),
            shape(legendre.shape, BF),
            shape((slot_dev, lats, degrees), BF),
            shape((lats, 128), F32),
            shape((orders, 128), jnp.int32),
            shape((8, orders), jnp.int32),
        ),
        flops=4 * 2 * 512**3,
    )(pre_act, legendre, quad_weights.reshape(1, lats), order_slots.reshape(1, orders))

    message = shape((ranks, 8, width), BF)
    rows = pltpu.VMEM((ranks * 8, width), F32)
    sent, out_grad = call(
        synth_kernel,
        (message, shape(next_grad.shape, F32)),
        scratch=[
            pltpu.VMEM((lons // 4, 16 * ranks), BF),
            pltpu.VMEM((10 * width, 16 * ranks), BF),
            pltpu.VMEM((lat_dev, lons, width), F32),
            rows,
        ],
        flops=2 * 1024 * 4096 * 512,
        limit=32,
    )(slots, next_grad, slope, table, order_columns)
    by_order = exchange(sent)
    first, second = call(legendre_kernel, (message, message), scratch=[rows, pltpu.VMEM((2, ranks * 8, width), F32)], flops=2 * 512**3 * 4)(
        by_order, up_table, down_table, weight, saved_coeffs, spectral_gain
    )
    first = exchange(first)
    second = exchange(call(share_kernel, message)(first, second))
    partial = call(first_kernel, shape(next_grad.shape, F32), scratch=[rows], flops=2 * 512**3 * 3)(
        first, order_rows, table, out_grad
    )
    outs = (shape(next_grad.shape, BF), shape((2, degrees, width), F32))
    return call(
        second_kernel,
        outs,
        scratch=[rows]
        + [pltpu.VMEM(o.shape, o.dtype) for o in outs]
        + [pltpu.SemaphoreType.DMA((9,))],
        far_out=True,
        flops=2 * 512**3 * 3,
    )(second, order_rows, table, partial)


def solution(mesh):
    ranks = P(RANKS, None, None)
    in_specs = (
        P(RANKS, None, "chan"),
        P(RANKS, None, "chan"),
        ranks,
        P(),
        P(),
        P(None, None, "chan"),
        P(RANKS, None, None, "chan"),
        ranks,
        ranks,
        ranks,
        ranks,
        ranks,
        P(RANKS, None),
    )
    out_specs = (P(RANKS, None, "chan"), P(None, None, "chan"))
    return jax.shard_map(
        on_device, mesh=mesh, in_specs=in_specs, out_specs=out_specs, check_vma=False
    )
```

time: 143 us -> 140 us (0.979)
  local copies, waits for them, and re-layouts: 12.8 us -> 9.35 us
    unnamed x45 -> x32, local copies, waits for them, and re-layouts: 11.7 us -> 9.35 us
where the time goes in v2:
time: 140 us; the launch traced here: 139 us
  blocking collectives  61.7 us (44%)
  starting transfers between devices  30.6 us (22%)
  waiting for transfers between devices  22.2 us (16%)
  Pallas kernels  14 us (10%)
  local copies, waits for them, and re-layouts  9.35 us (7%)
    all_to_all x2, blocking collectives, exchange(): lax.all_to_all(message, RANKS, split_axis=0, concat_axis=0, tiled=True)  61.7 us
    all_to_all x2, starting transfers between devices, exchange(): lax.all_to_all(message, RANKS, split_axis=0, concat_axis=0, tiled=True)  30.6 us
    all_to_all x2, waiting for transfers between devices, exchange(): lax.all_to_all(message, RANKS, split_axis=0, concat_axis=0, tiled=True)  22.2 us
    pallas_call x7, Pallas kernels, run(): pl.pallas_call(kernel, out_shape=out_shape, in_specs=specs, out_specs=jax...  14 us
    unnamed x32, local copies, waits for them, and re-layouts  9.35 us
  transfers between devices with their start and end apart: 2, of which 2 were waited for; matrix products, arithmetic and copies ran while one was open for 0% of the time, Pallas kernels for 2%

profile of v2, /device:TPU:6, one launch (start us, length us, event | category | flops | bytes accessed | tf_op | source)
XLA Modules:
  0.0 138.7 jit_solution(7542242348324277787)
XLA Ops:
  0.6 1.6 %shard_map.149 = f32[256,128]{1,0:T(8,128)} custom-call(s32[1]{0:T(128)} %bitcast.base_ref, bf16[16,256]{1,0:T(8,128)(2,1)} %bitcast.18, bf16[16,256]{1,0:T(8,128)(2,1)} %bitcast.19, bf16[16,256]{1,0:T(8,128)(2,1)} %bitcast.20, s32[16,256]{1,0:T(8,128)} %bitcast.16, s32[16,256]{1,0:T(8,128)} %bitcast.17, s32[1,256]{1,0:T(1,128)} %refs_5_.1), custom_call_target="tpu_custom_call" | custom-call | bytes 189444 | tf_op jit(solution)/shard_map/pallas_call | solution.py:35
  2.2 0.0 copy-start.9
  2.3 21.4 %all-to-all-start = ((f32[256,1,128]{2,1,0:T(1,128)}), f32[256,1,128]{2,1,0:T(1,128)S(1)}, u32[]{:S(2)}, u32[]{:S(2)}) async-start(f32[256,1,128]{2,1,0:T(1,128)} %bitcast.15), calls=%async_computation | async-start | bytes 262144 | tf_op jit(solution)/shard_map/all_to_all | solution.py:290
  23.6 0.0 copy-start.8
  23.6 0.0 copy-done.9
  23.7 0.7 copy-done.8
  24.3 0.0 copy-start.3
  24.3 1.2 copy-done.3
  25.5 0.0 copy-start.4
  25.5 1.0 copy-done.4
  26.6 0.0 copy-start
  26.6 0.0 copy-start.5
  26.6 2.1 %shard_map.150 = (f32[2,1024,128]{2,1,0:T(8,128)S(1)}, bf16[2,512,512]{2,1,0:T(8,128)(2,1)S(1)}, bf16[2,512,512]{2,1,0:T(8,128)(2,1)S(1)}, f32[512,128]{1,0:T(8,...) custom-call(bf16[2,1024,128]{2,1,0:T(8,128)(2,1)S(1)} %copy-done.4, bf16[2,512,512]{2,1,0:T(8,128)(2,1)S(1)} %copy-done.3, ...), custom_call_target="tpu_custom_call" | custom-call | flops 1073741824 | bytes 5263360 | tf_op jit(solution)/shard_map/pallas_call | solution.py:35
  28.7 0.0 copy-start.10
  28.7 1.0 copy-done.10
  29.7 0.0 copy-start.12
  29.7 1.0 copy-done.12
  30.7 0.0 copy-start.14
  30.7 1.0 copy-done.14
  31.7 4.7 %all-to-all-done = f32[256,1,128]{2,1,0:T(1,128)S(1)} async-done(((f32[256,1,128]{2,1,0:T(1,128)}), f32[256,1,128]{2,1,0:T(1,128)S(1)}, u32[]{:S(2)}, u32[]{:S(2)}) %all-to-all-start) | async-done | bytes 131104 | tf_op jit(solution)/shard_map/all_to_all | solution.py:290
  36.4 0.0 copy-done
  36.4 0.0 copy-done.5
  36.4 0.0 copy-start.15
  36.4 1.2 copy-done.15
  37.6 0.0 copy-start.11
  37.6 0.0 copy-start.13
  37.6 5.2 %shard_map.151 = (bf16[256,8,128]{2,1,0:T(8,128)(2,1)S(1)}, f32[2,1024,128]{2,1,0:T(8,128)S(1)}) custom-call(f32[256,128]{1,0:T(8,128)S(1)} %bitcast.12, bf16[2,1024,128]{2,1,0:T(8,128)(2,1)S(1)} %copy-done.5, f32[2,1024,128]{2,1,0:T(8,128)S(1)} %copy-done.15, bf16[2,512,512]{2,1,0:T(8,128)(2,1)S(1)} %copy-done, s32[512,128]{1,0:T(8,128)S(1)} %get-tuple-element.13.order_ref), custom_call_target="tpu_custom_call" | custom-call | flops 4294967296 | bytes 4587520 | tf_op jit(solution)/shard_map/pallas_call | solution.py:35
  42.9 0.0 copy-start.6
  42.9 0.0 copy-start.7
  42.9 33.2 %all_to_all.26.got_ref = bf16[256,8,128]{2,1,0:T(8,128)(2,1)S(1)} all-to-all(bf16[256,8,128]{2,1,0:T(8,128)(2,1)S(1)} %get-tuple-element.14), channel_id=1, replica_groups=mesh['lat'=64,'chan'=2,'obs'=4] {'lat','obs'}, dimensions={0} | all-to-all | bytes 1048576 | tf_op jit(solution)/shard_map/all_to_all | solution.py:290
  76.1 0.0 copy-done.11
  76.1 0.0 copy-done.13
  76.1 0.0 copy-done.6
  76.1 0.0 copy-done.7
  76.1 1.3 shard_map.152
  77.4 28.5 %all_to_all.27.got_ref = bf16[256,8,128]{2,1,0:T(8,128)(2,1)S(1)} all-to-all(bf16[256,8,128]{2,1,0:T(8,128)(2,1)S(1)} %get-tuple-element.18), channel_id=1, replica_groups=mesh['lat'=64,'chan'=2,'obs'=4] {'lat','obs'}, dimensions={0} | all-to-all | bytes 1048576 | tf_op jit(solution)/shard_map/all_to_all | solution.py:290
  105.9 1.0 shard_map.153
  106.8 9.2 %all-to-all-start.3 = ((bf16[256,8,128]{2,1,0:T(8,128)(2,1)}), bf16[256,8,128]{2,1,0:T(8,128)(2,1)S(1)}, u32[]{:S(2)}, u32[]{:S(2)}) async-start(bf16[256,8,128]{2,1,0:T(8,128)(2,1)} %shard_map.153), calls=%async_computation.3 | async-start | bytes 1048576 | tf_op jit(solution)/shard_map/all_to_all | solution.py:290
  116.1 1.0 shard_map.154.grad_ref
  117.0 0.0 copy-start.1
  117.1 1.0 copy-done.1
  118.0 17.4 %all-to-all-done.3.got_ref = bf16[256,8,128]{2,1,0:T(8,128)(2,1)S(1)} async-done(((bf16[256,8,128]{2,1,0:T(8,128)(2,1)}), bf16[256,8,128]{2,1,0:T(8,128)(2,1)S(1)}, u32[]{:S(2)}, u32[]{:S(2)}) %all-to-all-start.3) | async-done | bytes 524320 | tf_op jit(solution)/shard_map/all_to_all | solution.py:290
  135.5 0.0 copy-start.2
  135.5 1.2 copy-done.2
  136.7 1.8 %shard_map.155 = (bf16[2,1024,128]{2,1,0:T(8,128)(2,1)}, f32[2,512,128]{2,1,0:T(8,128)}) custom-call(bf16[256,8,128]{2,1,0:T(8,128)(2,1)S(1)} %all-to-all-done.3.got_ref, s32[8,512]{1,0:T(8,128)S(1)} %get-tuple-element.20.order_ref, bf16[2,512,512]{2,1,0:T(8,128)(2,1)S(1)} %copy-done, f32[2,1024,128]{2,1,0:T(8,128)S(1)} %copy-done.2), custom_call_target="tpu_custom_call" | custom-call | flops 805306368 | bytes 3686400 | tf_op jit(solution)/shard_map/pallas_call | solution.py:35
Async XLA Ops:
  2.2 21.4 %copy-start.9 = (s32[512]{0:T(512)S(1)}, s32[512]{0:T(512)}, u32[]{:S(2)}) copy-start(s32[512]{0:T(512)} %param.17) | copy-start | bytes 6148
  2.3 34.1 %all-to-all-start = ((f32[256,1,128]{2,1,0:T(1,128)}), f32[256,1,128]{2,1,0:T(1,128)S(1)}, u32[]{:S(2)}, u32[]{:S(2)}) async-start(f32[256,1,128]{2,1,0:T(1,128)} %bitcast.15), calls=%async_computation | async-start | bytes 262144 | tf_op jit(solution)/shard_map/all_to_all | solution.py:290
  23.6 0.7 copy-start.8
  24.3 1.2 copy-start.3
  25.5 1.0 copy-start.4
  26.6 9.8 %copy-start = (bf16[2,512,512]{2,1,0:T(8,128)(2,1)S(1)}, bf16[2,512,512]{2,1,0:T(8,128)(2,1)}, u32[]{:S(2)}) copy-start(bf16[2,512,512]{2,1,0:T(8,128)(2,1)} %constant.10.clone.table_ref) | copy-start | bytes 3145732
  26.6 9.8 %copy-start.5 = (bf16[2,1024,128]{2,1,0:T(8,128)(2,1)S(1)}, bf16[2,1024,128]{2,1,0:T(8,128)(2,1)}, u32[]{:S(2)}) copy-start(bf16[2,1024,128]{2,1,0:T(8,128)(2,1)} %next_ref.1) | copy-start | bytes 1572868
  28.7 1.0 copy-start.10
  29.7 1.0 copy-start.12
  30.7 1.0 copy-start.14
  36.4 1.2 copy-start.15
  37.6 38.5 %copy-start.11 = (bf16[2,512,512]{2,1,0:T(8,128)(2,1)S(1)}, bf16[2,512,512]{2,1,0:T(8,128)(2,1)}, u32[]{:S(2)}) copy-start(bf16[2,512,512]{2,1,0:T(8,128)(2,1)} %copy-done.10) | copy-start | bytes 3145732
  37.6 38.5 %copy-start.13 = (bf16[2,512,512]{2,1,0:T(8,128)(2,1)S(1)}, bf16[2,512,512]{2,1,0:T(8,128)(2,1)}, u32[]{:S(2)}) copy-start(bf16[2,512,512]{2,1,0:T(8,128)(2,1)} %copy-done.12) | copy-start | bytes 3145732
  42.9 33.2 %copy-start.6 = (bf16[2,2,512,128]{3,2,1,0:T(8,128)(2,1)S(1)}, bf16[2,2,512,128]{3,2,1,0:T(8,128)(2,1)}, u32[]{:S(2)}) copy-start(bf16[2,2,512,128]{3,2,1,0:T(8,128)(2,1)} %saved_ref.1) | copy-start | bytes 1572868
  42.9 33.2 %copy-start.7 = (f32[2,512,128]{2,1,0:T(8,128)S(1)}, f32[2,512,128]{2,1,0:T(8,128)}, u32[]{:S(2)}) copy-start(f32[2,512,128]{2,1,0:T(8,128)} %gain_ref.1) | copy-start | bytes 1572868
  106.8 28.6 %all-to-all-start.3 = ((bf16[256,8,128]{2,1,0:T(8,128)(2,1)}), bf16[256,8,128]{2,1,0:T(8,128)(2,1)S(1)}, u32[]{:S(2)}, u32[]{:S(2)}) async-start(bf16[256,8,128]{2,1,0:T(8,128)(2,1)} %shard_map.153), calls=%async_computation.3 | async-start | bytes 1048576 | tf_op jit(solution)/shard_map/all_to_all | solution.py:290
  117.0 1.0 copy-start.1
  135.5 1.2 copy-start.2

commit v3 on v2

--- a/solution.py
+++ b/solution.py
@@ -22,14 +22,16 @@
     return lax.dot_general(left, right, NT, preferred_element_type=F32)
 
 
-def call(kernel, out_shape, scratch=(), smem=0, far=False, far_out=False, flops=0, limit=16):
+def call(kernel, out_shape, scratch=(), smem=0, far=(), far_out=False, flops=0, limit=16):
     outs = out_shape if isinstance(out_shape, tuple) else (out_shape,)
     moved = sum(math.prod(o.shape) * o.dtype.itemsize for o in outs)
 
     def run(*args):
-        rest = pltpu.HBM if far else pltpu.VMEM
         specs = [
-            pl.BlockSpec(memory_space=pltpu.SMEM if i < smem else rest) for i in range(len(args))
+            pl.BlockSpec(
+                memory_space=pltpu.SMEM if i < smem else pltpu.HBM if i in far else pltpu.VMEM
+            )
+            for i in range(len(args))
         ]
         total = moved + sum(math.prod(a.shape) * a.dtype.itemsize for a in args)
         return pl.pallas_call(
@@ -47,19 +49,27 @@
     return run
 
 
-def iota(shape, axis):
-    return lax.broadcasted_iota(jnp.int32, shape, axis)
-
-
-def pack_kernel(base_ref, *refs):
-    sources, out_ref, buffers, sems = refs[:6], refs[6], refs[7:13], refs[13]
+def buffers_for(arrays):
+    return [pltpu.VMEM(a.shape, a.dtype) for a in arrays] + [pltpu.SemaphoreType.DMA((len(arrays),))]
+
+
+def start_copies(sources, targets, sems):
     copies = [
-        pltpu.make_async_copy(source, buffer, sems.at[i])
-        for i, (source, buffer) in enumerate(zip(sources, buffers))
+        pltpu.make_async_copy(source, target, sems.at[i])
+        for i, (source, target) in enumerate(zip(sources, targets))
     ]
     for copy in copies:
         copy.start()
-    for copy in copies:
+    return copies
+
+
+def iota(shape, axis):
+    return lax.broadcasted_iota(jnp.int32, shape, axis)
+
+
+def pack_kernel(base_ref, *refs):
+    sources, out_ref, buffers, sems = refs[:6], refs[6], refs[7:13], refs[13]
+    for copy in start_copies(sources, buffers, sems):
         copy.wait()
     value, lat_frac, lon_frac, corner, chan, counts = [buffer[...] for buffer in buffers]
     capacity, tiles = value.shape
@@ -75,39 +85,37 @@
     out_ref[...] = jnp.concatenate(fields, axis=0).T
 
 
-def ready_kernel(
-    pre_ref, legendre_ref, quad_ref, order_ref, slope_ref, up_ref, down_ref, weight_ref, cols_ref, rows_ref
+def ready_kernel(*refs):
+    sources, results = refs[:2], refs[2:5]
+    legendre_ref, quad_ref, in_sems, up_ref, down_ref, weight_ref, out_sems = refs[5:]
+    for copy in start_copies(sources, (legendre_ref, quad_ref), in_sems):
+        copy.wait()
+    lats = legendre_ref.shape[2]
+    half = lats // 2
+    place = iota((lats, lats), 0)
+    chosen = (place % half) * 2 + place // half == iota((lats, lats), 1)
+    quad = jnp.sum(jnp.where(chosen, quad_ref[...], 0.0), axis=1, keepdims=True)
+    weight_ref[...] = jnp.broadcast_to(quad, weight_ref.shape)
+    pick = chosen.astype(BF)
+    for s in range(legendre_ref.shape[0]):
+        up_ref[s] = dot_nt(legendre_ref[s], pick).astype(BF)
+        down_ref[s] = dot_nt(pick, legendre_ref[s]).astype(BF)
+    for copy in start_copies((up_ref, down_ref, weight_ref), results, out_sems):
+        copy.wait()
+
+
+def tall(row, count):
+    block = jnp.broadcast_to(row, (16, row.shape[1])).astype(BF)
+    return jnp.concatenate([block] * (count // 16), axis=0)
+
+
+def synth_kernel(
+    slots_ref, next_ref, pre_ref, table_ref, order_ref, sent_ref, grad_ref, slope_ref, rows_ref, cols_ref, field_ref, msg_ref
 ):
     values = pre_ref[...].astype(F32)
     cdf = 0.5 * (1.0 + lax.erf(values * 0.7071067811865476))
     density = jnp.exp(-0.5 * values * values) * 0.3989422804014327
     slope_ref[...] = cdf + values * density
-    lats = legendre_ref.shape[2]
-    half = lats // 2
-    place = iota((lats, lats), 0)
-    chosen = (place % half) * 2 + place // half == iota((lats, lats), 1)
-    pick = chosen.astype(BF)
-    for s in range(legendre_ref.shape[0]):
-        table = legendre_ref[s]
-        up_ref[s] = dot_nt(table, pick).astype(BF)
-        down_ref[s] = dot_nt(pick, table).astype(BF)
-    quad = jnp.sum(jnp.where(chosen, quad_ref[...], 0.0), axis=1, keepdims=True)
-    weight_ref[...] = jnp.broadcast_to(quad, weight_ref.shape)
-    order = jnp.where(chosen, order_ref[...].astype(F32), 0.0)
-    order = jnp.sum(order, axis=1, keepdims=True).astype(jnp.int32)
-    order = jnp.broadcast_to(order, cols_ref.shape)
-    cols_ref[...] = order
-    rows_ref[...] = order.T[:8]
-
-
-def tall(row, count):
-    block = jnp.broadcast_to(row, (16, row.shape[1])).astype(BF)
-    return jnp.concatenate([block] * (count // 16), axis=0)
-
-
-def synth_kernel(
-    slots_ref, next_ref, slope_ref, table_ref, order_ref, sent_ref, grad_ref, rows_ref, cols_ref, field_ref, msg_ref
-):
     lat_dev, lons, width = next_ref.shape
     ranks = slots_ref.shape[0]
     capacity = 16
@@ -169,7 +177,7 @@
         total = (both[:, :pair] + sign * both[:, pair:]) * (scale if r == 0 else -scale)
         total = total.astype(BF)
         for s in range(2):
-            chosen = (iota((ranks, orders), 1) == order_ref[s * ranks : (s + 1) * ranks, 0:1]).astype(BF)
+            chosen = (iota((ranks, orders), 1) == order_ref[:, s : s + 1]).astype(BF)
             placed = dot(chosen, total)
             for k in range(lat_dev):
                 row = s * 4 + r * 2 + k
@@ -228,44 +236,34 @@
     sent_ref[...] = jnp.where(iota(got_ref.shape, 1) < 4, half_ref[...], total)
 
 
-def natural(msg_ref, order_ref, orders, s):
-    ranks = msg_ref.shape[0] // 8
-    sign = jnp.where(iota((orders, 1), 0) % 2 == 0, 1.0, -1.0)
-    chosen = (iota((orders, ranks), 0) == order_ref[0:1, s * ranks : (s + 1) * ranks]).astype(BF)
-    both = []
-    for r in range(2):
-        lanes = [msg_ref[pl.ds(r * 2 + k, ranks, stride=8), :].astype(BF) for k in range(2)]
-        placed = dot(chosen, jnp.concatenate(lanes, axis=1))
-        both.append(jnp.concatenate([placed, placed * sign], axis=1).astype(BF))
-    return both
-
-
-def first_kernel(got_ref, order_ref, table_ref, grad_ref, out_ref, msg_ref):
+def field_kernel(
+    first_ref, second_ref, order_ref, table_ref, grad_ref, out_ref, gain_ref, msg_ref, field_ref, share_ref, sems
+):
     lat_dev, lons, width = grad_ref.shape
+    ranks = first_ref.shape[0]
     half = lons // 2
-    msg_ref[...] = got_ref[...].astype(F32).reshape(msg_ref.shape)
-    both = natural(msg_ref, order_ref, half, 0)
-    part = (dot(table_ref[0], both[0]) - dot(table_ref[1], both[1])) * (1.0 / lons)
-    for h in range(2):
-        span = slice(h * half, (h + 1) * half)
-        for k in range(lat_dev):
-            at = (h * lat_dev + k) * width
-            out_ref[k, span, :] = grad_ref[k, span, :] + part[:, at : at + width]
-
-
-def second_kernel(got_ref, order_ref, table_ref, grad_ref, out_ref, gain_ref, msg_ref, field_ref, share_ref, sems):
-    lat_dev, lons, width = grad_ref.shape
-    ranks = got_ref.shape[0]
-    half = lons // 2
-    msg_ref[...] = got_ref[...].astype(F32).reshape(msg_ref.shape)
+    msg_ref[1] = second_ref[...].astype(F32).reshape(msg_ref.shape[1:])
     for g in range(2):
         for h in range(2):
             share_ref[g, h * ranks : (h + 1) * ranks, :] = msg_ref[
-                pl.ds(4 + g * 2 + h, ranks, stride=8), :
+                1, pl.ds(4 + g * 2 + h, ranks, stride=8), :
             ]
     copies = [pltpu.make_async_copy(share_ref, gain_ref, sems.at[0])]
     copies[0].start()
-    both = natural(msg_ref, order_ref, half, 1)
+    msg_ref[0] = first_ref[...].astype(F32).reshape(msg_ref.shape[1:])
+    sign = jnp.where(iota((half, 1), 0) % 2 == 0, 1.0, -1.0)
+    chosen = [
+        (iota((half, ranks), 0) == order_ref[s : s + 1, :]).astype(BF) for s in range(2)
+    ]
+    chosen = jnp.concatenate(chosen, axis=1)
+    both = []
+    for r in range(2):
+        parts = []
+        for s in range(2):
+            lanes = [msg_ref[s, pl.ds(r * 2 + k, ranks, stride=8), :].astype(BF) for k in range(2)]
+            parts.append(jnp.concatenate(lanes, axis=1))
+        placed = dot(chosen, jnp.concatenate(parts, axis=0))
+        both.append(jnp.concatenate([placed, placed * sign], axis=1).astype(BF))
     block = half // 4
     for i in range(4):
         rows = slice(i * block, (i + 1) * block)
@@ -330,60 +328,67 @@
         call(
             pack_kernel,
             shape((ranks, 128), F32),
-            scratch=[pltpu.VMEM(a.shape, a.dtype) for a in slot_args]
-            + [pltpu.SemaphoreType.DMA((len(slot_args),))],
+            scratch=buffers_for(slot_args),
             smem=1,
-            far=True,
+            far=range(1, 7),
             limit=60,
         )(base, *slot_args)
     )
 
-    slope, up_table, down_table, weight, order_columns, order_rows = call(
+    ready_args = (legendre, quad_weights.reshape(1, lats))
+    ready = (
+        shape(legendre.shape, BF),
+        shape((slot_dev, lats, degrees), BF),
+        shape((lats, 128), F32),
+    )
+    prepared = call(
         ready_kernel,
-        (
-            shape(next_grad.shape, F32),
-            shape(legendre.shape, BF),
-            shape((slot_dev, lats, degrees), BF),
-            shape((lats, 128), F32),
-            shape((orders, 128), jnp.int32),
-            shape((8, orders), jnp.int32),
-        ),
+        ready,
+        scratch=buffers_for(ready_args) + buffers_for(ready),
+        far=range(2),
+        far_out=True,
         flops=4 * 2 * 512**3,
-    )(pre_act, legendre, quad_weights.reshape(1, lats), order_slots.reshape(1, orders))
+        limit=60,
+    )(*ready_args)
+    order_columns = order_slots.reshape(ranks, 2)
+    slots, prepared, order_columns, order_rows = lax.optimization_barrier(
+        (slots, prepared, order_columns, order_columns.T)
+    )
+    up_table, down_table, weight = prepared
 
     message = shape((ranks, 8, width), BF)
     rows = pltpu.VMEM((ranks * 8, width), F32)
+    pairs = pltpu.VMEM((2, ranks * 8, width), F32)
+    field = shape(next_grad.shape, F32)
     sent, out_grad = call(
         synth_kernel,
-        (message, shape(next_grad.shape, F32)),
+        (message, field),
         scratch=[
+            pltpu.VMEM(field.shape, F32),
             pltpu.VMEM((lons // 4, 16 * ranks), BF),
             pltpu.VMEM((10 * width, 16 * ranks), BF),
-            pltpu.VMEM((lat_dev, lons, width), F32),
+            pltpu.VMEM(field.shape, F32),
             rows,
         ],
         flops=2 * 1024 * 4096 * 512,
         limit=32,
-    )(slots, next_grad, slope, table, order_columns)
+    )(slots, next_grad, pre_act, table, order_columns)
     by_order = exchange(sent)
-    first, second = call(legendre_kernel, (message, message), scratch=[rows, pltpu.VMEM((2, ranks * 8, width), F32)], flops=2 * 512**3 * 4)(
-        by_order, up_table, down_table, weight, saved_coeffs, spectral_gain
-    )
+    first, second = call(
+        legendre_kernel, (message, message), scratch=[rows, pairs], flops=2 * 512**3 * 4
+    )(by_order, up_table, down_table, weight, saved_coeffs, spectral_gain)
     first = exchange(first)
     second = exchange(call(share_kernel, message)(first, second))
-    partial = call(first_kernel, shape(next_grad.shape, F32), scratch=[rows], flops=2 * 512**3 * 3)(
-        first, order_rows, table, out_grad
-    )
     outs = (shape(next_grad.shape, BF), shape((2, degrees, width), F32))
     return call(
-        second_kernel,
+        field_kernel,
         outs,
-        scratch=[rows]
+        scratch=[pairs]
         + [pltpu.VMEM(o.shape, o.dtype) for o in outs]
         + [pltpu.SemaphoreType.DMA((9,))],
         far_out=True,
         flops=2 * 512**3 * 3,
-    )(second, order_rows, table, partial)
+    )(first, second, order_rows, table, out_grad)
 
 
 def solution(mesh):

time: 140 us -> 133 us (0.950)
  blocking collectives: 61.7 us -> 86.2 us
  waiting for transfers between devices: 22.2 us -> 8.61 us
  starting transfers between devices: 30.6 us -> 21.4 us
  local copies, waits for them, and re-layouts: 9.35 us -> 0.26 us
    all_to_all x2 -> x3, blocking collectives: 61.7 us -> 86.2 us  [exchange(): lax.all_to_all(message, RANKS, split_axis=0, concat_axis=0, tiled=True)]
    all_to_all x2 -> x1, waiting for transfers between devices: 22.2 us -> 8.61 us  [exchange(): lax.all_to_all(message, RANKS, split_axis=0, concat_axis=0, tiled=True)]
    unnamed x32 -> x18, local copies, waits for them, and re-layouts: 9.35 us -> 0.04 us
    all_to_all x2 -> x1, starting transfers between devices: 30.6 us -> 21.4 us  [exchange(): lax.all_to_all(message, RANKS, split_axis=0, concat_axis=0, tiled=True)]
    pallas_call x7 -> x6, Pallas kernels: 14 us -> 14.6 us  [run(): pl.pallas_call(kernel, out_shape=out_shape, in_specs=specs, out_specs=jax...]
  transfers between devices with their start and end apart: 2 -> 1, of which waited for: 2 -> 1; matrix products, arithmetic and copies ran while one was open for 0% -> 0% of each run, Pallas kernels for 2% -> 3%
where the time goes in v3:
time: 133 us; the launch traced here: 132 us
  blocking collectives  86.2 us (65%)
  starting transfers between devices  21.4 us (16%)
  Pallas kernels  14.6 us (11%)
  waiting for transfers between devices  8.61 us (6%)
    all_to_all x3, blocking collectives, exchange(): lax.all_to_all(message, RANKS, split_axis=0, concat_axis=0, tiled=True)  86.2 us
    all_to_all x1, starting transfers between devices, exchange(): lax.all_to_all(message, RANKS, split_axis=0, concat_axis=0, tiled=True)  21.4 us
    pallas_call x6, Pallas kernels, run(): pl.pallas_call(kernel, out_shape=out_shape, in_specs=specs, out_specs=jax...  14.6 us
    all_to_all x1, waiting for transfers between devices, exchange(): lax.all_to_all(message, RANKS, split_axis=0, concat_axis=0, tiled=True)  8.61 us
  transfers between devices with their start and end apart: 1, of which 1 were waited for; matrix products, arithmetic and copies ran while one was open for 0% of the time, Pallas kernels for 3%

profile of v3, /device:TPU:6, one launch (start us, length us, event | category | flops | bytes accessed | tf_op | source)
XLA Modules:
  0.0 132.0 jit_solution(2645349233173886017)
XLA Ops:
  0.6 1.6 %shard_map.149 = f32[256,128]{1,0:T(8,128)} custom-call(s32[1]{0:T(128)} %bitcast.base_ref, bf16[16,256]{1,0:T(8,128)(2,1)} %bitcast.17, bf16[16,256]{1,0:T(8,128)(2,1)} %bitcast.18, bf16[16,256]{1,0:T(8,128)(2,1)} %bitcast.19, s32[16,256]{1,0:T(8,128)} %bitcast.15, s32[16,256]{1,0:T(8,128)} %bitcast.16, s32[1,256]{1,0:T(1,128)} %refs_5_.1), custom_call_target="tpu_custom_call" | custom-call | bytes 189444 | tf_op jit(solution)/shard_map/pallas_call | solution.py:37
  2.2 0.0 copy-start.8
  2.3 21.4 %all-to-all-start = ((f32[256,1,128]{2,1,0:T(1,128)}), f32[256,1,128]{2,1,0:T(1,128)S(1)}, u32[]{:S(2)}, u32[]{:S(2)}) async-start(f32[256,1,128]{2,1,0:T(1,128)} %bitcast.14), calls=%async_computation | async-start | bytes 262144 | tf_op jit(solution)/shard_map/all_to_all | solution.py:288
  23.6 0.0 copy-done.8
  23.6 0.1 reshape.17.order_ref
  23.8 0.1 copy.19
  23.9 0.0 copy-start
  23.9 0.0 copy-start.1
  23.9 0.0 copy-start.2
  23.9 3.9 %shard_map.150 = (bf16[2,512,512]{2,1,0:T(8,128)(2,1)}, bf16[2,512,512]{2,1,0:T(8,128)(2,1)}, f32[512,128]{1,0:T(8,128)}) custom-call(bf16[2,512,512]{2,1,0:T(8,128)(2,1)} %refs_0_.1, f32[1,512]{1,0:T(1,128)} %bitcast.20), custom_call_target="tpu_custom_call" | custom-call | flops 1073741824 | bytes 3409920 | tf_op jit(solution)/shard_map/pallas_call | solution.py:37
  27.8 8.6 %all-to-all-done = f32[256,1,128]{2,1,0:T(1,128)S(1)} async-done(((f32[256,1,128]{2,1,0:T(1,128)}), f32[256,1,128]{2,1,0:T(1,128)S(1)}, u32[]{:S(2)}, u32[]{:S(2)}) %all-to-all-start) | async-done | bytes 131104 | tf_op jit(solution)/shard_map/all_to_all | solution.py:288
  36.4 0.0 copy-done
  36.4 0.0 copy-done.1
  36.4 0.0 copy-done.2
  36.4 0.0 copy-start.5
  36.4 0.0 copy-start.6
  36.4 0.0 copy-start.7
  36.4 5.5 %shard_map.151 = (bf16[256,8,128]{2,1,0:T(8,128)(2,1)S(1)}, f32[2,1024,128]{2,1,0:T(8,128)S(1)}) custom-call(f32[256,128]{1,0:T(8,128)S(1)} %bitcast.12, bf16[2,1024,128]{2,1,0:T(8,128)(2,1)S(1)} %copy-done.1, bf16[2,1024,128]{2,1,0:T(8,128)(2,1)S(1)} %copy-done.2, bf16[2,512,512]{2,1,0:T(8,128)(2,1)S(1)} %copy-done, s32[256,2]{1,0:T(8,128)S(1)} %reshape.17.order_ref), custom_call_target="tpu_custom_call" | custom-call | flops 4294967296 | bytes 3803136 | tf_op jit(solution)/shard_map/pallas_call | solution.py:37
  42.0 0.0 copy-start.3
  42.0 0.0 copy-start.4
  42.0 29.3 %all_to_all.27.got_ref = bf16[256,8,128]{2,1,0:T(8,128)(2,1)S(1)} all-to-all(bf16[256,8,128]{2,1,0:T(8,128)(2,1)S(1)} %get-tuple-element.20), channel_id=1, replica_groups=mesh['lat'=64,'chan'=2,'obs'=4] {'lat','obs'}, dimensions={0} | all-to-all | bytes 1048576 | tf_op jit(solution)/shard_map/all_to_all | solution.py:288
  71.3 0.0 copy-done.5
  71.3 0.0 copy-done.6
  71.3 0.0 copy-done.7
  71.3 0.0 copy-done.3
  71.3 0.0 copy-done.4
  71.4 1.3 shard_map.152
  72.7 28.5 %all_to_all.28.got_ref.first_ref = bf16[256,8,128]{2,1,0:T(8,128)(2,1)S(1)} all-to-all(bf16[256,8,128]{2,1,0:T(8,128)(2,1)S(1)} %get-tuple-element.24), channel_id=1, replica_groups=mesh['lat'=64,'chan'=2,'obs'=4] {'lat','obs'}, dimensions={0} | all-to-all | bytes 1048576 | tf_op jit(solution)/shard_map/all_to_all | solution.py:288
  101.1 0.2 shard_map.153
  101.3 28.4 %all_to_all.29.second_ref = bf16[256,8,128]{2,1,0:T(8,128)(2,1)S(1)} all-to-all(bf16[256,8,128]{2,1,0:T(8,128)(2,1)S(1)} %shard_map.153), channel_id=1, replica_groups=mesh['lat'=64,'chan'=2,'obs'=4] {'lat','obs'}, dimensions={0} | all-to-all | bytes 1048576 | tf_op jit(solution)/shard_map/all_to_all | solution.py:288
  129.7 2.1 %shard_map.154 = (bf16[2,1024,128]{2,1,0:T(8,128)(2,1)}, f32[2,512,128]{2,1,0:T(8,128)}) custom-call(bf16[256,8,128]{2,1,0:T(8,128)(2,1)S(1)} %all_to_all.28.got_ref.first_ref, bf16[256,8,128]{2,1,0:T(8,128)(2,1)S(1)} %all_to_all.29.second_ref, s32[2,256]{1,0:T(2,128)S(1)} %bitcast.13, bf16[2,512,512]{2,1,0:T(8,128)(2,1)S(1)} %copy-done, ...), custom_call_target="tpu_custom_call" | custom-call | flops 805306368 | bytes 4196352 | tf_op jit(solution)/shard_map/pallas_call | solution.py:37
Async XLA Ops:
  2.2 21.4 %copy-start.8 = (s32[512]{0:T(512)S(1)}, s32[512]{0:T(512)}, u32[]{:S(2)}) copy-start(s32[512]{0:T(512)} %param.17) | copy-start | bytes 6148
  2.3 34.1 %all-to-all-start = ((f32[256,1,128]{2,1,0:T(1,128)}), f32[256,1,128]{2,1,0:T(1,128)S(1)}, u32[]{:S(2)}, u32[]{:S(2)}) async-start(f32[256,1,128]{2,1,0:T(1,128)} %bitcast.14), calls=%async_computation | async-start | bytes 262144 | tf_op jit(solution)/shard_map/all_to_all | solution.py:288
  23.9 12.5 %copy-start = (bf16[2,512,512]{2,1,0:T(8,128)(2,1)S(1)}, bf16[2,512,512]{2,1,0:T(8,128)(2,1)}, u32[]{:S(2)}) copy-start(bf16[2,512,512]{2,1,0:T(8,128)(2,1)} %constant.10.clone.table_ref) | copy-start | bytes 3145732
  23.9 12.5 %copy-start.1 = (bf16[2,1024,128]{2,1,0:T(8,128)(2,1)S(1)}, bf16[2,1024,128]{2,1,0:T(8,128)(2,1)}, u32[]{:S(2)}) copy-start(bf16[2,1024,128]{2,1,0:T(8,128)(2,1)} %next_ref.1) | copy-start | bytes 1572868
  23.9 12.5 %copy-start.2 = (bf16[2,1024,128]{2,1,0:T(8,128)(2,1)S(1)}, bf16[2,1024,128]{2,1,0:T(8,128)(2,1)}, u32[]{:S(2)}) copy-start(bf16[2,1024,128]{2,1,0:T(8,128)(2,1)} %pre_ref.1) | copy-start | bytes 1572868
  36.4 34.9 %copy-start.5 = (bf16[2,512,512]{2,1,0:T(8,128)(2,1)S(1)}, bf16[2,512,512]{2,1,0:T(8,128)(2,1)}, u32[]{:S(2)}) copy-start(bf16[2,512,512]{2,1,0:T(8,128)(2,1)} %get-tuple-element.21.up_ref) | copy-start | bytes 3145732
  36.4 34.9 %copy-start.6 = (bf16[2,512,512]{2,1,0:T(8,128)(2,1)S(1)}, bf16[2,512,512]{2,1,0:T(8,128)(2,1)}, u32[]{:S(2)}) copy-start(bf16[2,512,512]{2,1,0:T(8,128)(2,1)} %get-tuple-element.22.down_ref) | copy-start | bytes 3145732
  36.4 34.9 %copy-start.7 = (f32[512,128]{1,0:T(8,128)S(1)}, f32[512,128]{1,0:T(8,128)}, u32[]{:S(2)}) copy-start(f32[512,128]{1,0:T(8,128)} %get-tuple-element.23.weight_ref) | copy-start | bytes 786436
  42.0 29.4 %copy-start.3 = (bf16[2,2,512,128]{3,2,1,0:T(8,128)(2,1)S(1)}, bf16[2,2,512,128]{3,2,1,0:T(8,128)(2,1)}, u32[]{:S(2)}) copy-start(bf16[2,2,512,128]{3,2,1,0:T(8,128)(2,1)} %saved_ref.1) | copy-start | bytes 1572868
  42.0 29.4 %copy-start.4 = (f32[2,512,128]{2,1,0:T(8,128)S(1)}, f32[2,512,128]{2,1,0:T(8,128)}, u32[]{:S(2)}) copy-start(f32[2,512,128]{2,1,0:T(8,128)} %gain_ref.1) | copy-start | bytes 1572868

commit v4 on v3

--- a/solution.py
+++ b/solution.py
@@ -85,22 +85,34 @@
     out_ref[...] = jnp.concatenate(fields, axis=0).T
 
 
-def ready_kernel(*refs):
-    sources, results = refs[:2], refs[2:5]
-    legendre_ref, quad_ref, in_sems, up_ref, down_ref, weight_ref, out_sems = refs[5:]
-    for copy in start_copies(sources, (legendre_ref, quad_ref), in_sems):
-        copy.wait()
+def ready_kernel(far_legendre, far_quad, far_up, far_down, far_weight, legendre_ref, quad_ref, up_ref, down_ref, weight_ref, sems):
+    coming = [
+        pltpu.make_async_copy(far_legendre.at[0], legendre_ref.at[0], sems.at[0]),
+        pltpu.make_async_copy(far_legendre.at[1], legendre_ref.at[1], sems.at[1]),
+        pltpu.make_async_copy(far_quad, quad_ref, sems.at[2]),
+    ]
+    leaving = [pltpu.make_async_copy(weight_ref, far_weight, sems.at[3])]
+    for s in range(2):
+        leaving.append(pltpu.make_async_copy(up_ref.at[s], far_up.at[s], sems.at[4 + 2 * s]))
+        leaving.append(pltpu.make_async_copy(down_ref.at[s], far_down.at[s], sems.at[5 + 2 * s]))
+    for copy in coming:
+        copy.start()
     lats = legendre_ref.shape[2]
     half = lats // 2
     place = iota((lats, lats), 0)
     chosen = (place % half) * 2 + place // half == iota((lats, lats), 1)
+    pick = chosen.astype(BF)
+    for s in range(2):
+        coming[s].wait()
+        up_ref[s] = dot_nt(legendre_ref[s], pick).astype(BF)
+        leaving[1 + 2 * s].start()
+        down_ref[s] = dot_nt(pick, legendre_ref[s]).astype(BF)
+        leaving[2 + 2 * s].start()
+    coming[2].wait()
     quad = jnp.sum(jnp.where(chosen, quad_ref[...], 0.0), axis=1, keepdims=True)
     weight_ref[...] = jnp.broadcast_to(quad, weight_ref.shape)
-    pick = chosen.astype(BF)
-    for s in range(legendre_ref.shape[0]):
-        up_ref[s] = dot_nt(legendre_ref[s], pick).astype(BF)
-        down_ref[s] = dot_nt(pick, legendre_ref[s]).astype(BF)
-    for copy in start_copies((up_ref, down_ref, weight_ref), results, out_sems):
+    leaving[0].start()
+    for copy in leaving:
         copy.wait()
 
 
@@ -120,6 +132,11 @@
     ranks = slots_ref.shape[0]
     capacity = 16
     groups = lons // 4
+    orders = table_ref.shape[1]
+    chosen = [
+        (iota((ranks, orders), 1) == order_ref[:, s : s + 1]).astype(BF) for s in range(2)
+    ]
+    chosen = jnp.concatenate(chosen, axis=0)
     fields = slots_ref[...].T
     value = fields[0:16]
     lat_step = fields[16:32]
@@ -168,20 +185,22 @@
             parts.append((total * slope_ref[k, at : at + lons // 2, :]).astype(BF))
         halves.extend(parts)
     field = jnp.concatenate(halves, axis=1)
-    orders = table_ref.shape[1]
     order_ids = iota((orders, 1), 0)
     sign = jnp.where(order_ids % 2 == 0, 1.0, -1.0)
     scale = jnp.where(order_ids == 0, 1.0, 2.0)
+    totals = []
     for r in range(2):
         both = dot(table_ref[r], field)
         total = (both[:, :pair] + sign * both[:, pair:]) * (scale if r == 0 else -scale)
-        total = total.astype(BF)
-        for s in range(2):
-            chosen = (iota((ranks, orders), 1) == order_ref[:, s : s + 1]).astype(BF)
-            placed = dot(chosen, total)
+        totals.append(total.astype(BF))
+    placed = dot(chosen, jnp.concatenate(totals, axis=1))
+    for s in range(2):
+        for r in range(2):
             for k in range(lat_dev):
-                row = s * 4 + r * 2 + k
-                msg_ref[pl.ds(row, ranks, stride=8), :] = placed[:, k * width : (k + 1) * width]
+                at = r * pair + k * width
+                msg_ref[pl.ds(s * 4 + r * 2 + k, ranks, stride=8), :] = placed[
+                    s * ranks : (s + 1) * ranks, at : at + width
+                ]
     sent_ref[...] = msg_ref[...].reshape(ranks, 8, width).astype(BF)
 
 
@@ -251,29 +270,30 @@
     copies = [pltpu.make_async_copy(share_ref, gain_ref, sems.at[0])]
     copies[0].start()
     msg_ref[0] = first_ref[...].astype(F32).reshape(msg_ref.shape[1:])
-    sign = jnp.where(iota((half, 1), 0) % 2 == 0, 1.0, -1.0)
-    chosen = [
-        (iota((half, ranks), 0) == order_ref[s : s + 1, :]).astype(BF) for s in range(2)
-    ]
+    row = iota((half, ranks), 0)
+    order = (row % ranks) * 2 + row // ranks
+    chosen = [(order == order_ref[s : s + 1, :]).astype(BF) for s in range(2)]
     chosen = jnp.concatenate(chosen, axis=1)
-    both = []
+    placed = []
     for r in range(2):
         parts = []
         for s in range(2):
             lanes = [msg_ref[s, pl.ds(r * 2 + k, ranks, stride=8), :].astype(BF) for k in range(2)]
             parts.append(jnp.concatenate(lanes, axis=1))
-        placed = dot(chosen, jnp.concatenate(parts, axis=0))
-        both.append(jnp.concatenate([placed, placed * sign], axis=1).astype(BF))
+        placed.append(dot(chosen, jnp.concatenate(parts, axis=0)).astype(BF))
+    even = jnp.concatenate([p[:ranks] for p in placed], axis=0)
+    odd = jnp.concatenate([p[ranks:] for p in placed], axis=0)
     block = half // 4
     for i in range(4):
         rows = slice(i * block, (i + 1) * block)
-        part = dot(table_ref[0, rows, :], both[0]) - dot(table_ref[1, rows, :], both[1])
-        part = part * (1.0 / lons)
+        same = dot(table_ref[0, rows, :], even)
+        turned = dot(table_ref[1, rows, :], odd)
         for h in range(2):
             span = slice(h * half + i * block, h * half + (i + 1) * block)
             for k in range(lat_dev):
-                at = (h * lat_dev + k) * width
-                field_ref[k, span, :] = (grad_ref[k, span, :] + part[:, at : at + width]).astype(BF)
+                lanes = slice(k * width, (k + 1) * width)
+                part = same[:, lanes] + turned[:, lanes] if h == 0 else same[:, lanes] - turned[:, lanes]
+                field_ref[k, span, :] = (grad_ref[k, span, :] + part).astype(BF)
             copies.append(
                 pltpu.make_async_copy(
                     field_ref.at[:, span, :], out_ref.at[:, span, :], sems.at[len(copies)]
@@ -313,7 +333,11 @@
     angle = ((index[:, None] * index[None, :]) % lons).astype(np.float32) * np.float32(
         2.0 * math.pi / lons
     )
-    table = jnp.asarray(np.stack([np.cos(angle), np.sin(angle)]).astype(jnp.bfloat16))
+    waves = np.stack([np.cos(angle), np.sin(angle)]).astype(jnp.bfloat16)
+    table = jnp.asarray(waves)
+    back = np.stack([waves[0].astype(np.float32), -waves[1].astype(np.float32)]) / lons
+    back = [np.concatenate([back[0, :, p::2], back[1, :, p::2]], axis=1) for p in range(2)]
+    back = jnp.asarray(np.stack(back).astype(jnp.bfloat16))
 
     base = (lax.axis_index("chan") * width).astype(jnp.int32).reshape(1)
     slot_args = (
@@ -344,7 +368,9 @@
     prepared = call(
         ready_kernel,
         ready,
-        scratch=buffers_for(ready_args) + buffers_for(ready),
+        scratch=buffers_for(ready_args)[:-1]
+        + buffers_for(ready)[:-1]
+        + [pltpu.SemaphoreType.DMA((8,))],
         far=range(2),
         far_out=True,
         flops=4 * 2 * 512**3,
@@ -388,7 +414,7 @@
         + [pltpu.SemaphoreType.DMA((9,))],
         far_out=True,
         flops=2 * 512**3 * 3,
-    )(first, second, order_rows, table, out_grad)
+    )(first, second, order_rows, back, out_grad)
 
 
 def solution(mesh):

time: 133 us -> 132 us (level)
  no operation moved by 1% of the time
where the time goes in v4:
time: 132 us; the launch traced here: 131 us
  blocking collectives  86.1 us (65%)
  starting transfers between devices  21.4 us (16%)
  Pallas kernels  13.8 us (10%)
  waiting for transfers between devices  8.9 us (7%)
    all_to_all x3, blocking collectives, exchange(): lax.all_to_all(message, RANKS, split_axis=0, concat_axis=0, tiled=True)  86.1 us
    all_to_all x1, starting transfers between devices, exchange(): lax.all_to_all(message, RANKS, split_axis=0, concat_axis=0, tiled=True)  21.4 us
    pallas_call x6, Pallas kernels, run(): pl.pallas_call(kernel, out_shape=out_shape, in_specs=specs, out_specs=jax...  13.8 us
    all_to_all x1, waiting for transfers between devices, exchange(): lax.all_to_all(message, RANKS, split_axis=0, concat_axis=0, tiled=True)  8.9 us
  transfers between devices with their start and end apart: 1, of which 1 were waited for; matrix products, arithmetic and copies ran while one was open for 0% of the time, Pallas kernels for 3%

profile of v4, /device:TPU:6, one launch (start us, length us, event | category | flops | bytes accessed | tf_op | source)
XLA Modules:
  0.0 131.3 jit_solution(14282580697669178062)
XLA Ops:
  0.6 1.6 %shard_map.158 = f32[256,128]{1,0:T(8,128)} custom-call(s32[1]{0:T(128)} %bitcast.base_ref, bf16[16,256]{1,0:T(8,128)(2,1)} %bitcast.17, bf16[16,256]{1,0:T(8,128)(2,1)} %bitcast.18, bf16[16,256]{1,0:T(8,128)(2,1)} %bitcast.19, s32[16,256]{1,0:T(8,128)} %bitcast.15, s32[16,256]{1,0:T(8,128)} %bitcast.16, s32[1,256]{1,0:T(1,128)} %refs_5_.1), custom_call_target="tpu_custom_call" | custom-call | bytes 189444 | tf_op jit(solution)/shard_map/pallas_call | solution.py:37
  2.2 0.0 copy-start.9
  2.3 21.4 %all-to-all-start = ((f32[256,1,128]{2,1,0:T(1,128)}), f32[256,1,128]{2,1,0:T(1,128)S(1)}, u32[]{:S(2)}, u32[]{:S(2)}) async-start(f32[256,1,128]{2,1,0:T(1,128)} %bitcast.14), calls=%async_computation | async-start | bytes 262144 | tf_op jit(solution)/shard_map/all_to_all | solution.py:308
  23.6 0.0 copy-done.9
  23.6 0.1 reshape.17.order_ref
  23.8 0.1 copy.20
  23.9 0.0 copy-start.1
  23.9 0.0 copy-start.2
  23.9 0.0 copy-start.5
  23.9 3.6 %shard_map.159 = (bf16[2,512,512]{2,1,0:T(8,128)(2,1)}, bf16[2,512,512]{2,1,0:T(8,128)(2,1)}, f32[512,128]{1,0:T(8,128)}) custom-call(bf16[2,512,512]{2,1,0:T(8,128)(2,1)} %far_legendre.1, f32[1,512]{1,0:T(1,128)} %bitcast.20), custom_call_target="tpu_custom_call" | custom-call | flops 1073741824 | bytes 3409920 | tf_op jit(solution)/shard_map/pallas_call | solution.py:37
  27.5 8.9 %all-to-all-done = f32[256,1,128]{2,1,0:T(1,128)S(1)} async-done(((f32[256,1,128]{2,1,0:T(1,128)}), f32[256,1,128]{2,1,0:T(1,128)S(1)}, u32[]{:S(2)}, u32[]{:S(2)}) %all-to-all-start) | async-done | bytes 131104 | tf_op jit(solution)/shard_map/all_to_all | solution.py:308
  36.4 0.0 copy-done.1
  36.4 0.0 copy-done.2
  36.4 0.0 copy-done.5
  36.4 0.0 copy-start.6
  36.4 0.0 copy-start.7
  36.4 0.0 copy-start.8
  36.4 5.3 %shard_map.160 = (bf16[256,8,128]{2,1,0:T(8,128)(2,1)S(1)}, f32[2,1024,128]{2,1,0:T(8,128)S(1)}) custom-call(f32[256,128]{1,0:T(8,128)S(1)} %bitcast.12, bf16[2,1024,128]{2,1,0:T(8,128)(2,1)S(1)} %copy-done.1, bf16[2,1024,128]{2,1,0:T(8,128)(2,1)S(1)} %copy-done.2, bf16[2,512,512]{2,1,0:T(8,128)(2,1)S(1)} %copy-done.5, s32[256,2]{1,0:T(8,128)S(1)} %reshape.17.order_ref), custom_call_target="tpu_custom_call" | custom-call | flops 4294967296 | bytes 3803136 | tf_op jit(solution)/shard_map/pallas_call | solution.py:37
  41.7 0.0 copy-start.3
  41.7 0.0 copy-start.4
  41.8 29.1 %all_to_all.27.got_ref = bf16[256,8,128]{2,1,0:T(8,128)(2,1)S(1)} all-to-all(bf16[256,8,128]{2,1,0:T(8,128)(2,1)S(1)} %get-tuple-element.20), channel_id=1, replica_groups=mesh['lat'=64,'chan'=2,'obs'=4] {'lat','obs'}, dimensions={0} | all-to-all | bytes 1048576 | tf_op jit(solution)/shard_map/all_to_all | solution.py:308
  70.8 0.0 copy-done.6
  70.8 0.0 copy-done.7
  70.8 0.0 copy-done.8
  70.8 0.0 copy-done.3
  70.8 0.0 copy-done.4
  70.8 1.3 shard_map.161
  72.1 28.5 %all_to_all.28.got_ref.first_ref = bf16[256,8,128]{2,1,0:T(8,128)(2,1)S(1)} all-to-all(bf16[256,8,128]{2,1,0:T(8,128)(2,1)S(1)} %get-tuple-element.24), channel_id=1, replica_groups=mesh['lat'=64,'chan'=2,'obs'=4] {'lat','obs'}, dimensions={0} | all-to-all | bytes 1048576 | tf_op jit(solution)/shard_map/all_to_all | solution.py:308
  100.6 0.0 copy-start
  100.6 0.2 shard_map.162
  100.8 28.6 %all_to_all.29.second_ref = bf16[256,8,128]{2,1,0:T(8,128)(2,1)S(1)} all-to-all(bf16[256,8,128]{2,1,0:T(8,128)(2,1)S(1)} %shard_map.162), channel_id=1, replica_groups=mesh['lat'=64,'chan'=2,'obs'=4] {'lat','obs'}, dimensions={0} | all-to-all | bytes 1048576 | tf_op jit(solution)/shard_map/all_to_all | solution.py:308
  129.3 0.0 copy-done
  129.3 1.8 %shard_map.163 = (bf16[2,1024,128]{2,1,0:T(8,128)(2,1)}, f32[2,512,128]{2,1,0:T(8,128)}) custom-call(bf16[256,8,128]{2,1,0:T(8,128)(2,1)S(1)} %all_to_all.28.got_ref.first_ref, bf16[256,8,128]{2,1,0:T(8,128)(2,1)S(1)} %all_to_all.29.second_ref, s32[2,256]{1,0:T(2,128)S(1)} %bitcast.13, bf16[2,512,512]{2,1,0:T(8,128)(2,1)S(1)} %copy-done, ...), custom_call_target="tpu_custom_call" | custom-call | flops 805306368 | bytes 4196352 | tf_op jit(solution)/shard_map/pallas_call | solution.py:37
Async XLA Ops:
  2.2 21.4 %copy-start.9 = (s32[512]{0:T(512)S(1)}, s32[512]{0:T(512)}, u32[]{:S(2)}) copy-start(s32[512]{0:T(512)} %param.18) | copy-start | bytes 6148
  2.3 34.1 %all-to-all-start = ((f32[256,1,128]{2,1,0:T(1,128)}), f32[256,1,128]{2,1,0:T(1,128)S(1)}, u32[]{:S(2)}, u32[]{:S(2)}) async-start(f32[256,1,128]{2,1,0:T(1,128)} %bitcast.14), calls=%async_computation | async-start | bytes 262144 | tf_op jit(solution)/shard_map/all_to_all | solution.py:308
  23.9 12.5 %copy-start.1 = (bf16[2,1024,128]{2,1,0:T(8,128)(2,1)S(1)}, bf16[2,1024,128]{2,1,0:T(8,128)(2,1)}, u32[]{:S(2)}) copy-start(bf16[2,1024,128]{2,1,0:T(8,128)(2,1)} %next_ref.1) | copy-start | bytes 1572868
  23.9 12.5 %copy-start.2 = (bf16[2,1024,128]{2,1,0:T(8,128)(2,1)S(1)}, bf16[2,1024,128]{2,1,0:T(8,128)(2,1)}, u32[]{:S(2)}) copy-start(bf16[2,1024,128]{2,1,0:T(8,128)(2,1)} %pre_ref.1) | copy-start | bytes 1572868
  23.9 12.5 %copy-start.5 = (bf16[2,512,512]{2,1,0:T(8,128)(2,1)S(1)}, bf16[2,512,512]{2,1,0:T(8,128)(2,1)}, u32[]{:S(2)}) copy-start(bf16[2,512,512]{2,1,0:T(8,128)(2,1)} %constant.12.clone.table_ref) | copy-start | bytes 3145732
  36.4 34.4 %copy-start.6 = (bf16[2,512,512]{2,1,0:T(8,128)(2,1)S(1)}, bf16[2,512,512]{2,1,0:T(8,128)(2,1)}, u32[]{:S(2)}) copy-start(bf16[2,512,512]{2,1,0:T(8,128)(2,1)} %get-tuple-element.21.up_ref) | copy-start | bytes 3145732
  36.4 34.4 %copy-start.7 = (bf16[2,512,512]{2,1,0:T(8,128)(2,1)S(1)}, bf16[2,512,512]{2,1,0:T(8,128)(2,1)}, u32[]{:S(2)}) copy-start(bf16[2,512,512]{2,1,0:T(8,128)(2,1)} %get-tuple-element.22.down_ref) | copy-start | bytes 3145732
  36.4 34.4 %copy-start.8 = (f32[512,128]{1,0:T(8,128)S(1)}, f32[512,128]{1,0:T(8,128)}, u32[]{:S(2)}) copy-start(f32[512,128]{1,0:T(8,128)} %get-tuple-element.23.weight_ref) | copy-start | bytes 786436
  41.7 29.1 %copy-start.3 = (bf16[2,2,512,128]{3,2,1,0:T(8,128)(2,1)S(1)}, bf16[2,2,512,128]{3,2,1,0:T(8,128)(2,1)}, u32[]{:S(2)}) copy-start(bf16[2,2,512,128]{3,2,1,0:T(8,128)(2,1)} %saved_ref.1) | copy-start | bytes 1572868
  41.7 29.1 %copy-start.4 = (f32[2,512,128]{2,1,0:T(8,128)S(1)}, f32[2,512,128]{2,1,0:T(8,128)}, u32[]{:S(2)}) copy-start(f32[2,512,128]{2,1,0:T(8,128)} %gain_ref.1) | copy-start | bytes 1572868
  100.6 28.7 %copy-start = (bf16[2,512,512]{2,1,0:T(8,128)(2,1)S(1)}, bf16[2,512,512]{2,1,0:T(8,128)(2,1)}, u32[]{:S(2)}) copy-start(bf16[2,512,512]{2,1,0:T(8,128)(2,1)} %constant.13.clone.table_ref) | copy-start | bytes 3145732

commit v5 on v4

--- a/solution.py
+++ b/solution.py
@@ -22,7 +22,7 @@
     return lax.dot_general(left, right, NT, preferred_element_type=F32)
 
 
-def call(kernel, out_shape, scratch=(), smem=0, far=(), far_out=False, flops=0, limit=16):
+def call(kernel, out_shape, scratch=(), smem=0, far=(), far_out=False, aliases=None, flops=0, limit=16):
     outs = out_shape if isinstance(out_shape, tuple) else (out_shape,)
     moved = sum(math.prod(o.shape) * o.dtype.itemsize for o in outs)
 
@@ -42,6 +42,7 @@
                 lambda _: pl.BlockSpec(memory_space=pltpu.HBM if far_out else pltpu.VMEM), out_shape
             ),
             scratch_shapes=list(scratch),
+            input_output_aliases=aliases or {},
             compiler_params=pltpu.CompilerParams(vmem_limit_bytes=limit << 20),
             cost_estimate=pl.CostEstimate(flops=flops, bytes_accessed=total, transcendentals=0),
         )(*args)
@@ -85,35 +86,39 @@
     out_ref[...] = jnp.concatenate(fields, axis=0).T
 
 
-def ready_kernel(far_legendre, far_quad, far_up, far_down, far_weight, legendre_ref, quad_ref, up_ref, down_ref, weight_ref, sems):
-    coming = [
-        pltpu.make_async_copy(far_legendre.at[0], legendre_ref.at[0], sems.at[0]),
-        pltpu.make_async_copy(far_legendre.at[1], legendre_ref.at[1], sems.at[1]),
-        pltpu.make_async_copy(far_quad, quad_ref, sems.at[2]),
-    ]
-    leaving = [pltpu.make_async_copy(weight_ref, far_weight, sems.at[3])]
-    for s in range(2):
-        leaving.append(pltpu.make_async_copy(up_ref.at[s], far_up.at[s], sems.at[4 + 2 * s]))
-        leaving.append(pltpu.make_async_copy(down_ref.at[s], far_down.at[s], sems.at[5 + 2 * s]))
-    for copy in coming:
-        copy.start()
-    lats = legendre_ref.shape[2]
-    half = lats // 2
-    place = iota((lats, lats), 0)
-    chosen = (place % half) * 2 + place // half == iota((lats, lats), 1)
-    pick = chosen.astype(BF)
-    for s in range(2):
-        coming[s].wait()
-        up_ref[s] = dot_nt(legendre_ref[s], pick).astype(BF)
-        leaving[1 + 2 * s].start()
-        down_ref[s] = dot_nt(pick, legendre_ref[s]).astype(BF)
-        leaving[2 + 2 * s].start()
-    coming[2].wait()
-    quad = jnp.sum(jnp.where(chosen, quad_ref[...], 0.0), axis=1, keepdims=True)
-    weight_ref[...] = jnp.broadcast_to(quad, weight_ref.shape)
-    leaving[0].start()
-    for copy in leaving:
-        copy.wait()
+def ready_kernel(turn_ref, far_legendre, far_quad, *refs):
+    far_up, far_down, far_weight, legendre_ref, quad_ref, up_ref, down_ref, weight_ref, sems = refs[-9:]
+
+    @pl.when(turn_ref[0] == 1)
+    def _():
+        coming = [
+            pltpu.make_async_copy(far_legendre.at[0], legendre_ref.at[0], sems.at[0]),
+            pltpu.make_async_copy(far_legendre.at[1], legendre_ref.at[1], sems.at[1]),
+            pltpu.make_async_copy(far_quad, quad_ref, sems.at[2]),
+        ]
+        leaving = [pltpu.make_async_copy(weight_ref, far_weight, sems.at[3])]
+        for s in range(2):
+            leaving.append(pltpu.make_async_copy(up_ref.at[s], far_up.at[s], sems.at[4 + 2 * s]))
+            leaving.append(pltpu.make_async_copy(down_ref.at[s], far_down.at[s], sems.at[5 + 2 * s]))
+        for copy in coming:
+            copy.start()
+        lats = legendre_ref.shape[2]
+        half = lats // 2
+        place = iota((lats, lats), 0)
+        chosen = (place % half) * 2 + place // half == iota((lats, lats), 1)
+        pick = chosen.astype(BF)
+        for s in range(2):
+            coming[s].wait()
+            up_ref[s] = dot_nt(legendre_ref[s], pick).astype(BF)
+            leaving[1 + 2 * s].start()
+            down_ref[s] = dot_nt(pick, legendre_ref[s]).astype(BF)
+            leaving[2 + 2 * s].start()
+        coming[2].wait()
+        quad = jnp.sum(jnp.where(chosen, quad_ref[...], 0.0), axis=1, keepdims=True)
+        weight_ref[...] = jnp.broadcast_to(quad, weight_ref.shape)
+        leaving[0].start()
+        for copy in leaving:
+            copy.wait()
 
 
 def tall(row, count):
@@ -339,7 +344,7 @@
     back = [np.concatenate([back[0, :, p::2], back[1, :, p::2]], axis=1) for p in range(2)]
     back = jnp.asarray(np.stack(back).astype(jnp.bfloat16))
 
-    base = (lax.axis_index("chan") * width).astype(jnp.int32).reshape(1)
+    core = lax.axis_index("chan").astype(jnp.int32).reshape(1)
     slot_args = (
         obs_value[0],
         obs_lat_frac[0],
@@ -348,16 +353,14 @@
         obs_channel[0],
         slot_counts,
     )
-    slots = exchange(
-        call(
-            pack_kernel,
-            shape((ranks, 128), F32),
-            scratch=buffers_for(slot_args),
-            smem=1,
-            far=range(1, 7),
-            limit=60,
-        )(base, *slot_args)
-    )
+    packed = call(
+        pack_kernel,
+        shape((ranks, 128), F32),
+        scratch=buffers_for(slot_args),
+        smem=1,
+        far=range(1, 7),
+        limit=60,
+    )(core * width, *slot_args)
 
     ready_args = (legendre, quad_weights.reshape(1, lats))
     ready = (
@@ -365,17 +368,25 @@
         shape((slot_dev, lats, degrees), BF),
         shape((lats, 128), F32),
     )
-    prepared = call(
-        ready_kernel,
-        ready,
-        scratch=buffers_for(ready_args)[:-1]
-        + buffers_for(ready)[:-1]
-        + [pltpu.SemaphoreType.DMA((8,))],
-        far=range(2),
-        far_out=True,
-        flops=4 * 2 * 512**3,
-        limit=60,
-    )(*ready_args)
+
+    def prepare(turn, before=()):
+        return call(
+            ready_kernel,
+            ready,
+            scratch=buffers_for(ready_args)[:-1]
+            + buffers_for(ready)[:-1]
+            + [pltpu.SemaphoreType.DMA((8,))],
+            smem=1,
+            far=range(1, 6),
+            far_out=True,
+            aliases={3 + i: i for i in range(len(before))},
+            flops=4 * 2 * 512**3,
+            limit=60,
+        )(turn, *ready_args, *before)
+
+    packed, prepared = lax.optimization_barrier((packed, prepare(1 - core)))
+    slots = exchange(packed)
+    prepared = prepare(core, prepared)
     order_columns = order_slots.reshape(ranks, 2)
     slots, prepared, order_columns, order_rows = lax.optimization_barrier(
         (slots, prepared, order_columns, order_columns.T)

time: 132 us -> 130 us (0.985)
  blocking collectives: 86.1 us -> 79.9 us
  waiting for transfers between devices: 8.9 us -> 12.4 us
    all_to_all x3, blocking collectives: 86.1 us -> 79.9 us  [exchange(): lax.all_to_all(message, RANKS, split_axis=0, concat_axis=0, tiled=True)]
    all_to_all x1, waiting for transfers between devices: 8.9 us -> 12.4 us  [exchange(): lax.all_to_all(message, RANKS, split_axis=0, concat_axis=0, tiled=True)]
    pallas_call x6 -> x7, Pallas kernels: 13.8 us -> 13.7 us  [run(): pl.pallas_call(kernel, out_shape=out_shape, in_specs=specs, out_specs=jax...]
  transfers between devices with their start and end apart: 1 -> 1, of which waited for: 1 -> 1; matrix products, arithmetic and copies ran while one was open for 0% -> 0% of each run, Pallas kernels for 3% -> 0%
where the time goes in v5:
time: 130 us; the launch traced here: 129 us
  blocking collectives  79.9 us (61%)
  starting transfers between devices  21.4 us (16%)
  Pallas kernels  13.7 us (11%)
  waiting for transfers between devices  12.4 us (10%)
    all_to_all x3, blocking collectives, exchange(): lax.all_to_all(message, RANKS, split_axis=0, concat_axis=0, tiled=True)  79.9 us
    all_to_all x1, starting transfers between devices, exchange(): lax.all_to_all(message, RANKS, split_axis=0, concat_axis=0, tiled=True)  21.4 us
    pallas_call x7, Pallas kernels, run(): pl.pallas_call(kernel, out_shape=out_shape, in_specs=specs, out_specs=jax...  13.7 us
    all_to_all x1, waiting for transfers between devices, exchange(): lax.all_to_all(message, RANKS, split_axis=0, concat_axis=0, tiled=True)  12.4 us
  transfers between devices with their start and end apart: 1, of which 1 were waited for; matrix products, arithmetic and copies ran while one was open for 0% of the time, Pallas kernels for 0%

profile of v5, /device:TPU:6, one launch (start us, length us, event | category | flops | bytes accessed | tf_op | source)
XLA Modules:
  0.0 128.6 jit_solution(6809601047130321190)
XLA Ops:
  0.6 3.5 %shard_map.159 = (bf16[2,512,512]{2,1,0:T(8,128)(2,1)}, bf16[2,512,512]{2,1,0:T(8,128)(2,1)}, f32[512,128]{1,0:T(8,128)}) custom-call(s32[1]{0:T(128)S(6)} %sub.3.turn_ref, bf16[2,512,512]{2,1,0:T(8,128)(2,1)} %far_legendre.3, f32[1,512]{1,0:T(1,128)} %bitcast.20), custom_call_target="tpu_custom_call" | custom-call | flops 1073741824 | bytes 3409924 | tf_op jit(solution)/shard_map/pallas_call | solution.py:37
  4.1 1.6 %shard_map.158 = f32[256,128]{1,0:T(8,128)} custom-call(s32[1]{0:T(128)S(6)} %mul.3.base_ref, bf16[16,256]{1,0:T(8,128)(2,1)} %bitcast.17, bf16[16,256]{1,0:T(8,128)(2,1)} %bitcast.18, bf16[16,256]{1,0:T(8,128)(2,1)} %bitcast.19, s32[16,256]{1,0:T(8,128)} %bitcast.15, s32[16,256]{1,0:T(8,128)} %bitcast.16, s32[1,256]{1,0:T(1,128)} %refs_5_.1), custom_call_target="tpu_custom_call" | custom-call | bytes 189444 | tf_op jit(solution)/shard_map/pallas_call | solution.py:37
  5.7 0.0 copy-start.9
  5.7 21.4 %all-to-all-start = ((f32[256,1,128]{2,1,0:T(1,128)}), f32[256,1,128]{2,1,0:T(1,128)S(1)}, u32[]{:S(2)}, u32[]{:S(2)}) async-start(f32[256,1,128]{2,1,0:T(1,128)} %bitcast.14), calls=%async_computation | async-start | bytes 262144 | tf_op jit(solution)/shard_map/all_to_all | solution.py:313
  27.1 0.0 copy-done.9
  27.1 0.1 reshape.17.order_ref
  27.3 0.1 copy.23
  27.3 0.0 copy-start.1
  27.3 0.0 copy-start.2
  27.3 0.0 copy-start.5
  27.3 0.1 shard_map.160
  27.4 12.4 %all-to-all-done = f32[256,1,128]{2,1,0:T(1,128)S(1)} async-done(((f32[256,1,128]{2,1,0:T(1,128)}), f32[256,1,128]{2,1,0:T(1,128)S(1)}, u32[]{:S(2)}, u32[]{:S(2)}) %all-to-all-start) | async-done | bytes 131104 | tf_op jit(solution)/shard_map/all_to_all | solution.py:313
  39.9 0.0 copy-done.1
  39.9 0.0 copy-done.2
  39.9 0.0 copy-done.5
  39.9 0.0 copy-start.6
  39.9 0.0 copy-start.7
  39.9 0.0 copy-start.8
  39.9 5.3 %shard_map.161 = (bf16[256,8,128]{2,1,0:T(8,128)(2,1)S(1)}, f32[2,1024,128]{2,1,0:T(8,128)S(1)}) custom-call(f32[256,128]{1,0:T(8,128)S(1)} %bitcast.12, bf16[2,1024,128]{2,1,0:T(8,128)(2,1)S(1)} %copy-done.1, bf16[2,1024,128]{2,1,0:T(8,128)(2,1)S(1)} %copy-done.2, bf16[2,512,512]{2,1,0:T(8,128)(2,1)S(1)} %copy-done.5, s32[256,2]{1,0:T(8,128)S(1)} %reshape.17.order_ref), custom_call_target="tpu_custom_call" | custom-call | flops 4294967296 | bytes 3803136 | tf_op jit(solution)/shard_map/pallas_call | solution.py:37
  45.2 0.0 copy-start.3
  45.2 0.0 copy-start.4
  45.2 25.9 %all_to_all.27.got_ref = bf16[256,8,128]{2,1,0:T(8,128)(2,1)S(1)} all-to-all(bf16[256,8,128]{2,1,0:T(8,128)(2,1)S(1)} %get-tuple-element.34), channel_id=1, replica_groups=mesh['lat'=64,'chan'=2,'obs'=4] {'lat','obs'}, dimensions={0} | all-to-all | bytes 1048576 | tf_op jit(solution)/shard_map/all_to_all | solution.py:313
  71.1 0.0 copy-done.6
  71.1 0.0 copy-done.7
  71.1 0.0 copy-done.8
  71.1 0.0 copy-done.3
  71.1 0.0 copy-done.4
  71.1 1.3 %shard_map.162 = (bf16[256,8,128]{2,1,0:T(8,128)(2,1)S(1)}, bf16[256,8,128]{2,1,0:T(8,128)(2,1)S(1)}) custom-call(bf16[256,8,128]{2,1,0:T(8,128)(2,1)S(1)} %all_to_all.27.got_ref, bf16[2,512,512]{2,1,0:T(8,128)(2,1)S(1)} %copy-done.6, bf16[2,512,512]{2,1,0:T(8,128)(2,1)S(1)} %copy-done.7, f32[512,128]{1,0:T(8,128)S(1)} %copy-done.8, ...), custom_call_target="tpu_custom_call" | custom-call | flops 1073741824 | bytes 4980736 | tf_op jit(solution)/shard_map/pallas_call | solution.py:37
  72.4 26.0 %all_to_all.28.got_ref.first_ref = bf16[256,8,128]{2,1,0:T(8,128)(2,1)S(1)} all-to-all(bf16[256,8,128]{2,1,0:T(8,128)(2,1)S(1)} %get-tuple-element.38), channel_id=1, replica_groups=mesh['lat'=64,'chan'=2,'obs'=4] {'lat','obs'}, dimensions={0} | all-to-all | bytes 1048576 | tf_op jit(solution)/shard_map/all_to_all | solution.py:313
  98.4 0.0 copy-start
  98.4 0.2 shard_map.163
  98.6 28.1 %all_to_all.29.second_ref = bf16[256,8,128]{2,1,0:T(8,128)(2,1)S(1)} all-to-all(bf16[256,8,128]{2,1,0:T(8,128)(2,1)S(1)} %shard_map.163), channel_id=1, replica_groups=mesh['lat'=64,'chan'=2,'obs'=4] {'lat','obs'}, dimensions={0} | all-to-all | bytes 1048576 | tf_op jit(solution)/shard_map/all_to_all | solution.py:313
  126.6 0.0 copy-done
  126.6 1.8 %shard_map.164 = (bf16[2,1024,128]{2,1,0:T(8,128)(2,1)}, f32[2,512,128]{2,1,0:T(8,128)}) custom-call(bf16[256,8,128]{2,1,0:T(8,128)(2,1)S(1)} %all_to_all.28.got_ref.first_ref, bf16[256,8,128]{2,1,0:T(8,128)(2,1)S(1)} %all_to_all.29.second_ref, s32[2,256]{1,0:T(2,128)S(1)} %bitcast.13, bf16[2,512,512]{2,1,0:T(8,128)(2,1)S(1)} %copy-done, ...), custom_call_target="tpu_custom_call" | custom-call | flops 805306368 | bytes 4196352 | tf_op jit(solution)/shard_map/pallas_call | solution.py:37
Async XLA Ops:
  5.7 21.4 %copy-start.9 = (s32[512]{0:T(512)S(1)}, s32[512]{0:T(512)}, u32[]{:S(2)}) copy-start(s32[512]{0:T(512)} %param.18) | copy-start | bytes 6148
  5.7 34.1 %all-to-all-start = ((f32[256,1,128]{2,1,0:T(1,128)}), f32[256,1,128]{2,1,0:T(1,128)S(1)}, u32[]{:S(2)}, u32[]{:S(2)}) async-start(f32[256,1,128]{2,1,0:T(1,128)} %bitcast.14), calls=%async_computation | async-start | bytes 262144 | tf_op jit(solution)/shard_map/all_to_all | solution.py:313
  27.3 12.5 %copy-start.1 = (bf16[2,1024,128]{2,1,0:T(8,128)(2,1)S(1)}, bf16[2,1024,128]{2,1,0:T(8,128)(2,1)}, u32[]{:S(2)}) copy-start(bf16[2,1024,128]{2,1,0:T(8,128)(2,1)} %next_ref.1) | copy-start | bytes 1572868
  27.3 12.5 %copy-start.2 = (bf16[2,1024,128]{2,1,0:T(8,128)(2,1)S(1)}, bf16[2,1024,128]{2,1,0:T(8,128)(2,1)}, u32[]{:S(2)}) copy-start(bf16[2,1024,128]{2,1,0:T(8,128)(2,1)} %pre_ref.1) | copy-start | bytes 1572868
  27.3 12.5 %copy-start.5 = (bf16[2,512,512]{2,1,0:T(8,128)(2,1)S(1)}, bf16[2,512,512]{2,1,0:T(8,128)(2,1)}, u32[]{:S(2)}) copy-start(bf16[2,512,512]{2,1,0:T(8,128)(2,1)} %constant.14.clone.table_ref) | copy-start | bytes 3145732
  39.9 31.2 %copy-start.6 = (bf16[2,512,512]{2,1,0:T(8,128)(2,1)S(1)}, bf16[2,512,512]{2,1,0:T(8,128)(2,1)}, u32[]{:S(2)}) copy-start(bf16[2,512,512]{2,1,0:T(8,128)(2,1)} %get-tuple-element.35.up_ref) | copy-start | bytes 3145732
  39.9 31.2 %copy-start.7 = (bf16[2,512,512]{2,1,0:T(8,128)(2,1)S(1)}, bf16[2,512,512]{2,1,0:T(8,128)(2,1)}, u32[]{:S(2)}) copy-start(bf16[2,512,512]{2,1,0:T(8,128)(2,1)} %get-tuple-element.36.down_ref) | copy-start | bytes 3145732
  39.9 31.2 %copy-start.8 = (f32[512,128]{1,0:T(8,128)S(1)}, f32[512,128]{1,0:T(8,128)}, u32[]{:S(2)}) copy-start(f32[512,128]{1,0:T(8,128)} %get-tuple-element.37.weight_ref) | copy-start | bytes 786436
  45.2 25.9 %copy-start.3 = (bf16[2,2,512,128]{3,2,1,0:T(8,128)(2,1)S(1)}, bf16[2,2,512,128]{3,2,1,0:T(8,128)(2,1)}, u32[]{:S(2)}) copy-start(bf16[2,2,512,128]{3,2,1,0:T(8,128)(2,1)} %saved_ref.1) | copy-start | bytes 1572868
  45.2 25.9 %copy-start.4 = (f32[2,512,128]{2,1,0:T(8,128)S(1)}, f32[2,512,128]{2,1,0:T(8,128)}, u32[]{:S(2)}) copy-start(f32[2,512,128]{2,1,0:T(8,128)} %gain_ref.1) | copy-start | bytes 1572868
  98.4 28.2 %copy-start = (bf16[2,512,512]{2,1,0:T(8,128)(2,1)S(1)}, bf16[2,512,512]{2,1,0:T(8,128)(2,1)}, u32[]{:S(2)}) copy-start(bf16[2,512,512]{2,1,0:T(8,128)(2,1)} %constant.15.clone.table_ref) | copy-start | bytes 3145732

commit v6 on v5

--- a/solution.py
+++ b/solution.py
@@ -121,13 +121,47 @@
             copy.wait()
 
 
+def early_kernel(turn_ref, far_order, far_table, far_out, order_ref, table_ref, out_ref, sems):
+    @pl.when(turn_ref[0] == 1)
+    def _():
+        coming = start_copies((far_order, far_table), (order_ref, table_ref), sems)
+        coming[0].wait()
+        orders = table_ref.shape[1]
+        half = orders // 2
+        place = iota((orders, orders), 0)
+        chosen = (place % half) * 2 + place // half == iota((orders, orders), 1)
+        order = jnp.where(chosen, order_ref[...].astype(F32), 0.0)
+        order = jnp.sum(order, axis=1, keepdims=True).astype(jnp.int32)
+        scale = jnp.where(order == 0, 1.0, 2.0)
+        chosen = (iota((orders, orders), 1) == order).astype(BF)
+        coming[1].wait()
+        for r in range(2):
+            out_ref[r] = (dot(chosen, table_ref[r]) * (scale if r == 0 else -scale)).astype(BF)
+        for copy in start_copies((out_ref,), (far_out,), sems):
+            copy.wait()
+
+
 def tall(row, count):
     block = jnp.broadcast_to(row, (16, row.shape[1])).astype(BF)
     return jnp.concatenate([block] * (count // 16), axis=0)
 
 
 def synth_kernel(
-    slots_ref, next_ref, pre_ref, table_ref, order_ref, sent_ref, grad_ref, slope_ref, rows_ref, cols_ref, field_ref, msg_ref
+    core_ref,
+    slots_ref,
+    next_ref,
+    pre_ref,
+    table_ref,
+    early_ref,
+    order_ref,
+    sent_ref,
+    grad_ref,
+    slope_ref,
+    rows_ref,
+    cols_ref,
+    field_ref,
+    halves_ref,
+    msg_ref,
 ):
     values = pre_ref[...].astype(F32)
     cdf = 0.5 * (1.0 + lax.erf(values * 0.7071067811865476))
@@ -138,10 +172,6 @@
     capacity = 16
     groups = lons // 4
     orders = table_ref.shape[1]
-    chosen = [
-        (iota((ranks, orders), 1) == order_ref[:, s : s + 1]).astype(BF) for s in range(2)
-    ]
-    chosen = jnp.concatenate(chosen, axis=0)
     fields = slots_ref[...].T
     value = fields[0:16]
     lat_step = fields[16:32]
@@ -189,23 +219,41 @@
             grad_ref[k, at : at + lons // 2, :] = total
             parts.append((total * slope_ref[k, at : at + lons // 2, :]).astype(BF))
         halves.extend(parts)
-    field = jnp.concatenate(halves, axis=1)
-    order_ids = iota((orders, 1), 0)
-    sign = jnp.where(order_ids % 2 == 0, 1.0, -1.0)
-    scale = jnp.where(order_ids == 0, 1.0, 2.0)
-    totals = []
-    for r in range(2):
-        both = dot(table_ref[r], field)
-        total = (both[:, :pair] + sign * both[:, pair:]) * (scale if r == 0 else -scale)
-        totals.append(total.astype(BF))
-    placed = dot(chosen, jnp.concatenate(totals, axis=1))
-    for s in range(2):
+    halves_ref[...] = jnp.concatenate(halves, axis=1)
+
+    def store(total, r):
+        for s in range(2):
+            for k in range(lat_dev):
+                msg_ref[pl.ds(s * 4 + r * 2 + k, ranks, stride=8), :] = total[
+                    s * ranks : (s + 1) * ranks, k * width : (k + 1) * width
+                ]
+
+    @pl.when(core_ref[0] == 0)
+    def _():
+        order = jnp.concatenate([order_ref[:, s : s + 1] for s in range(2)], axis=0)
+        sign = jnp.where(order % 2 == 0, 1.0, -1.0)
         for r in range(2):
-            for k in range(lat_dev):
-                at = r * pair + k * width
-                msg_ref[pl.ds(s * 4 + r * 2 + k, ranks, stride=8), :] = placed[
-                    s * ranks : (s + 1) * ranks, at : at + width
-                ]
+            both = dot(early_ref[r], halves_ref[...])
+            store(both[:, :pair] + sign * both[:, pair:], r)
+
+    @pl.when(core_ref[0] == 1)
+    def _():
+        chosen = [
+            (iota((ranks, orders), 1) == order_ref[:, s : s + 1]).astype(BF) for s in range(2)
+        ]
+        chosen = jnp.concatenate(chosen, axis=0)
+        order_ids = iota((orders, 1), 0)
+        sign = jnp.where(order_ids % 2 == 0, 1.0, -1.0)
+        scale = jnp.where(order_ids == 0, 1.0, 2.0)
+        totals = []
+        for r in range(2):
+            both = dot(table_ref[r], halves_ref[...])
+            total = (both[:, :pair] + sign * both[:, pair:]) * (scale if r == 0 else -scale)
+            totals.append(total.astype(BF))
+        placed = dot(chosen, jnp.concatenate(totals, axis=1))
+        for r in range(2):
+            store(placed[:, r * pair : (r + 1) * pair], r)
+
     sent_ref[...] = msg_ref[...].reshape(ranks, 8, width).astype(BF)
 
 
@@ -384,7 +432,19 @@
             limit=60,
         )(turn, *ready_args, *before)
 
-    packed, prepared = lax.optimization_barrier((packed, prepare(1 - core)))
+    early_args = (order_slots.reshape(1, orders), table)
+    early = call(
+        early_kernel,
+        shape(table.shape, BF),
+        scratch=buffers_for(early_args)[:-1]
+        + [pltpu.VMEM(table.shape, BF), pltpu.SemaphoreType.DMA((2,))],
+        smem=1,
+        far=range(1, 3),
+        far_out=True,
+        flops=2 * 2 * 512**3,
+        limit=60,
+    )(1 - core, *early_args)
+    packed, prepared, early = lax.optimization_barrier((packed, prepare(1 - core), early))
     slots = exchange(packed)
     prepared = prepare(core, prepared)
     order_columns = order_slots.reshape(ranks, 2)
@@ -405,11 +465,13 @@
             pltpu.VMEM((lons // 4, 16 * ranks), BF),
             pltpu.VMEM((10 * width, 16 * ranks), BF),
             pltpu.VMEM(field.shape, F32),
+            pltpu.VMEM((lons // 2, 2 * lat_dev * width), BF),
             rows,
         ],
+        smem=1,
         flops=2 * 1024 * 4096 * 512,
         limit=32,
-    )(slots, next_grad, pre_act, table, order_columns)
+    )(core, slots, next_grad, pre_act, table, early, order_columns)
     by_order = exchange(sent)
     first, second = call(
         legendre_kernel, (message, message), scratch=[rows, pairs], flops=2 * 512**3 * 4

time: 130 us -> 128 us (0.985)
  blocking collectives: 79.9 us -> 76.2 us
  Pallas kernels: 13.7 us -> 15.8 us
    all_to_all x3, blocking collectives: 79.9 us -> 76.2 us  [exchange(): lax.all_to_all(message, RANKS, split_axis=0, concat_axis=0, tiled=True)]
    pallas_call x7 -> x8, Pallas kernels: 13.7 us -> 15.8 us  [run(): pl.pallas_call(kernel, out_shape=out_shape, in_specs=specs, out_specs=jax...]
where the time goes in v6:
time: 128 us; the launch traced here: 127 us
  blocking collectives  76.2 us (60%)
  starting transfers between devices  21.4 us (17%)
  Pallas kernels  15.8 us (12%)
  waiting for transfers between devices  12.4 us (10%)
    all_to_all x3, blocking collectives, exchange(): lax.all_to_all(message, RANKS, split_axis=0, concat_axis=0, tiled=True)  76.2 us
    all_to_all x1, starting transfers between devices, exchange(): lax.all_to_all(message, RANKS, split_axis=0, concat_axis=0, tiled=True)  21.4 us
    pallas_call x8, Pallas kernels, run(): pl.pallas_call(kernel, out_shape=out_shape, in_specs=specs, out_specs=jax...  15.8 us
    all_to_all x1, waiting for transfers between devices, exchange(): lax.all_to_all(message, RANKS, split_axis=0, concat_axis=0, tiled=True)  12.4 us
  transfers between devices with their start and end apart: 1, of which 1 were waited for; matrix products, arithmetic and copies ran while one was open for 0% of the time, Pallas kernels for 0%

profile of v6, /device:TPU:6, one launch (start us, length us, event | category | flops | bytes accessed | tf_op | source)
XLA Modules:
  0.0 127.0 jit_solution(15521623526807018096)
XLA Ops:
  0.6 3.5 %shard_map.159 = (bf16[2,512,512]{2,1,0:T(8,128)(2,1)}, bf16[2,512,512]{2,1,0:T(8,128)(2,1)}, f32[512,128]{1,0:T(8,128)}) custom-call(s32[1]{0:T(128)S(6)} %sub.4.turn_ref, bf16[2,512,512]{2,1,0:T(8,128)(2,1)} %far_legendre.3, f32[1,512]{1,0:T(1,128)} %bitcast.22), custom_call_target="tpu_custom_call" | custom-call | flops 1073741824 | bytes 3409924 | tf_op jit(solution)/shard_map/pallas_call | solution.py:37
  4.1 3.0 %shard_map.160.early_ref = bf16[2,512,512]{2,1,0:T(8,128)(2,1)} custom-call(s32[1]{0:T(128)S(6)} %sub.4.turn_ref, s32[1,512]{1,0:T(1,128)} %bitcast.21, bf16[2,512,512]{2,1,0:T(8,128)(2,1)} %constant.14.clone.far_table.table_ref), custom_call_target="tpu_custom_call" | custom-call | flops 536870912 | bytes 2099204 | tf_op jit(solution)/shard_map/pallas_call | solution.py:37
  7.1 1.6 %shard_map.158 = f32[256,128]{1,0:T(8,128)} custom-call(s32[1]{0:T(128)S(6)} %mul.3.base_ref, bf16[16,256]{1,0:T(8,128)(2,1)} %bitcast.18, bf16[16,256]{1,0:T(8,128)(2,1)} %bitcast.19, bf16[16,256]{1,0:T(8,128)(2,1)} %bitcast.20, s32[16,256]{1,0:T(8,128)} %bitcast.16, s32[16,256]{1,0:T(8,128)} %bitcast.17, s32[1,256]{1,0:T(1,128)} %refs_5_.1), custom_call_target="tpu_custom_call" | custom-call | bytes 189444 | tf_op jit(solution)/shard_map/pallas_call | solution.py:37
  8.7 0.0 copy-start.10
  8.7 21.4 %all-to-all-start = ((f32[256,1,128]{2,1,0:T(1,128)}), f32[256,1,128]{2,1,0:T(1,128)S(1)}, u32[]{:S(2)}, u32[]{:S(2)}) async-start(f32[256,1,128]{2,1,0:T(1,128)} %bitcast.15), calls=%async_computation | async-start | bytes 262144 | tf_op jit(solution)/shard_map/all_to_all | solution.py:361
  30.1 0.0 copy-done.10
  30.1 0.1 reshape.21.order_ref
  30.2 0.1 copy.23
  30.3 0.0 copy-start
  30.3 0.0 copy-start.1
  30.3 0.0 copy-start.3
  30.3 0.0 copy-start.4
  30.3 0.1 shard_map.161
  30.4 12.4 %all-to-all-done = f32[256,1,128]{2,1,0:T(1,128)S(1)} async-done(((f32[256,1,128]{2,1,0:T(1,128)}), f32[256,1,128]{2,1,0:T(1,128)S(1)}, u32[]{:S(2)}, u32[]{:S(2)}) %all-to-all-start) | async-done | bytes 131104 | tf_op jit(solution)/shard_map/all_to_all | solution.py:361
  42.8 0.0 copy-done
  42.8 0.0 copy-done.1
  42.8 0.0 copy-done.3
  42.8 0.0 copy-done.4
  42.8 0.0 copy-start.7
  42.8 0.0 copy-start.8
  42.9 0.0 copy-start.9
  42.9 4.3 %shard_map.162 = (bf16[256,8,128]{2,1,0:T(8,128)(2,1)S(1)}, f32[2,1024,128]{2,1,0:T(8,128)S(1)}) custom-call(s32[1]{0:T(128)} %bitcast.turn_ref.core_ref, f32[256,128]{1,0:T(8,128)S(1)} %bitcast.13, bf16[2,1024,128]{2,1,0:T(8,128)(2,1)S(1)} %copy-done.3, bf16[2,1024,128]{2,1,0:T(8,128)(2,1)S(1)} %copy-done.4, bf16[2,512,512]{2,1,0:T(8,128)(2,1)S(1)} %copy-done, ...), custom_call_target="tpu_custom_call" | custom-call | flops 4294967296 | bytes 4851716 | tf_op jit(solution)/shard_map/pallas_call | solution.py:37
  47.2 0.0 copy-start.5
  47.2 0.0 copy-start.6
  47.2 25.6 %all_to_all.27.got_ref = bf16[256,8,128]{2,1,0:T(8,128)(2,1)S(1)} all-to-all(bf16[256,8,128]{2,1,0:T(8,128)(2,1)S(1)} %get-tuple-element.36), channel_id=1, replica_groups=mesh['lat'=64,'chan'=2,'obs'=4] {'lat','obs'}, dimensions={0} | all-to-all | bytes 1048576 | tf_op jit(solution)/shard_map/all_to_all | solution.py:361
  72.9 0.0 copy-done.7
  72.9 0.0 copy-done.8
  72.9 0.0 copy-done.9
  72.9 0.0 copy-done.5
  72.9 0.0 copy-done.6
  72.9 1.3 %shard_map.163 = (bf16[256,8,128]{2,1,0:T(8,128)(2,1)S(1)}, bf16[256,8,128]{2,1,0:T(8,128)(2,1)S(1)}) custom-call(bf16[256,8,128]{2,1,0:T(8,128)(2,1)S(1)} %all_to_all.27.got_ref, bf16[2,512,512]{2,1,0:T(8,128)(2,1)S(1)} %copy-done.7, bf16[2,512,512]{2,1,0:T(8,128)(2,1)S(1)} %copy-done.8, f32[512,128]{1,0:T(8,128)S(1)} %copy-done.9, ...), custom_call_target="tpu_custom_call" | custom-call | flops 1073741824 | bytes 4980736 | tf_op jit(solution)/shard_map/pallas_call | solution.py:37
  74.2 25.2 %all_to_all.28.got_ref.first_ref = bf16[256,8,128]{2,1,0:T(8,128)(2,1)S(1)} all-to-all(bf16[256,8,128]{2,1,0:T(8,128)(2,1)S(1)} %get-tuple-element.40), channel_id=1, replica_groups=mesh['lat'=64,'chan'=2,'obs'=4] {'lat','obs'}, dimensions={0} | all-to-all | bytes 1048576 | tf_op jit(solution)/shard_map/all_to_all | solution.py:361
  99.5 0.0 copy-start.2
  99.5 0.2 shard_map.164
  99.6 25.4 %all_to_all.29.second_ref = bf16[256,8,128]{2,1,0:T(8,128)(2,1)S(1)} all-to-all(bf16[256,8,128]{2,1,0:T(8,128)(2,1)S(1)} %shard_map.164), channel_id=1, replica_groups=mesh['lat'=64,'chan'=2,'obs'=4] {'lat','obs'}, dimensions={0} | all-to-all | bytes 1048576 | tf_op jit(solution)/shard_map/all_to_all | solution.py:361
  125.0 0.0 copy-done.2
  125.0 1.8 %shard_map.165 = (bf16[2,1024,128]{2,1,0:T(8,128)(2,1)}, f32[2,512,128]{2,1,0:T(8,128)}) custom-call(bf16[256,8,128]{2,1,0:T(8,128)(2,1)S(1)} %all_to_all.28.got_ref.first_ref, bf16[256,8,128]{2,1,0:T(8,128)(2,1)S(1)} %all_to_all.29.second_ref, s32[2,256]{1,0:T(2,128)S(1)} %bitcast.14, bf16[2,512,512]{2,1,0:T(8,128)(2,1)S(1)} %copy-done.2, ...), custom_call_target="tpu_custom_call" | custom-call | flops 805306368 | bytes 4196352 | tf_op jit(solution)/shard_map/pallas_call | solution.py:37
Async XLA Ops:
  8.7 21.4 %copy-start.10 = (s32[512]{0:T(512)S(1)}, s32[512]{0:T(512)}, u32[]{:S(2)}) copy-start(s32[512]{0:T(512)} %param.18) | copy-start | bytes 6148
  8.7 34.1 %all-to-all-start = ((f32[256,1,128]{2,1,0:T(1,128)}), f32[256,1,128]{2,1,0:T(1,128)S(1)}, u32[]{:S(2)}, u32[]{:S(2)}) async-start(f32[256,1,128]{2,1,0:T(1,128)} %bitcast.15), calls=%async_computation | async-start | bytes 262144 | tf_op jit(solution)/shard_map/all_to_all | solution.py:361
  30.3 12.5 %copy-start = (bf16[2,512,512]{2,1,0:T(8,128)(2,1)S(1)}, bf16[2,512,512]{2,1,0:T(8,128)(2,1)}, u32[]{:S(2)}) copy-start(bf16[2,512,512]{2,1,0:T(8,128)(2,1)} %constant.14.clone.far_table.table_ref) | copy-start | bytes 3145732
  30.3 12.5 %copy-start.1 = (bf16[2,512,512]{2,1,0:T(8,128)(2,1)S(1)}, bf16[2,512,512]{2,1,0:T(8,128)(2,1)}, u32[]{:S(2)}) copy-start(bf16[2,512,512]{2,1,0:T(8,128)(2,1)} %shard_map.160.early_ref) | copy-start | bytes 3145732
  30.3 12.5 %copy-start.3 = (bf16[2,1024,128]{2,1,0:T(8,128)(2,1)S(1)}, bf16[2,1024,128]{2,1,0:T(8,128)(2,1)}, u32[]{:S(2)}) copy-start(bf16[2,1024,128]{2,1,0:T(8,128)(2,1)} %next_ref.1) | copy-start | bytes 1572868
  30.3 12.5 %copy-start.4 = (bf16[2,1024,128]{2,1,0:T(8,128)(2,1)S(1)}, bf16[2,1024,128]{2,1,0:T(8,128)(2,1)}, u32[]{:S(2)}) copy-start(bf16[2,1024,128]{2,1,0:T(8,128)(2,1)} %pre_ref.1) | copy-start | bytes 1572868
  42.8 30.0 %copy-start.7 = (bf16[2,512,512]{2,1,0:T(8,128)(2,1)S(1)}, bf16[2,512,512]{2,1,0:T(8,128)(2,1)}, u32[]{:S(2)}) copy-start(bf16[2,512,512]{2,1,0:T(8,128)(2,1)} %get-tuple-element.37.up_ref) | copy-start | bytes 3145732
  42.8 30.0 %copy-start.8 = (bf16[2,512,512]{2,1,0:T(8,128)(2,1)S(1)}, bf16[2,512,512]{2,1,0:T(8,128)(2,1)}, u32[]{:S(2)}) copy-start(bf16[2,512,512]{2,1,0:T(8,128)(2,1)} %get-tuple-element.38.down_ref) | copy-start | bytes 3145732
  42.9 30.0 %copy-start.9 = (f32[512,128]{1,0:T(8,128)S(1)}, f32[512,128]{1,0:T(8,128)}, u32[]{:S(2)}) copy-start(f32[512,128]{1,0:T(8,128)} %get-tuple-element.39.weight_ref) | copy-start | bytes 786436
  47.2 25.7 %copy-start.5 = (bf16[2,2,512,128]{3,2,1,0:T(8,128)(2,1)S(1)}, bf16[2,2,512,128]{3,2,1,0:T(8,128)(2,1)}, u32[]{:S(2)}) copy-start(bf16[2,2,512,128]{3,2,1,0:T(8,128)(2,1)} %saved_ref.1) | copy-start | bytes 1572868
  47.2 25.7 %copy-start.6 = (f32[2,512,128]{2,1,0:T(8,128)S(1)}, f32[2,512,128]{2,1,0:T(8,128)}, u32[]{:S(2)}) copy-start(f32[2,512,128]{2,1,0:T(8,128)} %gain_ref.1) | copy-start | bytes 1572868
  99.5 25.5 %copy-start.2 = (bf16[2,512,512]{2,1,0:T(8,128)(2,1)S(1)}, bf16[2,512,512]{2,1,0:T(8,128)(2,1)}, u32[]{:S(2)}) copy-start(bf16[2,512,512]{2,1,0:T(8,128)(2,1)} %constant.15.clone.table_ref) | copy-start | bytes 3145732

commit v7 on v6

--- a/solution.py
+++ b/solution.py
@@ -86,26 +86,24 @@
     out_ref[...] = jnp.concatenate(fields, axis=0).T
 
 
-def ready_kernel(turn_ref, far_legendre, far_quad, *refs):
-    far_up, far_down, far_weight, legendre_ref, quad_ref, up_ref, down_ref, weight_ref, sems = refs[-9:]
-
-    @pl.when(turn_ref[0] == 1)
-    def _():
-        coming = [
-            pltpu.make_async_copy(far_legendre.at[0], legendre_ref.at[0], sems.at[0]),
-            pltpu.make_async_copy(far_legendre.at[1], legendre_ref.at[1], sems.at[1]),
-            pltpu.make_async_copy(far_quad, quad_ref, sems.at[2]),
-        ]
-        leaving = [pltpu.make_async_copy(weight_ref, far_weight, sems.at[3])]
-        for s in range(2):
-            leaving.append(pltpu.make_async_copy(up_ref.at[s], far_up.at[s], sems.at[4 + 2 * s]))
-            leaving.append(pltpu.make_async_copy(down_ref.at[s], far_down.at[s], sems.at[5 + 2 * s]))
-        for copy in coming:
-            copy.start()
-        lats = legendre_ref.shape[2]
-        half = lats // 2
-        place = iota((lats, lats), 0)
-        chosen = (place % half) * 2 + place // half == iota((lats, lats), 1)
+def parted(count):
+    place = iota((count, count), 0)
+    return (place % (count // 2)) * 2 + place // (count // 2) == iota((count, count), 1)
+
+
+def legendre_tables(chosen, sources, buffers, results, far, sems):
+    legendre_ref, quad_ref = buffers
+    up_ref, down_ref, weight_ref = results
+    coming = [pltpu.make_async_copy(sources[0].at[s], legendre_ref.at[s], sems.at[s]) for s in range(2)]
+    coming.append(pltpu.make_async_copy(sources[1], quad_ref, sems.at[2]))
+    leaving = [pltpu.make_async_copy(weight_ref, far[2], sems.at[3])]
+    for s in range(2):
+        leaving.append(pltpu.make_async_copy(up_ref.at[s], far[0].at[s], sems.at[4 + 2 * s]))
+        leaving.append(pltpu.make_async_copy(down_ref.at[s], far[1].at[s], sems.at[5 + 2 * s]))
+    for copy in coming:
+        copy.start()
+
+    def work():
         pick = chosen.astype(BF)
         for s in range(2):
             coming[s].wait()
@@ -117,27 +115,45 @@
         quad = jnp.sum(jnp.where(chosen, quad_ref[...], 0.0), axis=1, keepdims=True)
         weight_ref[...] = jnp.broadcast_to(quad, weight_ref.shape)
         leaving[0].start()
+
+    return work, leaving
+
+
+def ready_kernel(turn_ref, far_legendre, far_quad, _up, _down, _weight, *refs):
+    far, buffers, results, sems = refs[:3], refs[3:5], refs[5:8], refs[8]
+
+    @pl.when(turn_ref[0] == 1)
+    def _():
+        chosen = parted(buffers[0].shape[2])
+        work, leaving = legendre_tables(chosen, (far_legendre, far_quad), buffers, results, far, sems)
+        work()
         for copy in leaving:
             copy.wait()
 
 
-def early_kernel(turn_ref, far_order, far_table, far_out, order_ref, table_ref, out_ref, sems):
+def early_kernel(turn_ref, far_legendre, far_quad, far_order, far_table, *refs):
+    far, far_early, buffers, results, sems = refs[:3], refs[3], refs[4:6], refs[6:9], refs[9]
+    order_ref, table_ref, early_ref, more_sems = refs[10:]
+
     @pl.when(turn_ref[0] == 1)
     def _():
-        coming = start_copies((far_order, far_table), (order_ref, table_ref), sems)
+        chosen = parted(buffers[0].shape[2])
+        work, leaving = legendre_tables(chosen, (far_legendre, far_quad), buffers, results, far, sems)
+        coming = start_copies((far_order, far_table), (order_ref, table_ref), more_sems)
+        work()
         coming[0].wait()
         orders = table_ref.shape[1]
-        half = orders // 2
-        place = iota((orders, orders), 0)
-        chosen = (place % half) * 2 + place // half == iota((orders, orders), 1)
         order = jnp.where(chosen, order_ref[...].astype(F32), 0.0)
         order = jnp.sum(order, axis=1, keepdims=True).astype(jnp.int32)
         scale = jnp.where(order == 0, 1.0, 2.0)
-        chosen = (iota((orders, orders), 1) == order).astype(BF)
+        placed = (iota((orders, orders), 1) == order).astype(BF)
         coming[1].wait()
         for r in range(2):
-            out_ref[r] = (dot(chosen, table_ref[r]) * (scale if r == 0 else -scale)).astype(BF)
-        for copy in start_copies((out_ref,), (far_out,), sems):
+            early_ref[r] = (dot(placed, table_ref[r]) * (scale if r == 0 else -scale)).astype(BF)
+            copy = pltpu.make_async_copy(early_ref.at[r], far_early.at[r], more_sems.at[2 + r])
+            copy.start()
+            leaving.append(copy)
+        for copy in leaving:
             copy.wait()
 
 
@@ -416,37 +432,36 @@
         shape((slot_dev, lats, degrees), BF),
         shape((lats, 128), F32),
     )
-
-    def prepare(turn, before=()):
-        return call(
-            ready_kernel,
-            ready,
-            scratch=buffers_for(ready_args)[:-1]
-            + buffers_for(ready)[:-1]
-            + [pltpu.SemaphoreType.DMA((8,))],
-            smem=1,
-            far=range(1, 6),
-            far_out=True,
-            aliases={3 + i: i for i in range(len(before))},
-            flops=4 * 2 * 512**3,
-            limit=60,
-        )(turn, *ready_args, *before)
-
+    ready_scratch = (
+        buffers_for(ready_args)[:-1] + buffers_for(ready)[:-1] + [pltpu.SemaphoreType.DMA((8,))]
+    )
     early_args = (order_slots.reshape(1, orders), table)
-    early = call(
+
+    *prepared, early = call(
         early_kernel,
-        shape(table.shape, BF),
-        scratch=buffers_for(early_args)[:-1]
-        + [pltpu.VMEM(table.shape, BF), pltpu.SemaphoreType.DMA((2,))],
+        (*ready, shape(table.shape, BF)),
+        scratch=ready_scratch
+        + buffers_for(early_args)[:-1]
+        + [pltpu.VMEM(table.shape, BF), pltpu.SemaphoreType.DMA((4,))],
         smem=1,
-        far=range(1, 3),
+        far=range(1, 5),
         far_out=True,
-        flops=2 * 2 * 512**3,
+        flops=6 * 2 * 512**3,
         limit=60,
-    )(1 - core, *early_args)
-    packed, prepared, early = lax.optimization_barrier((packed, prepare(1 - core), early))
+    )(1 - core, *ready_args, *early_args)
+    packed, prepared, early = lax.optimization_barrier((packed, prepared, early))
     slots = exchange(packed)
-    prepared = prepare(core, prepared)
+    prepared = call(
+        ready_kernel,
+        ready,
+        scratch=ready_scratch,
+        smem=1,
+        far=range(1, 6),
+        far_out=True,
+        aliases={3: 0, 4: 1, 5: 2},
+        flops=4 * 2 * 512**3,
+        limit=60,
+    )(core, *ready_args, *prepared)
     order_columns = order_slots.reshape(ranks, 2)
     slots, prepared, order_columns, order_rows = lax.optimization_barrier(
         (slots, prepared, order_columns, order_columns.T)

time: 128 us -> 126 us (0.984)
  Pallas kernels: 15.8 us -> 13.9 us
    pallas_call x8 -> x7, Pallas kernels: 15.8 us -> 13.9 us  [run(): pl.pallas_call(kernel, out_shape=out_shape, in_specs=specs, out_specs=jax...]
where the time goes in v7:
time: 126 us; the launch traced here: 125 us
  blocking collectives  76 us (60%)
  starting transfers between devices  21.4 us (17%)
  Pallas kernels  13.9 us (11%)
  waiting for transfers between devices  12.4 us (10%)
    all_to_all x3, blocking collectives, exchange(): lax.all_to_all(message, RANKS, split_axis=0, concat_axis=0, tiled=True)  76 us
    all_to_all x1, starting transfers between devices, exchange(): lax.all_to_all(message, RANKS, split_axis=0, concat_axis=0, tiled=True)  21.4 us
    pallas_call x7, Pallas kernels, run(): pl.pallas_call(kernel, out_shape=out_shape, in_specs=specs, out_specs=jax...  13.9 us
    all_to_all x1, waiting for transfers between devices, exchange(): lax.all_to_all(message, RANKS, split_axis=0, concat_axis=0, tiled=True)  12.4 us
  transfers between devices with their start and end apart: 1, of which 1 were waited for; matrix products, arithmetic and copies ran while one was open for 0% of the time, Pallas kernels for 0%

profile of v7, /device:TPU:6, one launch (start us, length us, event | category | flops | bytes accessed | tf_op | source)
XLA Modules:
  0.0 125.0 jit_solution(6113112569165266144)
XLA Ops:
  0.6 4.5 %shard_map.159 = (bf16[2,512,512]{2,1,0:T(8,128)(2,1)}, bf16[2,512,512]{2,1,0:T(8,128)(2,1)}, f32[512,128]{1,0:T(8,128)}, bf16[2,512,512]{2,1,0:T(8,128)(2,1)}) custom-call(s32[1]{0:T(128)S(6)} %sub.3.turn_ref, bf16[2,512,512]{2,1,0:T(8,128)(2,1)} %far_legendre.3, f32[1,512]{1,0:T(1,128)} %bitcast.22, s32[1,512]{1,0:T(1,128)} %bitcast.21, ...), custom_call_target="tpu_custom_call" | custom-call | flops 1610612736 | bytes 5509124 | tf_op jit(solution)/shard_map/pallas_call | solution.py:37
  5.2 1.6 %shard_map.158 = f32[256,128]{1,0:T(8,128)} custom-call(s32[1]{0:T(128)S(6)} %mul.3.base_ref, bf16[16,256]{1,0:T(8,128)(2,1)} %bitcast.18, bf16[16,256]{1,0:T(8,128)(2,1)} %bitcast.19, bf16[16,256]{1,0:T(8,128)(2,1)} %bitcast.20, s32[16,256]{1,0:T(8,128)} %bitcast.16, s32[16,256]{1,0:T(8,128)} %bitcast.17, s32[1,256]{1,0:T(1,128)} %refs_5_.1), custom_call_target="tpu_custom_call" | custom-call | bytes 189444 | tf_op jit(solution)/shard_map/pallas_call | solution.py:37
  6.8 0.0 copy-start.10
  6.8 21.4 %all-to-all-start = ((f32[256,1,128]{2,1,0:T(1,128)}), f32[256,1,128]{2,1,0:T(1,128)S(1)}, u32[]{:S(2)}, u32[]{:S(2)}) async-start(f32[256,1,128]{2,1,0:T(1,128)} %bitcast.15), calls=%async_computation | async-start | bytes 262144 | tf_op jit(solution)/shard_map/all_to_all | solution.py:377
  28.2 0.0 copy-done.10
  28.2 0.1 reshape.21.order_ref
  28.3 0.1 copy.23
  28.4 0.0 copy-start.1
  28.4 0.0 copy-start.2
  28.4 0.0 copy-start.5
  28.4 0.0 copy-start.9
  28.4 0.1 shard_map.160
  28.5 12.4 %all-to-all-done = f32[256,1,128]{2,1,0:T(1,128)S(1)} async-done(((f32[256,1,128]{2,1,0:T(1,128)}), f32[256,1,128]{2,1,0:T(1,128)S(1)}, u32[]{:S(2)}, u32[]{:S(2)}) %all-to-all-start) | async-done | bytes 131104 | tf_op jit(solution)/shard_map/all_to_all | solution.py:377
  40.9 0.0 copy-done.1
  40.9 0.0 copy-done.2
  41.0 0.0 copy-done.5
  41.0 0.0 copy-done.9
  41.0 0.0 copy-start.6
  41.0 0.0 copy-start.7
  41.0 0.0 copy-start.8
  41.0 4.4 %shard_map.161 = (bf16[256,8,128]{2,1,0:T(8,128)(2,1)S(1)}, f32[2,1024,128]{2,1,0:T(8,128)S(1)}) custom-call(s32[1]{0:T(128)} %bitcast.turn_ref.core_ref, f32[256,128]{1,0:T(8,128)S(1)} %bitcast.13, bf16[2,1024,128]{2,1,0:T(8,128)(2,1)S(1)} %copy-done.1, bf16[2,1024,128]{2,1,0:T(8,128)(2,1)S(1)} %copy-done.2, bf16[2,512,512]{2,1,0:T(8,128)(2,1)S(1)} %copy-done.5, ...), custom_call_target="tpu_custom_call" | custom-call | flops 4294967296 | bytes 4851716 | tf_op jit(solution)/shard_map/pallas_call | solution.py:37
  45.4 0.0 copy-start.3
  45.4 0.0 copy-start.4
  45.4 25.6 %all_to_all.27.got_ref = bf16[256,8,128]{2,1,0:T(8,128)(2,1)S(1)} all-to-all(bf16[256,8,128]{2,1,0:T(8,128)(2,1)S(1)} %get-tuple-element.38), channel_id=1, replica_groups=mesh['lat'=64,'chan'=2,'obs'=4] {'lat','obs'}, dimensions={0} | all-to-all | bytes 1048576 | tf_op jit(solution)/shard_map/all_to_all | solution.py:377
  70.9 0.0 copy-done.6
  70.9 0.0 copy-done.7
  70.9 0.0 copy-done.8
  71.0 0.0 copy-done.3
  71.0 0.0 copy-done.4
  71.0 1.3 %shard_map.162 = (bf16[256,8,128]{2,1,0:T(8,128)(2,1)S(1)}, bf16[256,8,128]{2,1,0:T(8,128)(2,1)S(1)}) custom-call(bf16[256,8,128]{2,1,0:T(8,128)(2,1)S(1)} %all_to_all.27.got_ref, bf16[2,512,512]{2,1,0:T(8,128)(2,1)S(1)} %copy-done.6, bf16[2,512,512]{2,1,0:T(8,128)(2,1)S(1)} %copy-done.7, f32[512,128]{1,0:T(8,128)S(1)} %copy-done.8, ...), custom_call_target="tpu_custom_call" | custom-call | flops 1073741824 | bytes 4980736 | tf_op jit(solution)/shard_map/pallas_call | solution.py:37
  72.3 25.2 %all_to_all.28.got_ref.first_ref = bf16[256,8,128]{2,1,0:T(8,128)(2,1)S(1)} all-to-all(bf16[256,8,128]{2,1,0:T(8,128)(2,1)S(1)} %get-tuple-element.42), channel_id=1, replica_groups=mesh['lat'=64,'chan'=2,'obs'=4] {'lat','obs'}, dimensions={0} | all-to-all | bytes 1048576 | tf_op jit(solution)/shard_map/all_to_all | solution.py:377
  97.5 0.0 copy-start
  97.5 0.2 shard_map.163
  97.7 25.3 %all_to_all.29.second_ref = bf16[256,8,128]{2,1,0:T(8,128)(2,1)S(1)} all-to-all(bf16[256,8,128]{2,1,0:T(8,128)(2,1)S(1)} %shard_map.163), channel_id=1, replica_groups=mesh['lat'=64,'chan'=2,'obs'=4] {'lat','obs'}, dimensions={0} | all-to-all | bytes 1048576 | tf_op jit(solution)/shard_map/all_to_all | solution.py:377
  122.9 0.0 copy-done
  122.9 1.9 %shard_map.164 = (bf16[2,1024,128]{2,1,0:T(8,128)(2,1)}, f32[2,512,128]{2,1,0:T(8,128)}) custom-call(bf16[256,8,128]{2,1,0:T(8,128)(2,1)S(1)} %all_to_all.28.got_ref.first_ref, bf16[256,8,128]{2,1,0:T(8,128)(2,1)S(1)} %all_to_all.29.second_ref, s32[2,256]{1,0:T(2,128)S(1)} %bitcast.14, bf16[2,512,512]{2,1,0:T(8,128)(2,1)S(1)} %copy-done, ...), custom_call_target="tpu_custom_call" | custom-call | flops 805306368 | bytes 4196352 | tf_op jit(solution)/shard_map/pallas_call | solution.py:37
Async XLA Ops:
  6.8 21.4 %copy-start.10 = (s32[512]{0:T(512)S(1)}, s32[512]{0:T(512)}, u32[]{:S(2)}) copy-start(s32[512]{0:T(512)} %param.18) | copy-start | bytes 6148
  6.8 34.1 %all-to-all-start = ((f32[256,1,128]{2,1,0:T(1,128)}), f32[256,1,128]{2,1,0:T(1,128)S(1)}, u32[]{:S(2)}, u32[]{:S(2)}) async-start(f32[256,1,128]{2,1,0:T(1,128)} %bitcast.15), calls=%async_computation | async-start | bytes 262144 | tf_op jit(solution)/shard_map/all_to_all | solution.py:377
  28.4 12.5 %copy-start.1 = (bf16[2,1024,128]{2,1,0:T(8,128)(2,1)S(1)}, bf16[2,1024,128]{2,1,0:T(8,128)(2,1)}, u32[]{:S(2)}) copy-start(bf16[2,1024,128]{2,1,0:T(8,128)(2,1)} %next_ref.1) | copy-start | bytes 1572868
  28.4 12.5 %copy-start.2 = (bf16[2,1024,128]{2,1,0:T(8,128)(2,1)S(1)}, bf16[2,1024,128]{2,1,0:T(8,128)(2,1)}, u32[]{:S(2)}) copy-start(bf16[2,1024,128]{2,1,0:T(8,128)(2,1)} %pre_ref.1) | copy-start | bytes 1572868
  28.4 12.5 %copy-start.5 = (bf16[2,512,512]{2,1,0:T(8,128)(2,1)S(1)}, bf16[2,512,512]{2,1,0:T(8,128)(2,1)}, u32[]{:S(2)}) copy-start(bf16[2,512,512]{2,1,0:T(8,128)(2,1)} %constant.14.clone.far_table.table_ref) | copy-start | bytes 3145732
  28.4 12.5 %copy-start.9 = (bf16[2,512,512]{2,1,0:T(8,128)(2,1)S(1)}, bf16[2,512,512]{2,1,0:T(8,128)(2,1)}, u32[]{:S(2)}) copy-start(bf16[2,512,512]{2,1,0:T(8,128)(2,1)} %get-tuple-element.36.early_ref) | copy-start | bytes 3145732
  41.0 30.0 %copy-start.6 = (bf16[2,512,512]{2,1,0:T(8,128)(2,1)S(1)}, bf16[2,512,512]{2,1,0:T(8,128)(2,1)}, u32[]{:S(2)}) copy-start(bf16[2,512,512]{2,1,0:T(8,128)(2,1)} %get-tuple-element.39.up_ref) | copy-start | bytes 3145732
  41.0 30.0 %copy-start.7 = (bf16[2,512,512]{2,1,0:T(8,128)(2,1)S(1)}, bf16[2,512,512]{2,1,0:T(8,128)(2,1)}, u32[]{:S(2)}) copy-start(bf16[2,512,512]{2,1,0:T(8,128)(2,1)} %get-tuple-element.40.down_ref) | copy-start | bytes 3145732
  41.0 30.0 %copy-start.8 = (f32[512,128]{1,0:T(8,128)S(1)}, f32[512,128]{1,0:T(8,128)}, u32[]{:S(2)}) copy-start(f32[512,128]{1,0:T(8,128)} %get-tuple-element.41.weight_ref) | copy-start | bytes 786436
  45.4 25.6 %copy-start.3 = (bf16[2,2,512,128]{3,2,1,0:T(8,128)(2,1)S(1)}, bf16[2,2,512,128]{3,2,1,0:T(8,128)(2,1)}, u32[]{:S(2)}) copy-start(bf16[2,2,512,128]{3,2,1,0:T(8,128)(2,1)} %saved_ref.1) | copy-start | bytes 1572868
  45.4 25.6 %copy-start.4 = (f32[2,512,128]{2,1,0:T(8,128)S(1)}, f32[2,512,128]{2,1,0:T(8,128)}, u32[]{:S(2)}) copy-start(f32[2,512,128]{2,1,0:T(8,128)} %gain_ref.1) | copy-start | bytes 1572868
  97.5 25.5 %copy-start = (bf16[2,512,512]{2,1,0:T(8,128)(2,1)S(1)}, bf16[2,512,512]{2,1,0:T(8,128)(2,1)}, u32[]{:S(2)}) copy-start(bf16[2,512,512]{2,1,0:T(8,128)(2,1)} %constant.15.clone.table_ref) | copy-start | bytes 3145732

commit v8 on v7

--- a/solution.py
+++ b/solution.py
@@ -177,6 +177,7 @@
     cols_ref,
     field_ref,
     halves_ref,
+    total_ref,
     msg_ref,
 ):
     values = pre_ref[...].astype(F32)
@@ -217,25 +218,27 @@
                 hit, tall(weight[p : p + 1], width), nothing
             )
     pair = lat_dev * width
-    found = [
-        dot_nt(rows_ref[...], cols_ref[j * pair : (j + 1) * pair, :]) for j in range(5)
-    ]
-    found[0] = found[0] + pltpu.roll(found[4], 1, 0)
+
+    def found(j):
+        return dot_nt(rows_ref[...], cols_ref[j * pair : (j + 1) * pair, :])
+
     for j in range(4):
+        part = found(j)
+        if j == 0:
+            part = part + pltpu.roll(found(4), 1, 0)
         for k in range(lat_dev):
-            field_ref[k, pl.ds(j, groups, stride=4), :] = found[j][:, k * width : (k + 1) * width]
-    halves = []
-    for h in range(2):
-        at = h * (lons // 2)
-        parts = []
-        for k in range(lat_dev):
-            total = next_ref[k, at : at + lons // 2, :].astype(F32) + field_ref[
-                k, at : at + lons // 2, :
-            ]
-            grad_ref[k, at : at + lons // 2, :] = total
-            parts.append((total * slope_ref[k, at : at + lons // 2, :]).astype(BF))
-        halves.extend(parts)
-    halves_ref[...] = jnp.concatenate(halves, axis=1)
+            field_ref[k, pl.ds(j, groups, stride=4), :] = part[:, k * width : (k + 1) * width]
+    block = 128
+    for k in range(lat_dev):
+        for h in range(2):
+            lanes = slice(h * pair + k * width, h * pair + (k + 1) * width)
+            for i in range(lons // 2 // block):
+                span = slice(h * lons // 2 + i * block, h * lons // 2 + (i + 1) * block)
+                total = next_ref[k, span, :].astype(F32) + field_ref[k, span, :]
+                grad_ref[k, span, :] = total
+                halves_ref[i * block : (i + 1) * block, lanes] = (
+                    total * slope_ref[k, span, :]
+                ).astype(BF)
 
     def store(total, r):
         for s in range(2):
@@ -261,20 +264,18 @@
         order_ids = iota((orders, 1), 0)
         sign = jnp.where(order_ids % 2 == 0, 1.0, -1.0)
         scale = jnp.where(order_ids == 0, 1.0, 2.0)
-        totals = []
         for r in range(2):
             both = dot(table_ref[r], halves_ref[...])
             total = (both[:, :pair] + sign * both[:, pair:]) * (scale if r == 0 else -scale)
-            totals.append(total.astype(BF))
-        placed = dot(chosen, jnp.concatenate(totals, axis=1))
+            total_ref[:, r * pair : (r + 1) * pair] = total.astype(BF)
         for r in range(2):
-            store(placed[:, r * pair : (r + 1) * pair], r)
+            store(dot(chosen, total_ref[:, r * pair : (r + 1) * pair]), r)
 
     sent_ref[...] = msg_ref[...].reshape(ranks, 8, width).astype(BF)
 
 
 def legendre_kernel(
-    got_ref, up_ref, down_ref, weight_ref, saved_ref, gain_ref, first_ref, second_ref, msg_ref, out_ref
+    got_ref, up_ref, down_ref, weight_ref, saved_ref, gain_ref, first_ref, second_ref, msg_ref, out_ref, field_ref, coeff_ref
 ):
     ranks, rows, width = got_ref.shape
     msg_ref[...] = got_ref[...].astype(F32).reshape(ranks * rows, width)
@@ -282,23 +283,23 @@
     gain_imag = gain_ref[1]
     terms = [None, None]
     for s in range(2):
-        parts = []
         for r in range(2):
-            lanes = [
-                msg_ref[pl.ds(s * 4 + r * 2 + k, ranks, stride=8), :].astype(BF) for k in range(2)
-            ]
-            parts.append(jnp.concatenate(lanes, axis=0))
-        found = dot(up_ref[s], jnp.concatenate(parts, axis=1))
+            for k in range(2):
+                field_ref[s, k * ranks : (k + 1) * ranks, r * width : (r + 1) * width] = msg_ref[
+                    pl.ds(s * 4 + r * 2 + k, ranks, stride=8), :
+                ].astype(BF)
+    for s in range(2):
+        found = dot(up_ref[s], field_ref[s])
         real = found[:, :width]
         imag = found[:, width:]
         saved_real = saved_ref[s, 0].astype(F32)
         saved_imag = saved_ref[s, 1].astype(F32)
+        coeff_ref[s, :, :width] = (gain_real * real + gain_imag * imag).astype(BF)
+        coeff_ref[s, :, width:] = (gain_real * imag - gain_imag * real).astype(BF)
         new = (real * saved_real + imag * saved_imag, imag * saved_real - real * saved_imag)
         terms = [n if t is None else t + n for t, n in zip(terms, new)]
-        coeff = jnp.concatenate(
-            [gain_real * real + gain_imag * imag, gain_real * imag - gain_imag * real], axis=1
-        ).astype(BF)
-        lat_grad = dot(down_ref[s], coeff)
+    for s in range(2):
+        lat_grad = dot(down_ref[s], coeff_ref[s])
         for r in range(2):
             weighted = lat_grad[:, r * width : (r + 1) * width] * weight_ref[...]
             for k in range(2):
@@ -481,6 +482,7 @@
             pltpu.VMEM((10 * width, 16 * ranks), BF),
             pltpu.VMEM(field.shape, F32),
             pltpu.VMEM((lons // 2, 2 * lat_dev * width), BF),
+            pltpu.VMEM((orders, 2 * lat_dev * width), BF),
             rows,
         ],
         smem=1,
@@ -489,7 +491,11 @@
     )(core, slots, next_grad, pre_act, table, early, order_columns)
     by_order = exchange(sent)
     first, second = call(
-        legendre_kernel, (message, message), scratch=[rows, pairs], flops=2 * 512**3 * 4
+        legendre_kernel,
+        (message, message),
+        scratch=[rows, pairs]
+        + [pltpu.VMEM((slot_dev, n, 2 * width), BF) for n in (lats, degrees)],
+        flops=2 * 512**3 * 4
     )(by_order, up_table, down_table, weight, saved_coeffs, spectral_gain)
     first = exchange(first)
     second = exchange(call(share_kernel, message)(first, second))

time: 126 us -> 126 us (level)
  no operation moved by 1% of the time
where the time goes in v8:
time: 126 us; the launch traced here: 125 us
  blocking collectives  75.9 us (60%)
  starting transfers between devices  21.4 us (17%)
  Pallas kernels  13.8 us (11%)
  waiting for transfers between devices  12.4 us (10%)
    all_to_all x3, blocking collectives, exchange(): lax.all_to_all(message, RANKS, split_axis=0, concat_axis=0, tiled=True)  75.9 us
    all_to_all x1, starting transfers between devices, exchange(): lax.all_to_all(message, RANKS, split_axis=0, concat_axis=0, tiled=True)  21.4 us
    pallas_call x7, Pallas kernels, run(): pl.pallas_call(kernel, out_shape=out_shape, in_specs=specs, out_specs=jax...  13.8 us
    all_to_all x1, waiting for transfers between devices, exchange(): lax.all_to_all(message, RANKS, split_axis=0, concat_axis=0, tiled=True)  12.4 us
  transfers between devices with their start and end apart: 1, of which 1 were waited for; matrix products, arithmetic and copies ran while one was open for 0% of the time, Pallas kernels for 0%

profile of v8, /device:TPU:6, one launch (start us, length us, event | category | flops | bytes accessed | tf_op | source)
XLA Modules:
  0.0 124.7 jit_solution(13492280614109930014)
XLA Ops:
  0.6 4.5 %shard_map.159 = (bf16[2,512,512]{2,1,0:T(8,128)(2,1)}, bf16[2,512,512]{2,1,0:T(8,128)(2,1)}, f32[512,128]{1,0:T(8,128)}, bf16[2,512,512]{2,1,0:T(8,128)(2,1)}) custom-call(s32[1]{0:T(128)S(6)} %sub.3.turn_ref, bf16[2,512,512]{2,1,0:T(8,128)(2,1)} %far_legendre.3, f32[1,512]{1,0:T(1,128)} %bitcast.22, s32[1,512]{1,0:T(1,128)} %bitcast.21, ...), custom_call_target="tpu_custom_call" | custom-call | flops 1610612736 | bytes 5509124 | tf_op jit(solution)/shard_map/pallas_call | solution.py:37
  5.2 1.6 %shard_map.158 = f32[256,128]{1,0:T(8,128)} custom-call(s32[1]{0:T(128)S(6)} %mul.3.base_ref, bf16[16,256]{1,0:T(8,128)(2,1)} %bitcast.18, bf16[16,256]{1,0:T(8,128)(2,1)} %bitcast.19, bf16[16,256]{1,0:T(8,128)(2,1)} %bitcast.20, s32[16,256]{1,0:T(8,128)} %bitcast.16, s32[16,256]{1,0:T(8,128)} %bitcast.17, s32[1,256]{1,0:T(1,128)} %refs_5_.1), custom_call_target="tpu_custom_call" | custom-call | bytes 189444 | tf_op jit(solution)/shard_map/pallas_call | solution.py:37
  6.8 0.0 copy-start.10
  6.8 21.4 %all-to-all-start = ((f32[256,1,128]{2,1,0:T(1,128)}), f32[256,1,128]{2,1,0:T(1,128)S(1)}, u32[]{:S(2)}, u32[]{:S(2)}) async-start(f32[256,1,128]{2,1,0:T(1,128)} %bitcast.15), calls=%async_computation | async-start | bytes 262144 | tf_op jit(solution)/shard_map/all_to_all | solution.py:378
  28.2 0.0 copy-done.10
  28.2 0.1 reshape.21.order_ref
  28.3 0.1 copy.23
  28.4 0.0 copy-start.1
  28.4 0.0 copy-start.2
  28.4 0.0 copy-start.5
  28.4 0.0 copy-start.9
  28.4 0.1 shard_map.160
  28.5 12.4 %all-to-all-done = f32[256,1,128]{2,1,0:T(1,128)S(1)} async-done(((f32[256,1,128]{2,1,0:T(1,128)}), f32[256,1,128]{2,1,0:T(1,128)S(1)}, u32[]{:S(2)}, u32[]{:S(2)}) %all-to-all-start) | async-done | bytes 131104 | tf_op jit(solution)/shard_map/all_to_all | solution.py:378
  40.9 0.0 copy-done.1
  40.9 0.0 copy-done.2
  41.0 0.0 copy-done.5
  41.0 0.0 copy-done.9
  41.0 0.0 copy-start.6
  41.0 0.0 copy-start.7
  41.0 0.0 copy-start.8
  41.0 4.3 %shard_map.161 = (bf16[256,8,128]{2,1,0:T(8,128)(2,1)S(1)}, f32[2,1024,128]{2,1,0:T(8,128)S(1)}) custom-call(s32[1]{0:T(128)} %bitcast.turn_ref.core_ref, f32[256,128]{1,0:T(8,128)S(1)} %bitcast.13, bf16[2,1024,128]{2,1,0:T(8,128)(2,1)S(1)} %copy-done.1, bf16[2,1024,128]{2,1,0:T(8,128)(2,1)S(1)} %copy-done.2, bf16[2,512,512]{2,1,0:T(8,128)(2,1)S(1)} %copy-done.5, ...), custom_call_target="tpu_custom_call" | custom-call | flops 4294967296 | bytes 4851716 | tf_op jit(solution)/shard_map/pallas_call | solution.py:37
  45.3 0.0 copy-start.3
  45.3 0.0 copy-start.4
  45.3 25.6 %all_to_all.27.got_ref = bf16[256,8,128]{2,1,0:T(8,128)(2,1)S(1)} all-to-all(bf16[256,8,128]{2,1,0:T(8,128)(2,1)S(1)} %get-tuple-element.38), channel_id=1, replica_groups=mesh['lat'=64,'chan'=2,'obs'=4] {'lat','obs'}, dimensions={0} | all-to-all | bytes 1048576 | tf_op jit(solution)/shard_map/all_to_all | solution.py:378
  70.9 0.0 copy-done.6
  70.9 0.0 copy-done.7
  70.9 0.0 copy-done.8
  70.9 0.0 copy-done.3
  70.9 0.0 copy-done.4
  70.9 1.3 %shard_map.162 = (bf16[256,8,128]{2,1,0:T(8,128)(2,1)S(1)}, bf16[256,8,128]{2,1,0:T(8,128)(2,1)S(1)}) custom-call(bf16[256,8,128]{2,1,0:T(8,128)(2,1)S(1)} %all_to_all.27.got_ref, bf16[2,512,512]{2,1,0:T(8,128)(2,1)S(1)} %copy-done.6, bf16[2,512,512]{2,1,0:T(8,128)(2,1)S(1)} %copy-done.7, f32[512,128]{1,0:T(8,128)S(1)} %copy-done.8, ...), custom_call_target="tpu_custom_call" | custom-call | flops 1073741824 | bytes 4980736 | tf_op jit(solution)/shard_map/pallas_call | solution.py:37
  72.2 25.1 %all_to_all.28.got_ref.first_ref = bf16[256,8,128]{2,1,0:T(8,128)(2,1)S(1)} all-to-all(bf16[256,8,128]{2,1,0:T(8,128)(2,1)S(1)} %get-tuple-element.42), channel_id=1, replica_groups=mesh['lat'=64,'chan'=2,'obs'=4] {'lat','obs'}, dimensions={0} | all-to-all | bytes 1048576 | tf_op jit(solution)/shard_map/all_to_all | solution.py:378
  97.3 0.0 copy-start
  97.3 0.2 shard_map.163
  97.4 25.2 %all_to_all.29.second_ref = bf16[256,8,128]{2,1,0:T(8,128)(2,1)S(1)} all-to-all(bf16[256,8,128]{2,1,0:T(8,128)(2,1)S(1)} %shard_map.163), channel_id=1, replica_groups=mesh['lat'=64,'chan'=2,'obs'=4] {'lat','obs'}, dimensions={0} | all-to-all | bytes 1048576 | tf_op jit(solution)/shard_map/all_to_all | solution.py:378
  122.7 0.0 copy-done
  122.7 1.9 %shard_map.164 = (bf16[2,1024,128]{2,1,0:T(8,128)(2,1)}, f32[2,512,128]{2,1,0:T(8,128)}) custom-call(bf16[256,8,128]{2,1,0:T(8,128)(2,1)S(1)} %all_to_all.28.got_ref.first_ref, bf16[256,8,128]{2,1,0:T(8,128)(2,1)S(1)} %all_to_all.29.second_ref, s32[2,256]{1,0:T(2,128)S(1)} %bitcast.14, bf16[2,512,512]{2,1,0:T(8,128)(2,1)S(1)} %copy-done, ...), custom_call_target="tpu_custom_call" | custom-call | flops 805306368 | bytes 4196352 | tf_op jit(solution)/shard_map/pallas_call | solution.py:37
Async XLA Ops:
  6.8 21.4 %copy-start.10 = (s32[512]{0:T(512)S(1)}, s32[512]{0:T(512)}, u32[]{:S(2)}) copy-start(s32[512]{0:T(512)} %param.18) | copy-start | bytes 6148
  6.8 34.1 %all-to-all-start = ((f32[256,1,128]{2,1,0:T(1,128)}), f32[256,1,128]{2,1,0:T(1,128)S(1)}, u32[]{:S(2)}, u32[]{:S(2)}) async-start(f32[256,1,128]{2,1,0:T(1,128)} %bitcast.15), calls=%async_computation | async-start | bytes 262144 | tf_op jit(solution)/shard_map/all_to_all | solution.py:378
  28.4 12.5 %copy-start.1 = (bf16[2,1024,128]{2,1,0:T(8,128)(2,1)S(1)}, bf16[2,1024,128]{2,1,0:T(8,128)(2,1)}, u32[]{:S(2)}) copy-start(bf16[2,1024,128]{2,1,0:T(8,128)(2,1)} %next_ref.1) | copy-start | bytes 1572868
  28.4 12.5 %copy-start.2 = (bf16[2,1024,128]{2,1,0:T(8,128)(2,1)S(1)}, bf16[2,1024,128]{2,1,0:T(8,128)(2,1)}, u32[]{:S(2)}) copy-start(bf16[2,1024,128]{2,1,0:T(8,128)(2,1)} %pre_ref.1) | copy-start | bytes 1572868
  28.4 12.5 %copy-start.5 = (bf16[2,512,512]{2,1,0:T(8,128)(2,1)S(1)}, bf16[2,512,512]{2,1,0:T(8,128)(2,1)}, u32[]{:S(2)}) copy-start(bf16[2,512,512]{2,1,0:T(8,128)(2,1)} %constant.14.clone.far_table.table_ref) | copy-start | bytes 3145732
  28.4 12.5 %copy-start.9 = (bf16[2,512,512]{2,1,0:T(8,128)(2,1)S(1)}, bf16[2,512,512]{2,1,0:T(8,128)(2,1)}, u32[]{:S(2)}) copy-start(bf16[2,512,512]{2,1,0:T(8,128)(2,1)} %get-tuple-element.36.early_ref) | copy-start | bytes 3145732
  41.0 29.9 %copy-start.6 = (bf16[2,512,512]{2,1,0:T(8,128)(2,1)S(1)}, bf16[2,512,512]{2,1,0:T(8,128)(2,1)}, u32[]{:S(2)}) copy-start(bf16[2,512,512]{2,1,0:T(8,128)(2,1)} %get-tuple-element.39.up_ref) | copy-start | bytes 3145732
  41.0 29.9 %copy-start.7 = (bf16[2,512,512]{2,1,0:T(8,128)(2,1)S(1)}, bf16[2,512,512]{2,1,0:T(8,128)(2,1)}, u32[]{:S(2)}) copy-start(bf16[2,512,512]{2,1,0:T(8,128)(2,1)} %get-tuple-element.40.down_ref) | copy-start | bytes 3145732
  41.0 29.9 %copy-start.8 = (f32[512,128]{1,0:T(8,128)S(1)}, f32[512,128]{1,0:T(8,128)}, u32[]{:S(2)}) copy-start(f32[512,128]{1,0:T(8,128)} %get-tuple-element.41.weight_ref) | copy-start | bytes 786436
  45.3 25.6 %copy-start.3 = (bf16[2,2,512,128]{3,2,1,0:T(8,128)(2,1)S(1)}, bf16[2,2,512,128]{3,2,1,0:T(8,128)(2,1)}, u32[]{:S(2)}) copy-start(bf16[2,2,512,128]{3,2,1,0:T(8,128)(2,1)} %saved_ref.1) | copy-start | bytes 1572868
  45.3 25.6 %copy-start.4 = (f32[2,512,128]{2,1,0:T(8,128)S(1)}, f32[2,512,128]{2,1,0:T(8,128)}, u32[]{:S(2)}) copy-start(f32[2,512,128]{2,1,0:T(8,128)} %gain_ref.1) | copy-start | bytes 1572868
  97.3 25.4 %copy-start = (bf16[2,512,512]{2,1,0:T(8,128)(2,1)S(1)}, bf16[2,512,512]{2,1,0:T(8,128)(2,1)}, u32[]{:S(2)}) copy-start(bf16[2,512,512]{2,1,0:T(8,128)(2,1)} %constant.15.clone.table_ref) | copy-start | bytes 3145732

commit v9 on v8

--- a/solution.py
+++ b/solution.py
@@ -98,23 +98,31 @@
     coming.append(pltpu.make_async_copy(sources[1], quad_ref, sems.at[2]))
     leaving = [pltpu.make_async_copy(weight_ref, far[2], sems.at[3])]
     for s in range(2):
-        leaving.append(pltpu.make_async_copy(up_ref.at[s], far[0].at[s], sems.at[4 + 2 * s]))
-        leaving.append(pltpu.make_async_copy(down_ref.at[s], far[1].at[s], sems.at[5 + 2 * s]))
-    for copy in coming:
+        leaving.append(pltpu.make_async_copy(up_ref.at[s], far[0].at[s], sems.at[4 + s]))
+        for h in range(2):
+            rows = slice(h * 256, (h + 1) * 256)
+            leaving.append(
+                pltpu.make_async_copy(
+                    down_ref.at[s, rows], far[1].at[s, rows], sems.at[6 + 2 * s + h]
+                )
+            )
+    for copy in coming[2:] + coming[:2]:
         copy.start()
 
     def work():
+        coming[2].wait()
+        quad = jnp.sum(jnp.where(chosen, quad_ref[...], 0.0), axis=1, keepdims=True)
+        weight_ref[...] = jnp.broadcast_to(quad, weight_ref.shape)
+        leaving[0].start()
         pick = chosen.astype(BF)
         for s in range(2):
             coming[s].wait()
             up_ref[s] = dot_nt(legendre_ref[s], pick).astype(BF)
-            leaving[1 + 2 * s].start()
-            down_ref[s] = dot_nt(pick, legendre_ref[s]).astype(BF)
-            leaving[2 + 2 * s].start()
-        coming[2].wait()
-        quad = jnp.sum(jnp.where(chosen, quad_ref[...], 0.0), axis=1, keepdims=True)
-        weight_ref[...] = jnp.broadcast_to(quad, weight_ref.shape)
-        leaving[0].start()
+            leaving[1 + 3 * s].start()
+            for h in range(2):
+                rows = slice(h * 256, (h + 1) * 256)
+                down_ref[s, rows] = dot_nt(pick[rows], legendre_ref[s]).astype(BF)
+                leaving[2 + 3 * s + h].start()
 
     return work, leaving
 
@@ -434,7 +442,7 @@
         shape((lats, 128), F32),
     )
     ready_scratch = (
-        buffers_for(ready_args)[:-1] + buffers_for(ready)[:-1] + [pltpu.SemaphoreType.DMA((8,))]
+        buffers_for(ready_args)[:-1] + buffers_for(ready)[:-1] + [pltpu.SemaphoreType.DMA((10,))]
     )
     early_args = (order_slots.reshape(1, orders), table)
 

time: 126 us -> 126 us (level)
  no operation moved by 1% of the time
where the time goes in v9:
time: 126 us; the launch traced here: 125 us
  blocking collectives  75.8 us (60%)
  starting transfers between devices  21.4 us (17%)
  Pallas kernels  13.8 us (11%)
  waiting for transfers between devices  12.4 us (10%)
    all_to_all x3, blocking collectives, exchange(): lax.all_to_all(message, RANKS, split_axis=0, concat_axis=0, tiled=True)  75.8 us
    all_to_all x1, starting transfers between devices, exchange(): lax.all_to_all(message, RANKS, split_axis=0, concat_axis=0, tiled=True)  21.4 us
    pallas_call x7, Pallas kernels, run(): pl.pallas_call(kernel, out_shape=out_shape, in_specs=specs, out_specs=jax...  13.8 us
    all_to_all x1, waiting for transfers between devices, exchange(): lax.all_to_all(message, RANKS, split_axis=0, concat_axis=0, tiled=True)  12.4 us
  transfers between devices with their start and end apart: 1, of which 1 were waited for; matrix products, arithmetic and copies ran while one was open for 0% of the time, Pallas kernels for 0%

profile of v9, /device:TPU:6, one launch (start us, length us, event | category | flops | bytes accessed | tf_op | source)
XLA Modules:
  0.0 124.6 jit_solution(6312024690842026322)
XLA Ops:
  0.6 4.4 %shard_map.159 = (bf16[2,512,512]{2,1,0:T(8,128)(2,1)}, bf16[2,512,512]{2,1,0:T(8,128)(2,1)}, f32[512,128]{1,0:T(8,128)}, bf16[2,512,512]{2,1,0:T(8,128)(2,1)}) custom-call(s32[1]{0:T(128)S(6)} %sub.3.turn_ref, bf16[2,512,512]{2,1,0:T(8,128)(2,1)} %far_legendre.3, f32[1,512]{1,0:T(1,128)} %bitcast.22, s32[1,512]{1,0:T(1,128)} %bitcast.21, ...), custom_call_target="tpu_custom_call" | custom-call | flops 1610612736 | bytes 5509124 | tf_op jit(solution)/shard_map/pallas_call | solution.py:37
  5.0 1.6 %shard_map.158 = f32[256,128]{1,0:T(8,128)} custom-call(s32[1]{0:T(128)S(6)} %mul.3.base_ref, bf16[16,256]{1,0:T(8,128)(2,1)} %bitcast.18, bf16[16,256]{1,0:T(8,128)(2,1)} %bitcast.19, bf16[16,256]{1,0:T(8,128)(2,1)} %bitcast.20, s32[16,256]{1,0:T(8,128)} %bitcast.16, s32[16,256]{1,0:T(8,128)} %bitcast.17, s32[1,256]{1,0:T(1,128)} %refs_5_.1), custom_call_target="tpu_custom_call" | custom-call | bytes 189444 | tf_op jit(solution)/shard_map/pallas_call | solution.py:37
  6.7 0.0 copy-start.10
  6.7 21.4 %all-to-all-start = ((f32[256,1,128]{2,1,0:T(1,128)}), f32[256,1,128]{2,1,0:T(1,128)S(1)}, u32[]{:S(2)}, u32[]{:S(2)}) async-start(f32[256,1,128]{2,1,0:T(1,128)} %bitcast.15), calls=%async_computation | async-start | bytes 262144 | tf_op jit(solution)/shard_map/all_to_all | solution.py:386
  28.0 0.0 copy-done.10
  28.1 0.1 reshape.21.order_ref
  28.2 0.1 copy.23
  28.3 0.0 copy-start.1
  28.3 0.0 copy-start.2
  28.3 0.0 copy-start.5
  28.3 0.0 copy-start.9
  28.3 0.1 shard_map.160
  28.4 12.4 %all-to-all-done = f32[256,1,128]{2,1,0:T(1,128)S(1)} async-done(((f32[256,1,128]{2,1,0:T(1,128)}), f32[256,1,128]{2,1,0:T(1,128)S(1)}, u32[]{:S(2)}, u32[]{:S(2)}) %all-to-all-start) | async-done | bytes 131104 | tf_op jit(solution)/shard_map/all_to_all | solution.py:386
  40.8 0.0 copy-done.1
  40.8 0.0 copy-done.2
  40.8 0.0 copy-done.5
  40.8 0.0 copy-done.9
  40.8 0.0 copy-start.6
  40.8 0.0 copy-start.7
  40.8 0.0 copy-start.8
  40.9 4.4 %shard_map.161 = (bf16[256,8,128]{2,1,0:T(8,128)(2,1)S(1)}, f32[2,1024,128]{2,1,0:T(8,128)S(1)}) custom-call(s32[1]{0:T(128)} %bitcast.turn_ref.core_ref, f32[256,128]{1,0:T(8,128)S(1)} %bitcast.13, bf16[2,1024,128]{2,1,0:T(8,128)(2,1)S(1)} %copy-done.1, bf16[2,1024,128]{2,1,0:T(8,128)(2,1)S(1)} %copy-done.2, bf16[2,512,512]{2,1,0:T(8,128)(2,1)S(1)} %copy-done.5, ...), custom_call_target="tpu_custom_call" | custom-call | flops 4294967296 | bytes 4851716 | tf_op jit(solution)/shard_map/pallas_call | solution.py:37
  45.3 0.0 copy-start.3
  45.3 0.0 copy-start.4
  45.3 25.5 %all_to_all.27.got_ref = bf16[256,8,128]{2,1,0:T(8,128)(2,1)S(1)} all-to-all(bf16[256,8,128]{2,1,0:T(8,128)(2,1)S(1)} %get-tuple-element.38), channel_id=1, replica_groups=mesh['lat'=64,'chan'=2,'obs'=4] {'lat','obs'}, dimensions={0} | all-to-all | bytes 1048576 | tf_op jit(solution)/shard_map/all_to_all | solution.py:386
  70.8 0.0 copy-done.6
  70.8 0.0 copy-done.7
  70.8 0.0 copy-done.8
  70.8 0.0 copy-done.3
  70.8 0.0 copy-done.4
  70.8 1.3 %shard_map.162 = (bf16[256,8,128]{2,1,0:T(8,128)(2,1)S(1)}, bf16[256,8,128]{2,1,0:T(8,128)(2,1)S(1)}) custom-call(bf16[256,8,128]{2,1,0:T(8,128)(2,1)S(1)} %all_to_all.27.got_ref, bf16[2,512,512]{2,1,0:T(8,128)(2,1)S(1)} %copy-done.6, bf16[2,512,512]{2,1,0:T(8,128)(2,1)S(1)} %copy-done.7, f32[512,128]{1,0:T(8,128)S(1)} %copy-done.8, ...), custom_call_target="tpu_custom_call" | custom-call | flops 1073741824 | bytes 4980736 | tf_op jit(solution)/shard_map/pallas_call | solution.py:37
  72.1 25.0 %all_to_all.28.got_ref.first_ref = bf16[256,8,128]{2,1,0:T(8,128)(2,1)S(1)} all-to-all(bf16[256,8,128]{2,1,0:T(8,128)(2,1)S(1)} %get-tuple-element.42), channel_id=1, replica_groups=mesh['lat'=64,'chan'=2,'obs'=4] {'lat','obs'}, dimensions={0} | all-to-all | bytes 1048576 | tf_op jit(solution)/shard_map/all_to_all | solution.py:386
  97.1 0.0 copy-start
  97.1 0.2 shard_map.163
  97.3 25.3 %all_to_all.29.second_ref = bf16[256,8,128]{2,1,0:T(8,128)(2,1)S(1)} all-to-all(bf16[256,8,128]{2,1,0:T(8,128)(2,1)S(1)} %shard_map.163), channel_id=1, replica_groups=mesh['lat'=64,'chan'=2,'obs'=4] {'lat','obs'}, dimensions={0} | all-to-all | bytes 1048576 | tf_op jit(solution)/shard_map/all_to_all | solution.py:386
  122.6 0.0 copy-done
  122.6 1.9 %shard_map.164 = (bf16[2,1024,128]{2,1,0:T(8,128)(2,1)}, f32[2,512,128]{2,1,0:T(8,128)}) custom-call(bf16[256,8,128]{2,1,0:T(8,128)(2,1)S(1)} %all_to_all.28.got_ref.first_ref, bf16[256,8,128]{2,1,0:T(8,128)(2,1)S(1)} %all_to_all.29.second_ref, s32[2,256]{1,0:T(2,128)S(1)} %bitcast.14, bf16[2,512,512]{2,1,0:T(8,128)(2,1)S(1)} %copy-done, ...), custom_call_target="tpu_custom_call" | custom-call | flops 805306368 | bytes 4196352 | tf_op jit(solution)/shard_map/pallas_call | solution.py:37
Async XLA Ops:
  6.7 21.4 %copy-start.10 = (s32[512]{0:T(512)S(1)}, s32[512]{0:T(512)}, u32[]{:S(2)}) copy-start(s32[512]{0:T(512)} %param.18) | copy-start | bytes 6148
  6.7 34.1 %all-to-all-start = ((f32[256,1,128]{2,1,0:T(1,128)}), f32[256,1,128]{2,1,0:T(1,128)S(1)}, u32[]{:S(2)}, u32[]{:S(2)}) async-start(f32[256,1,128]{2,1,0:T(1,128)} %bitcast.15), calls=%async_computation | async-start | bytes 262144 | tf_op jit(solution)/shard_map/all_to_all | solution.py:386
  28.3 12.5 %copy-start.1 = (bf16[2,1024,128]{2,1,0:T(8,128)(2,1)S(1)}, bf16[2,1024,128]{2,1,0:T(8,128)(2,1)}, u32[]{:S(2)}) copy-start(bf16[2,1024,128]{2,1,0:T(8,128)(2,1)} %next_ref.1) | copy-start | bytes 1572868
  28.3 12.5 %copy-start.2 = (bf16[2,1024,128]{2,1,0:T(8,128)(2,1)S(1)}, bf16[2,1024,128]{2,1,0:T(8,128)(2,1)}, u32[]{:S(2)}) copy-start(bf16[2,1024,128]{2,1,0:T(8,128)(2,1)} %pre_ref.1) | copy-start | bytes 1572868
  28.3 12.5 %copy-start.5 = (bf16[2,512,512]{2,1,0:T(8,128)(2,1)S(1)}, bf16[2,512,512]{2,1,0:T(8,128)(2,1)}, u32[]{:S(2)}) copy-start(bf16[2,512,512]{2,1,0:T(8,128)(2,1)} %constant.14.clone.far_table.table_ref) | copy-start | bytes 3145732
  28.3 12.5 %copy-start.9 = (bf16[2,512,512]{2,1,0:T(8,128)(2,1)S(1)}, bf16[2,512,512]{2,1,0:T(8,128)(2,1)}, u32[]{:S(2)}) copy-start(bf16[2,512,512]{2,1,0:T(8,128)(2,1)} %get-tuple-element.36.early_ref) | copy-start | bytes 3145732
  40.8 30.0 %copy-start.6 = (bf16[2,512,512]{2,1,0:T(8,128)(2,1)S(1)}, bf16[2,512,512]{2,1,0:T(8,128)(2,1)}, u32[]{:S(2)}) copy-start(bf16[2,512,512]{2,1,0:T(8,128)(2,1)} %get-tuple-element.39.up_ref) | copy-start | bytes 3145732
  40.8 30.0 %copy-start.7 = (bf16[2,512,512]{2,1,0:T(8,128)(2,1)S(1)}, bf16[2,512,512]{2,1,0:T(8,128)(2,1)}, u32[]{:S(2)}) copy-start(bf16[2,512,512]{2,1,0:T(8,128)(2,1)} %get-tuple-element.40.down_ref) | copy-start | bytes 3145732
  40.8 30.0 %copy-start.8 = (f32[512,128]{1,0:T(8,128)S(1)}, f32[512,128]{1,0:T(8,128)}, u32[]{:S(2)}) copy-start(f32[512,128]{1,0:T(8,128)} %get-tuple-element.41.weight_ref) | copy-start | bytes 786436
  45.3 25.5 %copy-start.3 = (bf16[2,2,512,128]{3,2,1,0:T(8,128)(2,1)S(1)}, bf16[2,2,512,128]{3,2,1,0:T(8,128)(2,1)}, u32[]{:S(2)}) copy-start(bf16[2,2,512,128]{3,2,1,0:T(8,128)(2,1)} %saved_ref.1) | copy-start | bytes 1572868
  45.3 25.5 %copy-start.4 = (f32[2,512,128]{2,1,0:T(8,128)S(1)}, f32[2,512,128]{2,1,0:T(8,128)}, u32[]{:S(2)}) copy-start(f32[2,512,128]{2,1,0:T(8,128)} %gain_ref.1) | copy-start | bytes 1572868
  97.1 25.5 %copy-start = (bf16[2,512,512]{2,1,0:T(8,128)(2,1)S(1)}, bf16[2,512,512]{2,1,0:T(8,128)(2,1)}, u32[]{:S(2)}) copy-start(bf16[2,512,512]{2,1,0:T(8,128)(2,1)} %constant.15.clone.table_ref) | copy-start | bytes 3145732
